TPU v7x, 256 devices: a whole 4x4x8 slice. The times are simulated.
256 devices in a mesh: bins: 64 (over y, x_hi, z), band: 4 (over x_lo, core).
Axes of the slice: x: 4 (x_hi: 2, x_lo: 2; x = x_hi * 2 + x_lo), y: 4, z: 8, core: 2. Of those that a mesh axis runs over, the one named last changes fastest.
Arguments:
- features: bfloat16 [2048, 64], P('bins'), may hold values from -6 to 6
- left_weight: bfloat16 [64, 64], replicated, may hold values from -0.75 to 0.75
- right_weight: bfloat16 [64, 64], replicated, may hold values from -0.75 to 0.75
- offset_embed: bfloat16 [64, 512], P(None, 'band'), may hold values from -4 to 4
- kernels: bfloat16 [2, 3, 3, 64, 64], replicated, may hold values from -0.4375 to 0.4375
- dilation: int32 [2], replicated, may hold values from 1 to 4, as said below
- cotangent: bfloat16 [2048, 64, 512], P('bins', None, 'band'), may hold values from -6 to 6
Outputs:
- pair_map: bfloat16 [2048, 64, 512], P('bins', None, 'band')
- grad_features: float32 [2048, 64], P('bins')
- grad_left: float32 [64, 64], replicated
- grad_right: float32 [64, 64], replicated
- grad_offset: float32 [64, 512], P(None, 'band')
- grad_kernels: float32 [2, 3, 3, 64, 64], replicated
Inputs may be any that keep to these rules, and one draw needn't show every extreme that they name: Each entry is one layer's dilation; the largest entry equals 4.
All inputs are finite; a program needn't handle non-finite values.
Results may differ from a plain program's by a relative error of at most 0.02.
Values may be sent and summed in bfloat16 or wider, within the bound.
No kernel may reach another device: no remote copies, remote signals or barrier semaphores. Data moves between devices by JAX's collectives and lax.ppermute only.
A program may use at most 64 MiB of HBM per device.

v0:
```python
import math

import jax
import jax.numpy as jnp
from jax import lax
from jax.sharding import PartitionSpec as P

LAYERS = 2
MAXDIL = 4


def passed_along(block, axis, distance):
    devices = range(lax.axis_size(axis))
    route = [(i - distance, i) for i in devices if i - distance in devices]
    return lax.ppermute(block, axis, route)


def with_halo(block, sides, width):
    for axis, dim in sides:
        count = lax.axis_size(axis)
        forward = [(i, i + 1) for i in range(count - 1)]
        backward = [(target, source) for source, target in forward]
        low = lax.ppermute(
            lax.slice_in_dim(block, block.shape[dim] - width, None, axis=dim), axis, forward
        )
        high = lax.ppermute(lax.slice_in_dim(block, 0, width, axis=dim), axis, backward)
        block = jnp.concatenate([low, block, high], axis=dim)
    return block


def silu_slope(value):
    sigma = jax.nn.sigmoid(value)
    return sigma * (1.0 + value * (1.0 - sigma))


def tap_view(padded, row_start, col_start, bin_rows, group_width):
    return lax.dynamic_slice(
        padded, (row_start, jnp.int32(0), col_start), (bin_rows, padded.shape[1], group_width)
    )


def per_device(features, left_weight, right_weight, offset_embed, kernels, dilation, cotangent):
    bin_rows = features.shape[0]
    channels = features.shape[1]
    group_width = offset_embed.shape[1]
    total_bins = bin_rows * lax.axis_size("bins")
    total_band = group_width * lax.axis_size("band")
    bin_index = lax.axis_index("bins")
    band_index = lax.axis_index("band")
    window_len = bin_rows + group_width
    blocks = group_width // bin_rows
    reach = total_band // bin_rows
    left = jnp.dot(features, left_weight, preferred_element_type=jnp.float32).astype(jnp.bfloat16)
    right = jnp.dot(features, right_weight, preferred_element_type=jnp.float32).astype(jnp.bfloat16)
    arrived = [right]
    for lag in range(1, reach + 1):
        arrived.append(passed_along(right, "bins", -lag))
    stacked = jnp.stack(arrived)
    window = lax.dynamic_slice_in_dim(stacked, band_index * blocks, blocks + 1, 0).reshape(
        window_len, channels
    )
    flat = jnp.broadcast_to(
        window.T[:, None, : window_len - 1], (channels, bin_rows, window_len - 1)
    )
    flat = flat.reshape(channels, bin_rows * (window_len - 1))
    flat = jnp.pad(flat, ((0, 0), (0, bin_rows))).reshape(channels, bin_rows, window_len)[
        :, :, :group_width
    ]
    lagged = jnp.transpose(flat, (1, 0, 2))
    global_bins = bin_index * bin_rows + jnp.arange(bin_rows, dtype=jnp.int32)
    global_offsets = band_index * group_width + jnp.arange(group_width, dtype=jnp.int32)
    mask = (global_bins[:, None] + global_offsets[None, :] < total_bins).astype(jnp.float32)[
        :, None, :
    ]
    summed = (
        left.astype(jnp.float32)[:, :, None]
        + lagged.astype(jnp.float32)
        + offset_embed.astype(jnp.float32)[None]
    )
    state = (jax.nn.silu(summed) * mask).astype(jnp.bfloat16)
    padded_states = []
    pres = []
    for layer in range(LAYERS):
        rate = dilation[layer]
        padded = with_halo(state, (("bins", 0), ("band", 2)), MAXDIL)
        padded_states.append(padded)
        total = jnp.zeros((bin_rows, channels, group_width), jnp.float32)
        for row_tap in range(3):
            for col_tap in range(3):
                view = tap_view(
                    padded,
                    MAXDIL + rate * (row_tap - 1),
                    MAXDIL + rate * (col_tap - 1),
                    bin_rows,
                    group_width,
                )
                total = total + jnp.einsum(
                    "icd,ce->ied",
                    view,
                    kernels[layer, row_tap, col_tap],
                    preferred_element_type=jnp.float32,
                )
        pres.append(total)
        state = (jax.nn.silu(total) * mask).astype(jnp.bfloat16)
    back = cotangent.astype(jnp.float32)
    kernel_grads = [None] * LAYERS
    for layer in reversed(range(LAYERS)):
        rate = dilation[layer]
        grad_pre = (back * mask * silu_slope(pres[layer])).astype(jnp.bfloat16)
        padded_grad = with_halo(grad_pre, (("bins", 0), ("band", 2)), MAXDIL)
        taps = []
        fresh = jnp.zeros((bin_rows, channels, group_width), jnp.float32)
        for row_tap in range(3):
            for col_tap in range(3):
                view = tap_view(
                    padded_states[layer],
                    MAXDIL + rate * (row_tap - 1),
                    MAXDIL + rate * (col_tap - 1),
                    bin_rows,
                    group_width,
                )
                taps.append(
                    jnp.einsum("icd,ied->ce", view, grad_pre, preferred_element_type=jnp.float32)
                )
                mirror = tap_view(
                    padded_grad,
                    MAXDIL - rate * (row_tap - 1),
                    MAXDIL - rate * (col_tap - 1),
                    bin_rows,
                    group_width,
                )
                fresh = fresh + jnp.einsum(
                    "ied,ce->icd",
                    mirror,
                    kernels[layer, row_tap, col_tap],
                    preferred_element_type=jnp.float32,
                )
        kernel_grads[layer] = jnp.stack(taps).reshape(3, 3, channels, channels)
        back = fresh
    grad_sum = back * mask * silu_slope(summed)
    left_grad = jnp.sum(grad_sum, axis=2)
    offset_part = jnp.sum(grad_sum, axis=0)
    spread = jnp.pad(jnp.transpose(grad_sum, (1, 0, 2)), ((0, 0), (0, 0), (0, bin_rows)))
    spread = spread.reshape(channels, bin_rows * window_len)[:, : bin_rows * (window_len - 1)]
    window_grad = spread.reshape(channels, bin_rows, window_len - 1).sum(axis=1)
    window_grad = jnp.pad(window_grad, ((0, 0), (0, 1))).T
    pieces = window_grad.reshape(blocks + 1, bin_rows, channels)
    empty = jnp.zeros((reach, bin_rows, channels), jnp.float32)
    framed = jnp.concatenate([empty, pieces, empty], 0)
    right_grad = lax.dynamic_index_in_dim(framed, reach - band_index * blocks, 0, keepdims=False)
    for lag in range(1, reach + 1):
        piece = lax.dynamic_index_in_dim(
            framed, reach + lag - band_index * blocks, 0, keepdims=False
        )
        right_grad = right_grad + passed_along(piece, "bins", lag)
    highest = lax.Precision.HIGHEST
    feature_part = jnp.dot(
        left_grad, left_weight.astype(jnp.float32).T, precision=highest
    ) + jnp.dot(right_grad, right_weight.astype(jnp.float32).T, precision=highest)
    grad_features = lax.psum(feature_part, "band") / math.sqrt(total_band)
    offset_sum = lax.psum(offset_part, "bins")
    left_part = jnp.dot(features.astype(jnp.float32).T, left_grad, precision=highest)
    right_part = jnp.dot(features.astype(jnp.float32).T, right_grad, precision=highest)
    kernel_sum, left_sum, right_sum = lax.psum(
        (jnp.stack(kernel_grads), left_part, right_part), ("bins", "band")
    )
    whole_scale = math.sqrt(total_bins * total_band)
    return (
        state,
        grad_features,
        left_sum / whole_scale,
        right_sum / whole_scale,
        offset_sum / math.sqrt(total_bins),
        kernel_sum / whole_scale,
    )


def solution(mesh):
    return jax.shard_map(
        per_device,
        mesh=mesh,
        in_specs=(P("bins", None), P(), P(), P(None, "band"), P(), P(), P("bins", None, "band")),
        out_specs=(P("bins", None, "band"), P("bins", None), P(), P(), P(None, "band"), P()),
        check_vma=False,
    )
```

profile of v0, /device:TPU:1, one launch (start us, length us, event | category | flops | bytes accessed | tf_op | source)
XLA Modules:
  0.0 782.0 jit_solution(17445417174002254758)
XLA Ops:
  19.6 26.8 %collective-permute-start.1 = (bf16[32,64]{1,0:T(8,128)(2,1)S(1)}, bf16[32,64]{1,0:T(8,128)(2,1)S(1)}, u32[]{:S(2)}, u32[]{:S(2)}) collective-permute-start(bf16[32,64]{1,0:T(8,128)(2,1)S(1)} %get-tuple-element.71), channel_id=1, source_target_pairs={{8,0},{12,4},{16,8},{20,12},{24,16},{28,20},{32,24},{36,28},{40,32... | collective-permute-start | bytes 12296 | tf_op jit(solution)/shard_map/ppermute | solution.py:15
  46.4 4.3 collective-permute-done.1
  52.0 5.7 collective-permute-done.2
  59.0 7.0 collective-permute-done.3
  67.3 10.6 %collective-permute-done.4 = bf16[32,64]{1,0:T(8,128)(2,1)S(1)} collective-permute-done((bf16[32,64]{1,0:T(8,128)(2,1)S(1)}, bf16[32,64]{1,0:T(8,128)(2,1)S(1)}, u32[]{:S(2)}, u32[]{:S(2)}) %collective-permute-start.4) | collective-permute-done | bytes 4128 | tf_op jit(solution)/shard_map/ppermute | solution.py:15
  79.2 8.2 %collective-permute-done.5 = bf16[32,64]{1,0:T(8,128)(2,1)S(1)} collective-permute-done((bf16[32,64]{1,0:T(8,128)(2,1)S(1)}, bf16[32,64]{1,0:T(8,128)(2,1)S(1)}, u32[]{:S(2)}, u32[]{:S(2)}) %collective-permute-start.5) | collective-permute-done | bytes 4128 | tf_op jit(solution)/shard_map/ppermute | solution.py:15
  88.7 7.3 collective-permute-done.6
  97.3 4.6 collective-permute-done.7
  103.2 5.5 collective-permute-done.8
  110.0 6.4 collective-permute-done.9
  117.7 11.0 %collective-permute-done.10 = bf16[32,64]{1,0:T(8,128)(2,1)S(1)} collective-permute-done((bf16[32,64]{1,0:T(8,128)(2,1)S(1)}, bf16[32,64]{1,0:T(8,128)(2,1)S(1)}, u32[]{:S(2)}, u32[]{:S(2)}) %collective-permute-start.10) | collective-permute-done | bytes 4128 | tf_op jit(solution)/shard_map/ppermute | solution.py:15
  130.0 3.0 collective-permute-done.15
  136.7 4.2 collective-permute-start.16
  142.2 6.1 collective-permute-done.17
  150.0 15.6 %collective-permute-start.19 = (bf16[40,64,4]{1,0,2:T(8,128)(2,1)S(1)}, bf16[40,64,4]{1,0,2:T(8,128)(2,1)S(1)}, u32[]{:S(2)}, u32[]{:S(2)}) collective-permute-start(bf16[40,64,4]{1,0,2:T(8,128)(2,1)S(1)} %copy.153), channel_id=1, source_target_pairs={{1,0},{2,1},{3,2},{5,4},{6,5},{7,6},{9,8},{10,9},{11,10},{13,12},{... | collective-permute-start | bytes 61448 | tf_op jit(solution)/shard_map/ppermute | solution.py:26
  178.5 3.6 collective-permute-start.20
  183.4 3.8 collective-permute-done.21
  189.1 3.8 collective-permute-start.22
  212.1 3.4 collective-permute-start.24
  228.6 5.3 collective-permute-start.26
  243.9 2.9 collective-permute-start.28
  254.9 5.8 collective-permute-start.30
  277.5 297.7 %psum.38 = f32[64,128]{1,0:T(8,128)S(1)} all-reduce(f32[64,128]{1,0:T(8,128)S(1)} %get-tuple-element.30), channel_id=1, replica_groups=mesh['bins'=64,'band'=4] {'bins'}, use_global_device_ids=true, to_apply=%region_6.7 | all-reduce | flops 8192 | bytes 65536 | tf_op jit(solution)/shard_map/psum | solution.py:161
  583.6 14.9 %collective-permute-start.41 = (f32[32,64]{1,0:T(8,128)S(1)}, f32[32,64]{1,0:T(8,128)S(1)}, u32[]{:S(2)}, u32[]{:S(2)}) collective-permute-start(f32[32,64]{1,0:T(8,128)S(1)} %get-tuple-element.51), channel_id=1, source_target_pairs={{0,40},{4,44},{8,48},{12,52},{16,56},{20,60},{24,64},{28,68},{32,7... | collective-permute-start | bytes 24584 | tf_op jit(solution)/shard_map/ppermute | solution.py:15
  599.9 4.2 collective-permute-start.39
  605.7 2.9 collective-permute-start.37
  608.6 4.9 collective-permute-start.36
  613.5 3.4 collective-permute-start.35
  616.9 3.7 collective-permute-start.34
  620.7 3.9 collective-permute-start.33
  625.8 68.1 %psum.35 = f32[32,64]{1,0:T(8,128)S(1)} all-reduce(f32[32,64]{1,0:T(8,128)S(1)} %convolution_add_fusion.32), channel_id=1, replica_groups=mesh['bins'=64,'band'=4] {'band'}, use_global_device_ids=true, to_apply=%region_2.3 | all-reduce | flops 2048 | bytes 16384 | tf_op jit(solution)/shard_map/psum | solution.py:160
  693.9 76.8 %all-reduce.3 = (f32[64,64]{0,1:T(8,128)S(1)}, f32[64,64]{0,1:T(8,128)S(1)}) all-reduce(f32[64,64]{0,1:T(8,128)S(1)} %convolution_bitcast_fusion.19, f32[64,64]{0,1:T(8,128)S(1)} %convolution_bitcast_fusion.18), channel_id=1, replica_groups=mesh['bins'=64,'band'=4] {'bins','band'}, use_global_device_ids=true, to_apply=%region_3.4 | all-reduce | flops 8192 | bytes 65536 | tf_op jit(solution)/shard_map/psum | solution.py:164
  (258 shorter events, 121.5 us)
Async XLA Ops:
  7.2 765.6 %all-reduce.6.cloned.1.call-start = ((), (), s32[]{:S(2)}) async-start(), calls=%async_computation | async-start | bytes 1179648 | tf_op jit(solution)/shard_map/psum | solution.py:164
  8.7 121.3 %collective-permute-start.14 = (bf16[32,64]{1,0:T(8,128)(2,1)S(1)}, bf16[32,64]{1,0:T(8,128)(2,1)S(1)}, u32[]{:S(2)}, u32[]{:S(2)}) collective-permute-start(bf16[32,64]{1,0:T(8,128)(2,1)S(1)} %get-tuple-element.71), channel_id=1, source_target_pairs={{60,0},{64,4},{68,8},{72,12},{76,16},{80,20},{84,24},{88,28},{92,3... | collective-permute-start | bytes 12296 | tf_op jit(solution)/shard_map/ppermute | solution.py:15
  10.0 120.0 %collective-permute-start.13 = (bf16[32,64]{1,0:T(8,128)(2,1)S(1)}, bf16[32,64]{1,0:T(8,128)(2,1)S(1)}, u32[]{:S(2)}, u32[]{:S(2)}) collective-permute-start(bf16[32,64]{1,0:T(8,128)(2,1)S(1)} %get-tuple-element.71), channel_id=1, source_target_pairs={{56,0},{60,4},{64,8},{68,12},{72,16},{76,20},{80,24},{84,28},{88,3... | collective-permute-start | bytes 12296 | tf_op jit(solution)/shard_map/ppermute | solution.py:15
  11.3 118.7 %collective-permute-start.12 = (bf16[32,64]{1,0:T(8,128)(2,1)S(1)}, bf16[32,64]{1,0:T(8,128)(2,1)S(1)}, u32[]{:S(2)}, u32[]{:S(2)}) collective-permute-start(bf16[32,64]{1,0:T(8,128)(2,1)S(1)} %get-tuple-element.71), channel_id=1, source_target_pairs={{52,0},{56,4},{60,8},{64,12},{68,16},{72,20},{76,24},{80,28},{84,3... | collective-permute-start | bytes 12296 | tf_op jit(solution)/shard_map/ppermute | solution.py:15
  12.6 117.3 %collective-permute-start.11 = (bf16[32,64]{1,0:T(8,128)(2,1)S(1)}, bf16[32,64]{1,0:T(8,128)(2,1)S(1)}, u32[]{:S(2)}, u32[]{:S(2)}) collective-permute-start(bf16[32,64]{1,0:T(8,128)(2,1)S(1)} %get-tuple-element.71), channel_id=1, source_target_pairs={{48,0},{52,4},{56,8},{60,12},{64,16},{68,20},{72,24},{76,28},{80,3... | collective-permute-start | bytes 12296 | tf_op jit(solution)/shard_map/ppermute | solution.py:15
  19.6 31.1 %collective-permute-start.1 = (bf16[32,64]{1,0:T(8,128)(2,1)S(1)}, bf16[32,64]{1,0:T(8,128)(2,1)S(1)}, u32[]{:S(2)}, u32[]{:S(2)}) collective-permute-start(bf16[32,64]{1,0:T(8,128)(2,1)S(1)} %get-tuple-element.71), channel_id=1, source_target_pairs={{8,0},{12,4},{16,8},{20,12},{24,16},{28,20},{32,24},{36,28},{40,32... | collective-permute-start | bytes 12296 | tf_op jit(solution)/shard_map/ppermute | solution.py:15
  57.7 8.3 %collective-permute-start.3 = (bf16[32,64]{1,0:T(8,128)(2,1)S(1)}, bf16[32,64]{1,0:T(8,128)(2,1)S(1)}, u32[]{:S(2)}, u32[]{:S(2)}) collective-permute-start(bf16[32,64]{1,0:T(8,128)(2,1)S(1)} %get-tuple-element.71), channel_id=1, source_target_pairs={{16,0},{20,4},{24,8},{28,12},{32,16},{36,20},{40,24},{44,28},{48,3... | collective-permute-start | bytes 12296 | tf_op jit(solution)/shard_map/ppermute | solution.py:15
  66.0 11.9 %collective-permute-start.4 = (bf16[32,64]{1,0:T(8,128)(2,1)S(1)}, bf16[32,64]{1,0:T(8,128)(2,1)S(1)}, u32[]{:S(2)}, u32[]{:S(2)}) collective-permute-start(bf16[32,64]{1,0:T(8,128)(2,1)S(1)} %get-tuple-element.71), channel_id=1, source_target_pairs={{20,0},{24,4},{28,8},{32,12},{36,16},{40,20},{44,24},{48,28},{52,3... | collective-permute-start | bytes 12296 | tf_op jit(solution)/shard_map/ppermute | solution.py:15
  77.9 9.5 %collective-permute-start.5 = (bf16[32,64]{1,0:T(8,128)(2,1)S(1)}, bf16[32,64]{1,0:T(8,128)(2,1)S(1)}, u32[]{:S(2)}, u32[]{:S(2)}) collective-permute-start(bf16[32,64]{1,0:T(8,128)(2,1)S(1)} %get-tuple-element.71), channel_id=1, source_target_pairs={{24,0},{28,4},{32,8},{36,12},{40,16},{44,20},{48,24},{52,28},{56,3... | collective-permute-start | bytes 12296 | tf_op jit(solution)/shard_map/ppermute | solution.py:15
  87.4 8.6 %collective-permute-start.6 = (bf16[32,64]{1,0:T(8,128)(2,1)S(1)}, bf16[32,64]{1,0:T(8,128)(2,1)S(1)}, u32[]{:S(2)}, u32[]{:S(2)}) collective-permute-start(bf16[32,64]{1,0:T(8,128)(2,1)S(1)} %get-tuple-element.71), channel_id=1, source_target_pairs={{28,0},{32,4},{36,8},{40,12},{44,16},{48,20},{52,24},{56,28},{60,3... | collective-permute-start | bytes 12296 | tf_op jit(solution)/shard_map/ppermute | solution.py:15
  108.7 7.7 collective-permute-start.9
  116.4 12.3 %collective-permute-start.10 = (bf16[32,64]{1,0:T(8,128)(2,1)S(1)}, bf16[32,64]{1,0:T(8,128)(2,1)S(1)}, u32[]{:S(2)}, u32[]{:S(2)}) collective-permute-start(bf16[32,64]{1,0:T(8,128)(2,1)S(1)} %get-tuple-element.71), channel_id=1, source_target_pairs={{44,0},{48,4},{52,8},{56,12},{60,16},{64,20},{68,24},{72,28},{76,3... | collective-permute-start | bytes 12296 | tf_op jit(solution)/shard_map/ppermute | solution.py:15
  150.0 21.3 %collective-permute-start.19 = (bf16[40,64,4]{1,0,2:T(8,128)(2,1)S(1)}, bf16[40,64,4]{1,0,2:T(8,128)(2,1)S(1)}, u32[]{:S(2)}, u32[]{:S(2)}) collective-permute-start(bf16[40,64,4]{1,0,2:T(8,128)(2,1)S(1)} %copy.153), channel_id=1, source_target_pairs={{1,0},{2,1},{3,2},{5,4},{6,5},{7,6},{9,8},{10,9},{11,10},{13,12},{... | collective-permute-start | bytes 61448 | tf_op jit(solution)/shard_map/ppermute | solution.py:26
  189.1 12.7 %collective-permute-start.22 = (bf16[40,64,4]{1,0,2:T(8,128)(2,1)}, bf16[40,64,4]{1,0,2:T(8,128)(2,1)S(1)}, u32[]{:S(2)}, u32[]{:S(2)}) collective-permute-start(bf16[40,64,4]{1,0,2:T(8,128)(2,1)} %copy.165), channel_id=1, source_target_pairs={{0,1},{1,2},{2,3},{4,5},{5,6},{6,7},{8,9},{9,10},{10,11},{12,13},{... | collective-permute-start | bytes 61448 | tf_op jit(solution)/shard_map/ppermute | solution.py:23
  193.2 9.8 %collective-permute-start.23 = (bf16[40,64,4]{1,0,2:T(8,128)(2,1)S(1)}, bf16[40,64,4]{1,0,2:T(8,128)(2,1)S(1)}, u32[]{:S(2)}, u32[]{:S(2)}) collective-permute-start(bf16[40,64,4]{1,0,2:T(8,128)(2,1)S(1)} %copy.166), channel_id=1, source_target_pairs={{1,0},{2,1},{3,2},{5,4},{6,5},{7,6},{9,8},{10,9},{11,10},{13,12},{... | collective-permute-start | bytes 61448 | tf_op jit(solution)/shard_map/ppermute | solution.py:26
  212.1 7.5 collective-permute-start.24
  226.7 9.6 %collective-permute-start.27 = (bf16[40,64,4]{1,0,2:T(8,128)(2,1)}, bf16[40,64,4]{1,0,2:T(8,128)(2,1)}, u32[]{:S(2)}, u32[]{:S(2)}) collective-permute-start(bf16[40,64,4]{1,0,2:T(8,128)(2,1)} %copy.179), channel_id=1, source_target_pairs={{1,0},{2,1},{3,2},{5,4},{6,5},{7,6},{9,8},{10,9},{11,10},{13,12},{... | collective-permute-start | bytes 61448 | tf_op jit(solution)/shard_map/ppermute | solution.py:26
  243.9 7.4 collective-permute-start.28
  252.9 9.1 %collective-permute-start.31 = (bf16[40,64,4]{1,0,2:T(8,128)(2,1)S(1)}, bf16[40,64,4]{1,0,2:T(8,128)(2,1)S(1)}, u32[]{:S(2)}, u32[]{:S(2)}) collective-permute-start(bf16[40,64,4]{1,0,2:T(8,128)(2,1)S(1)} %copy.192), channel_id=1, source_target_pairs={{1,0},{2,1},{3,2},{5,4},{6,5},{7,6},{9,8},{10,9},{11,10},{13,12},{... | collective-permute-start | bytes 61448 | tf_op jit(solution)/shard_map/ppermute | solution.py:26
  274.6 305.8 %collective-permute-start.32 = (f32[32,64]{1,0:T(8,128)S(1)}, f32[32,64]{1,0:T(8,128)S(1)}, u32[]{:S(2)}, u32[]{:S(2)}) collective-permute-start(f32[32,64]{1,0:T(8,128)S(1)} %get-tuple-element.44), channel_id=1, source_target_pairs={{0,4},{4,8},{8,12},{12,16},{16,20},{20,24},{24,28},{28,32},{32,36}... | collective-permute-start | bytes 24584 | tf_op jit(solution)/shard_map/ppermute | solution.py:15
  577.8 20.8 %collective-permute-start.45 = (f32[32,64]{1,0:T(8,128)S(1)}, f32[32,64]{1,0:T(8,128)S(1)}, u32[]{:S(2)}, u32[]{:S(2)}) collective-permute-start(f32[32,64]{1,0:T(8,128)S(1)} %get-tuple-element.47), channel_id=1, source_target_pairs={{0,56},{4,60},{8,64},{12,68},{16,72},{20,76},{24,80},{28,84},{32,8... | collective-permute-start | bytes 24584 | tf_op jit(solution)/shard_map/ppermute | solution.py:15
  579.1 20.8 %collective-permute-start.44 = (f32[32,64]{1,0:T(8,128)S(1)}, f32[32,64]{1,0:T(8,128)S(1)}, u32[]{:S(2)}, u32[]{:S(2)}) collective-permute-start(f32[32,64]{1,0:T(8,128)S(1)} %get-tuple-element.48), channel_id=1, source_target_pairs={{0,52},{4,56},{8,60},{12,64},{16,68},{20,72},{24,76},{28,80},{32,8... | collective-permute-start | bytes 24584 | tf_op jit(solution)/shard_map/ppermute | solution.py:15
  580.4 23.7 %collective-permute-start.43 = (f32[32,64]{1,0:T(8,128)S(1)}, f32[32,64]{1,0:T(8,128)S(1)}, u32[]{:S(2)}, u32[]{:S(2)}) collective-permute-start(f32[32,64]{1,0:T(8,128)S(1)} %get-tuple-element.49), channel_id=1, source_target_pairs={{0,48},{4,52},{8,56},{12,60},{16,64},{20,68},{24,72},{28,76},{32,8... | collective-permute-start | bytes 24584 | tf_op jit(solution)/shard_map/ppermute | solution.py:15
  582.3 23.4 %collective-permute-start.42 = (f32[32,64]{1,0:T(8,128)S(1)}, f32[32,64]{1,0:T(8,128)S(1)}, u32[]{:S(2)}, u32[]{:S(2)}) collective-permute-start(f32[32,64]{1,0:T(8,128)S(1)} %get-tuple-element.50), channel_id=1, source_target_pairs={{0,44},{4,48},{8,52},{12,56},{16,60},{20,64},{24,68},{28,72},{32,7... | collective-permute-start | bytes 24584 | tf_op jit(solution)/shard_map/ppermute | solution.py:15
  583.6 25.0 %collective-permute-start.41 = (f32[32,64]{1,0:T(8,128)S(1)}, f32[32,64]{1,0:T(8,128)S(1)}, u32[]{:S(2)}, u32[]{:S(2)}) collective-permute-start(f32[32,64]{1,0:T(8,128)S(1)} %get-tuple-element.51), channel_id=1, source_target_pairs={{0,40},{4,44},{8,48},{12,52},{16,56},{20,60},{24,64},{28,68},{32,7... | collective-permute-start | bytes 24584 | tf_op jit(solution)/shard_map/ppermute | solution.py:15
  598.6 14.9 %collective-permute-start.40 = (f32[32,64]{1,0:T(8,128)S(1)}, f32[32,64]{1,0:T(8,128)S(1)}, u32[]{:S(2)}, u32[]{:S(2)}) collective-permute-start(f32[32,64]{1,0:T(8,128)S(1)} %get-tuple-element.52), channel_id=1, source_target_pairs={{0,36},{4,40},{8,44},{12,48},{16,52},{20,56},{24,60},{28,64},{32,6... | collective-permute-start | bytes 24584 | tf_op jit(solution)/shard_map/ppermute | solution.py:15
  599.9 17.0 %collective-permute-start.39 = (f32[32,64]{1,0:T(8,128)S(1)}, f32[32,64]{1,0:T(8,128)S(1)}, u32[]{:S(2)}, u32[]{:S(2)}) collective-permute-start(f32[32,64]{1,0:T(8,128)S(1)} %get-tuple-element.53), channel_id=1, source_target_pairs={{0,32},{4,36},{8,40},{12,44},{16,48},{20,52},{24,56},{28,60},{32,6... | collective-permute-start | bytes 24584 | tf_op jit(solution)/shard_map/ppermute | solution.py:15
  604.1 16.5 %collective-permute-start.38 = (f32[32,64]{1,0:T(8,128)S(1)}, f32[32,64]{1,0:T(8,128)S(1)}, u32[]{:S(2)}, u32[]{:S(2)}) collective-permute-start(f32[32,64]{1,0:T(8,128)S(1)} %get-tuple-element.54), channel_id=1, source_target_pairs={{0,28},{4,32},{8,36},{12,40},{16,44},{20,48},{24,52},{28,56},{32,6... | collective-permute-start | bytes 24584 | tf_op jit(solution)/shard_map/ppermute | solution.py:15
  605.7 19.1 %collective-permute-start.37 = (f32[32,64]{1,0:T(8,128)S(1)}, f32[32,64]{1,0:T(8,128)S(1)}, u32[]{:S(2)}, u32[]{:S(2)}) collective-permute-start(f32[32,64]{1,0:T(8,128)S(1)} %get-tuple-element.55), channel_id=1, source_target_pairs={{0,24},{4,28},{8,32},{12,36},{16,40},{20,44},{24,48},{28,52},{32,5... | collective-permute-start | bytes 24584 | tf_op jit(solution)/shard_map/ppermute | solution.py:15
  608.6 16.2 %collective-permute-start.36 = (f32[32,64]{1,0:T(8,128)S(1)}, f32[32,64]{1,0:T(8,128)S(1)}, u32[]{:S(2)}, u32[]{:S(2)}) collective-permute-start(f32[32,64]{1,0:T(8,128)S(1)} %get-tuple-element.56), channel_id=1, source_target_pairs={{0,20},{4,24},{8,28},{12,32},{16,36},{20,40},{24,44},{28,48},{32,5... | collective-permute-start | bytes 24584 | tf_op jit(solution)/shard_map/ppermute | solution.py:15
  613.5 11.3 %collective-permute-start.35 = (f32[32,64]{1,0:T(8,128)S(1)}, f32[32,64]{1,0:T(8,128)S(1)}, u32[]{:S(2)}, u32[]{:S(2)}) collective-permute-start(f32[32,64]{1,0:T(8,128)S(1)} %get-tuple-element.57), channel_id=1, source_target_pairs={{0,16},{4,20},{8,24},{12,28},{16,32},{20,36},{24,40},{28,44},{32,4... | collective-permute-start | bytes 24584 | tf_op jit(solution)/shard_map/ppermute | solution.py:15
  616.9 7.9 %collective-permute-start.34 = (f32[32,64]{1,0:T(8,128)S(1)}, f32[32,64]{1,0:T(8,128)S(1)}, u32[]{:S(2)}, u32[]{:S(2)}) collective-permute-start(f32[32,64]{1,0:T(8,128)S(1)} %get-tuple-element.58), channel_id=1, source_target_pairs={{0,12},{4,16},{8,20},{12,24},{16,28},{20,32},{24,36},{28,40},{32,4... | collective-permute-start | bytes 24584 | tf_op jit(solution)/shard_map/ppermute | solution.py:15
  (41 other events, 1136.2 us)
Sparse Core Ops, SparseCore 0:
  261.8 258.7 all-reduce.5
where the time goes:
time: 792 us; the launch traced here: 782 us
  blocking collectives  443 us (56%)
  starting transfers between devices  155 us (20%)
  waiting for transfers between devices  87.9 us (11%)
  local copies, waits for them, and re-layouts  32.2 us (4%)
  matrix products  26.4 us (3%)
  between operations  25.1 us (3%)
  other arithmetic  12.6 us (2%)
    psum x1, blocking collectives, per_device(): offset_sum = lax.psum(offset_part, 'bins')  298 us
    ppermute x32, starting transfers between devices, passed_along(): return lax.ppermute(block, axis, route)  97.2 us
    ppermute x32, waiting for transfers between devices, passed_along(): return lax.ppermute(block, axis, route)  77 us
    psum x1, blocking collectives, per_device(): lax.psum((jnp.stack(kernel_grads), left_part, right_part), ('bins', 'band'))  76.8 us
    psum x1, blocking collectives, per_device(): grad_features = lax.psum(feature_part, 'band') / math.sqrt(total_band)  68.1 us
    ppermute x8, starting transfers between devices, with_halo(): lax.ppermute(lax.slice_in_dim(block, block.shape[dim] - width, None, axis...  31.2 us
    ppermute x8, starting transfers between devices, with_halo(): lax.ppermute(lax.slice_in_dim(block, 0, width, axis=dim), axis, backward)  26.7 us
  transfers between devices with their start and end apart: 49, of which 18 were waited for; matrix products, arithmetic and copies ran while one was open for 4% of the time, Pallas kernels for 0%

commit v1 on v0

v1 whole, which is shorter than its diff:
```python
import functools
import math

import jax
import jax.numpy as jnp
from jax import lax
from jax.experimental import pallas as pl
from jax.experimental.pallas import tpu as pltpu
from jax.sharding import PartitionSpec as P

LAYERS = 2
MAXDIL = 4
F32 = jnp.float32
BF16 = jnp.bfloat16
WIDE = 256
RIM0 = 16
RIM1 = 12
RIM2 = 8
RIM3 = 4
LIMIT = 56 * 1024 * 1024


def sigmoid(value):
    return 0.5 * jnp.tanh(0.5 * value) + 0.5


def turned(value, amount):
    return pltpu.roll(value, amount, 1)


def row_mask(bin_id, first_offset, total_bins, total_band, lanes):
    lane = lax.broadcasted_iota(jnp.int32, (1, lanes), 1)
    offset = first_offset + jnp.where(lane < 192, lane, lane - WIDE)
    top = jnp.minimum(total_band, total_bins - bin_id)
    top = jnp.where(bin_id >= 0, top, 0)
    return jnp.where((offset >= 0) & (offset < top), 1.0, 0.0).astype(F32)


def forward_kernel(
    rows, channels, total_bins, total_band,
    place, dil, lo, own, hi, w0, w1, w2, w3, w4, w5, w6, lw, rw, emb_lo, emb, emb_hi, taps,
    s0, s1, slope_s, slope0, proj,
):
    c = channels
    first_bin = place[0] * rows
    group = emb.shape[1]
    first_offset = place[1] * group
    fw = jnp.concatenate([w0[...], w1[...], w2[...], w3[...], w4[...], w5[...], w6[...]], 0)
    right = jnp.dot(fw, rw[...], preferred_element_type=F32).astype(BF16).astype(F32)
    near = jnp.concatenate([lo[...], own[...], hi[...]], 0)
    left = jnp.dot(near, lw[...], preferred_element_type=F32).astype(BF16).astype(F32)
    right = jnp.concatenate([right, jnp.zeros((WIDE - right.shape[0], c), F32)], 0)
    left = jnp.concatenate([left, jnp.zeros((WIDE - left.shape[0], c), F32)], 0)
    proj[...] = jnp.concatenate([right, left], 1).T
    lane = lax.broadcasted_iota(jnp.int32, (1, group), 1)
    beside = jnp.where(lane < group // 2, emb_hi[...].astype(F32), emb_lo[...].astype(F32))
    embed = jnp.concatenate([emb[...].astype(F32), beside], 1)

    def state_row(row, carry):
        bin_id = first_bin - RIM0 + row
        lag = turned(proj[0:c, :], WIDE - RIM0 - row)
        mine = turned(proj[c : 2 * c, :], WIDE - rows + RIM0 - row)[:, 0:1]
        summed = mine + lag + embed
        sig = sigmoid(summed)
        mask = row_mask(bin_id, first_offset, total_bins, total_band, WIDE)
        at = pl.ds(pl.multiple_of(row * c, c), c)
        s0[at, :] = (summed * sig * mask).astype(BF16)

        @pl.when((row >= RIM0) & (row < RIM0 + rows))
        def _():
            slope = sig * (1.0 + summed * (1.0 - sig)) * mask
            slope_s[pl.ds(pl.multiple_of((row - RIM0) * c, c), c), :] = slope[:, 0:group]

        return carry

    lax.fori_loop(0, rows + 2 * RIM0, state_row, 0)

    rate = dil[0]

    def layer_row(row, carry):
        bin_id = first_bin - RIM1 + row
        base = row + RIM0 - RIM1
        view = jnp.concatenate(
            [s0[pl.ds(pl.multiple_of((base + rate * k) * c, c), c), :] for k in (-1, 0, 1)], 0
        )
        parts = jnp.dot(taps[0], view, preferred_element_type=F32)
        pre = (
            turned(parts[0:c], rate) + parts[c : 2 * c] + turned(parts[2 * c : 3 * c], WIDE - rate)
        )
        sig = sigmoid(pre)
        mask = row_mask(bin_id, first_offset, total_bins, total_band, WIDE)
        at = pl.ds(pl.multiple_of(row * c, c), c)
        s1[at, :] = (pre * sig * mask).astype(BF16)
        slope0[at, :] = sig * (1.0 + pre * (1.0 - sig)) * mask
        return carry

    lax.fori_loop(0, rows + 2 * RIM1, layer_row, 0)


def backward_kernel(
    rows, channels, total_bins, total_band,
    place, dil, s0, s1, slope_s, slope0, cot, taps, back_taps, lo, own, w1, w2, w3, w4, w5, lw, rw,
    pair_map, payload, feature_left, feature_right,
    g1, g0, sums, edge,
):
    c = channels
    first_bin = place[0] * rows
    group = pair_map.shape[2]
    first_offset = place[1] * group
    rate0, rate1 = dil[0], dil[1]

    def layer_row(row, carry):
        bin_id = first_bin - RIM2 + row
        base = row + RIM1 - RIM2
        view = jnp.concatenate(
            [s1[pl.ds(pl.multiple_of((base + rate1 * k) * c, c), c), :] for k in (-1, 0, 1)], 0
        )
        parts = jnp.dot(taps[1], view, preferred_element_type=F32)
        pre = (
            turned(parts[0:c], rate1)
            + parts[c : 2 * c]
            + turned(parts[2 * c : 3 * c], WIDE - rate1)
        )
        sig = sigmoid(pre)
        mask = row_mask(bin_id, first_offset, total_bins, total_band, WIDE)
        slope = sig * (1.0 + pre * (1.0 - sig)) * mask
        g1[pl.ds(pl.multiple_of(row * c, c), c), :] = (cot[row].astype(F32) * slope).astype(BF16)

        @pl.when((row >= RIM2) & (row < RIM2 + rows))
        def _():
            pair_map[row - RIM2] = (pre * sig * mask).astype(BF16)[:, 0:group]

        return carry

    lax.fori_loop(0, rows + 2 * RIM2, layer_row, 0)

    def back_parts(layer, rate, grads, base):
        view = jnp.concatenate(
            [grads[pl.ds(pl.multiple_of((base - rate * k) * c, c), c), :] for k in (-1, 0, 1)], 0
        )
        parts = jnp.dot(back_taps[layer], view, preferred_element_type=F32)
        return (
            turned(parts[0:c], WIDE - rate) + parts[c : 2 * c] + turned(parts[2 * c : 3 * c], rate)
        )

    def back_row(row, carry):
        back = back_parts(1, rate1, g1, row + RIM2 - RIM3)
        at = pl.ds(pl.multiple_of((row + RIM1 - RIM3) * c, c), c)
        g0[pl.ds(pl.multiple_of(row * c, c), c), :] = (back * slope0[at, :]).astype(BF16)
        return carry

    lax.fori_loop(0, rows + 2 * RIM3, back_row, 0)

    def tap_sums(rate, state, rim_s, grads, rim_g):
        def one(row, total):
            view = jnp.concatenate(
                [
                    state[pl.ds(pl.multiple_of((row + rim_s + rate * k) * c, c), c), :]
                    for k in (-1, 0, 1)
                ],
                0,
            )
            grad = grads[pl.ds(pl.multiple_of((row + rim_g) * c, c), c), 0:group].astype(F32)
            grad = jnp.concatenate([grad, jnp.zeros((c, WIDE - group), F32)], 1)
            shifted = jnp.concatenate(
                [turned(grad, WIDE - rate), grad, turned(grad, rate)], 0
            ).astype(BF16)
            return total + lax.dot_general(
                view, shifted, (((1,), (1,)), ((), ())), preferred_element_type=F32
            )

        return lax.fori_loop(0, rows, one, jnp.zeros((3 * c, 3 * c), F32))

    total1 = tap_sums(rate1, s1, RIM1, g1, RIM2)
    payload[3 * c : 6 * c, :] = total1[:, 0:128]
    edge[...] = total1[:, 128 : 3 * c]
    total0 = tap_sums(rate0, s0, RIM0, g0, RIM3)
    payload[0 : 3 * c, :] = total0[:, 0:128]
    payload[6 * c : 9 * c, :] = jnp.concatenate([total0[:, 128 : 3 * c], edge[...]], 1)

    lane = lax.broadcasted_iota(jnp.int32, (1, 128), 1)
    sums[...] = jnp.zeros_like(sums)

    def last_row(row, carry):
        back = back_parts(0, rate0, g0, row + RIM3)
        at = pl.ds(pl.multiple_of(row * c, c), c)
        grad = back[:, 0:group] * slope_s[at, :]
        sums[:, 0:128] += jnp.where(lane == row, jnp.sum(grad, axis=1, keepdims=True), 0.0)
        wide = jnp.concatenate([grad, jnp.zeros((c, WIDE - group), F32)], 1)
        sums[:, 128 : 128 + WIDE] += turned(wide, row)
        sums[:, 128 + WIDE : 256 + WIDE] += grad
        return carry

    lax.fori_loop(0, rows, last_row, 0)

    highest = lax.Precision.HIGHEST
    both = sums[:, 0 : 128 + WIDE]
    both = jnp.concatenate([both, jnp.zeros_like(both)], 0).T
    left_grad = both[0:rows, 0:c]
    right_grad = both[128 : 128 + rows + group, 0:c]
    window = jnp.concatenate([w1[...], w2[...], w3[...], w4[...], w5[...]], 0).astype(F32)
    feats = jnp.concatenate([own[...].astype(F32), window], 0)
    feats = jnp.concatenate([feats, jnp.zeros((WIDE - feats.shape[0], c), F32)], 0)
    feats = jnp.concatenate([feats, jnp.zeros_like(feats)], 1).T[0:c]
    grad_left = jnp.dot(feats[:, 0:rows], left_grad, precision=highest, preferred_element_type=F32)
    grad_right = jnp.dot(
        feats[:, rows : 2 * rows + group], right_grad, precision=highest,
        preferred_element_type=F32,
    )
    payload[9 * c : 10 * c, :] = jnp.concatenate([grad_left, grad_right], 1)
    payload[10 * c :, :] = jnp.zeros((payload.shape[0] - 10 * c, 128), F32)
    at = pl.ds(pl.multiple_of((10 + place[1]) * c, c), c)
    payload[at, :] = sums[:, 128 + WIDE : 256 + WIDE]
    transposed = (((1,), (1,)), ((), ()))
    feature_left[...] = lax.dot_general(
        left_grad, lw[...].astype(F32), transposed, precision=highest, preferred_element_type=F32
    )
    feature_right[...] = lax.dot_general(
        right_grad, rw[...].astype(F32), transposed, precision=highest, preferred_element_type=F32
    ).reshape(feature_right.shape)


def unpack_kernel(channels, whole_scale, offset_scale, place, total, left, right, offset, kernels):
    c = channels
    for layer in range(2):
        for p in range(3):
            main = total[(3 * layer + p) * c : (3 * layer + p + 1) * c, :] * whole_scale
            rest = total[(6 + p) * c : (7 + p) * c, :] * whole_scale
            kernels[layer, p, 0] = main[:, 0:c]
            kernels[layer, p, 1] = main[:, c : 2 * c]
            kernels[layer, p, 2] = rest[:, layer * c : (layer + 1) * c]
    both = total[9 * c : 10 * c, :] * whole_scale
    left[...] = both[:, 0:c]
    right[...] = both[:, c : 2 * c]
    at = pl.ds(pl.multiple_of((10 + place[1]) * c, c), c)
    offset[...] = total[at, :] * offset_scale


def per_device(features, left_weight, right_weight, offset_embed, kernels, dilation, cotangent):
    rows, c = features.shape
    group = offset_embed.shape[1]
    bins, band = lax.axis_size("bins"), lax.axis_size("band")
    devices = bins * band
    total_bins, total_band = rows * bins, group * band
    blocks = group // rows
    every = ("bins", "band")
    place = jnp.stack([lax.axis_index("bins"), lax.axis_index("band")]).astype(jnp.int32)

    def joint(bin_step, band_step, skew=0):
        route = []
        for i in range(bins):
            for b in range(band):
                i2, b2 = i + bin_step + skew * b, b + band_step
                if 0 <= i2 < bins and 0 <= b2 < band:
                    route.append((i2 * band + b2, i * band + b))
        return route

    def fetch(block, bin_step, band_step, skew=0):
        return lax.ppermute(block, every, joint(bin_step, band_step, skew))

    def deliver(block, bin_step, skew):
        route = [(target, source) for source, target in joint(bin_step, 0, skew)]
        return lax.ppermute(block, every, route)

    window = [fetch(features, k, 0, blocks) for k in range(-1, blocks + 2)]
    lo, hi = fetch(features, -1, 0), fetch(features, 1, 0)
    emb_lo, emb_hi = fetch(offset_embed, 0, -1), fetch(offset_embed, 0, 1)
    cot_rows = jnp.concatenate(
        [fetch(cotangent[rows - RIM2 :], -1, 0), cotangent, fetch(cotangent[:RIM2], 1, 0)], 0
    )
    cot_lo = fetch(cot_rows[:, :, group - RIM2 :], 0, -1)
    cot_hi = fetch(cot_rows[:, :, :RIM2], 0, 1)
    gap = jnp.zeros((rows + 2 * RIM2, c, WIDE - group - 2 * RIM2), BF16)
    cot = jnp.concatenate([cot_rows, cot_hi, gap, cot_lo], 2)

    taps = jnp.transpose(kernels, (0, 2, 4, 1, 3)).reshape(LAYERS, 3 * c, 3 * c)
    back_taps = jnp.transpose(kernels, (0, 2, 3, 1, 4)).reshape(LAYERS, 3 * c, 3 * c)

    smem = pl.BlockSpec(memory_space=pltpu.SMEM)
    vmem = pl.BlockSpec(memory_space=pltpu.VMEM)
    s0, s1, slope_s, slope0 = pl.pallas_call(
        functools.partial(forward_kernel, rows, c, total_bins, total_band),
        out_shape=(
            jax.ShapeDtypeStruct(((rows + 2 * RIM0) * c, WIDE), BF16),
            jax.ShapeDtypeStruct(((rows + 2 * RIM1) * c, WIDE), BF16),
            jax.ShapeDtypeStruct((rows * c, group), F32),
            jax.ShapeDtypeStruct(((rows + 2 * RIM1) * c, WIDE), F32),
        ),
        in_specs=[smem] * 2 + [vmem] * 16,
        out_specs=(vmem,) * 4,
        scratch_shapes=[pltpu.VMEM((2 * c, WIDE), F32)],
        compiler_params=pltpu.CompilerParams(vmem_limit_bytes=LIMIT),
        name="forward",
    )(
        place, dilation, lo, features, hi, *window, left_weight, right_weight,
        emb_lo, offset_embed, emb_hi, taps,
    )
    slots = 4 * devices
    pair_map, payload, feature_left, feature_right = pl.pallas_call(
        functools.partial(backward_kernel, rows, c, total_bins, total_band),
        out_shape=(
            jax.ShapeDtypeStruct((rows, c, group), BF16),
            jax.ShapeDtypeStruct((slots, 128), F32),
            jax.ShapeDtypeStruct((rows, c), F32),
            jax.ShapeDtypeStruct((blocks + 1, rows, c), F32),
        ),
        in_specs=[smem] * 2 + [vmem] * 16,
        out_specs=(vmem,) * 4,
        scratch_shapes=[
            pltpu.VMEM(((rows + 2 * RIM2) * c, WIDE), BF16),
            pltpu.VMEM(((rows + 2 * RIM3) * c, WIDE), BF16),
            pltpu.VMEM((c, 256 + WIDE), F32),
            pltpu.VMEM((3 * c, 3 * c - 128), F32),
        ],
        compiler_params=pltpu.CompilerParams(vmem_limit_bytes=LIMIT),
        name="backward",
    )(
        place, dilation, s0, s1, slope_s, slope0, cot, taps, back_taps, lo, features,
        *window[1:6], left_weight, right_weight,
    )
    shares = lax.all_to_all(payload.reshape(devices, 4, 128), every, 0, 0, tiled=True)
    feature_sum = feature_left
    for k in range(blocks + 1):
        feature_sum = feature_sum + deliver(feature_right[k], k, blocks)
    feature_all = feature_sum
    for step in range(1, band):
        route = [(b, (b + step) % band) for b in range(band)]
        feature_all = feature_all + lax.ppermute(feature_sum, "band", route)
    share = jnp.broadcast_to(jnp.sum(shares, axis=0, keepdims=True), shares.shape)
    total = lax.all_to_all(share, every, 0, 0, tiled=True).reshape(slots, 128)
    whole_scale = 1.0 / math.sqrt(total_bins * total_band)
    grad_left, grad_right, grad_offset, grad_kernels = pl.pallas_call(
        functools.partial(unpack_kernel, c, whole_scale, 1.0 / math.sqrt(total_bins)),
        out_shape=(
            jax.ShapeDtypeStruct((c, c), F32),
            jax.ShapeDtypeStruct((c, c), F32),
            jax.ShapeDtypeStruct((c, group), F32),
            jax.ShapeDtypeStruct((LAYERS, 3, 3, c, c), F32),
        ),
        in_specs=[smem, vmem],
        out_specs=(vmem,) * 4,
        compiler_params=pltpu.CompilerParams(vmem_limit_bytes=LIMIT),
        name="unpack",
    )(place, total)
    return (
        pair_map,
        feature_all / math.sqrt(total_band),
        grad_left,
        grad_right,
        grad_offset,
        grad_kernels,
    )


def solution(mesh):
    return jax.shard_map(
        per_device,
        mesh=mesh,
        in_specs=(P("bins", None), P(), P(), P(None, "band"), P(), P(), P("bins", None, "band")),
        out_specs=(P("bins", None, "band"), P("bins", None), P(), P(), P(None, "band"), P()),
        check_vma=False,
    )
```

time: 792 us -> 241 us (0.30)
  blocking collectives: 443 us -> 54.4 us
  Pallas kernels: 0 us -> 93.1 us
  starting transfers between devices: 155 us -> 69.6 us
  waiting for transfers between devices: 87.9 us -> 5.99 us
  matrix products: 26.4 us -> 0 us
  between operations: 25.1 us -> 1.2 us
  local copies, waits for them, and re-layouts: 32.2 us -> 9.17 us
  other arithmetic: 12.6 us -> 3.37 us
    psum x3 -> x0, blocking collectives: 443 us -> none  [the longest x1 298 us: per_device(): offset_sum = lax.psum(offset_part, 'bins')]
    pallas_call x0 -> x3, Pallas kernels: none -> 93.1 us  [the longest x1 59.9 us: per_device(): pl.pallas_call(functools.partial(backward_kernel, rows, c, total_bins, to...]
    ppermute x48 -> x23, starting transfers between devices: 155 us -> 64.3 us  [the longest x15 35 us: fetch(): return lax.ppermute(block, every, joint(bin_step, band_step, skew))]
    ppermute x48 -> x23, waiting for transfers between devices: 87.9 us -> 5.99 us  [the longest x15 3.93 us: fetch(): return lax.ppermute(block, every, joint(bin_step, band_step, skew))]
    all_to_all x0 -> x1, blocking collectives: none -> 54.4 us  [per_device(): lax.all_to_all(payload.reshape(devices, 4, 128), every, 0, 0, tiled=True)]
    dot_general x60 -> x0, matrix products: 26.4 us -> none  [the longest x18 9.42 us: per_device(): jnp.einsum('icd,ce->ied', view, kernels[layer, row_tap, col_tap], preferr...]
  transfers between devices with their start and end apart: 49 -> 24, of which waited for: 18 -> 3; matrix products, arithmetic and copies ran while one was open for 4% -> 3% of each run, Pallas kernels for 0% -> 13%
where the time goes in v1:
time: 241 us; the launch traced here: 237 us
  Pallas kernels  93.1 us (39%)
  starting transfers between devices  69.6 us (29%)
  blocking collectives  54.4 us (23%)
  local copies, waits for them, and re-layouts  9.17 us (4%)
  waiting for transfers between devices  5.99 us (2%)
  other arithmetic  3.37 us (1%)
    pallas_call x1, Pallas kernels, per_device(): pl.pallas_call(functools.partial(backward_kernel, rows, c, total_bins, to...  59.9 us
    all_to_all x1, blocking collectives, per_device(): lax.all_to_all(payload.reshape(devices, 4, 128), every, 0, 0, tiled=True)  54.4 us
    ppermute x15, starting transfers between devices, fetch(): return lax.ppermute(block, every, joint(bin_step, band_step, skew))  35 us
    pallas_call x1, Pallas kernels, per_device(): pl.pallas_call(functools.partial(forward_kernel, rows, c, total_bins, tot...  31.1 us
    ppermute x5, starting transfers between devices, deliver(): return lax.ppermute(block, every, route)  26.4 us
    all_to_all x1, starting transfers between devices, per_device(): total = lax.all_to_all(share, every, 0, 0, tiled=True).reshape(slots, 128)  5.26 us
  transfers between devices with their start and end apart: 24, of which 3 were waited for; matrix products, arithmetic and copies ran while one was open for 3% of the time, Pallas kernels for 13%

profile of v1, /device:TPU:1, one launch (start us, length us, event | category | flops | bytes accessed | tf_op | source)
XLA Modules:
  0.0 236.7 jit_solution(1767326170501080658)
XLA Ops:
  0.6 1.0 fusion.1
  1.6 4.4 %collective-permute-start.11 = (bf16[8,64,128]{2,1,0:T(8,128)(2,1)S(1)}, bf16[8,64,128]{2,1,0:T(8,128)(2,1)S(1)}, u32[]{:S(2)}, u32[]{:S(2)}) collective-permute-start(bf16[8,64,128]{2,1,0:T(8,128)(2,1)S(1)} %get-tuple-element.33), channel_id=1, source_target_pairs={{0,4},{1,5},{2,6},{3,7},{4,8},{5,9},{6,10},{7,11},{8,12},{9,13},{1... | collective-permute-start | bytes 393224 | tf_op jit(solution)/shard_map/ppermute | solution.py:259
  6.0 1.3 collective-permute-start.8
  7.3 1.3 collective-permute-start.7
  8.6 1.3 collective-permute-start.6
  9.9 1.3 collective-permute-start.5
  11.2 1.3 collective-permute-start.12
  12.6 1.2 constant_dynamic-update-slice_fusion.1
  13.7 3.9 %collective-permute-done.12 = bf16[8,64,128]{2,1,0:T(8,128)(2,1)S(1)} collective-permute-done((bf16[8,64,128]{2,1,0:T(8,128)(2,1)S(1)}, bf16[8,64,128]{2,1,0:T(8,128)(2,1)S(1)}, u32[]{:S(2)}, u32[]{:S(2)}) %collective-permute-start.12) | collective-permute-done | bytes 131104 | tf_op jit(solution)/shard_map/ppermute | solution.py:259
  17.6 1.3 collective-permute-start.4
  19.0 1.3 collective-permute-start.3
  20.3 1.3 collective-permute-start.2
  21.6 1.3 collective-permute-start.1
  23.9 4.2 %collective-permute-start = (bf16[32,64]{1,0:T(8,128)(2,1)S(1)}, bf16[32,64]{1,0:T(8,128)(2,1)S(1)}, u32[]{:S(2)}, u32[]{:S(2)}) collective-permute-start(bf16[32,64]{1,0:T(8,128)(2,1)S(1)} %copy-done.3), channel_id=1, source_target_pairs={{0,4},{1,5},{2,6},{3,7},{4,8},{5,9},{6,10},{7,11},{8,12},{9,13},{1... | collective-permute-start | bytes 12296 | tf_op jit(solution)/shard_map/ppermute | solution.py:259
  28.1 4.9 %collective-permute-start.9 = (bf16[64,128]{1,0:T(8,128)(2,1)S(1)}, bf16[64,128]{1,0:T(8,128)(2,1)S(1)}, u32[]{:S(2)}, u32[]{:S(2)}) collective-permute-start(bf16[64,128]{1,0:T(8,128)(2,1)S(1)} %copy-done.10), channel_id=1, source_target_pairs={{0,1},{1,2},{2,3},{4,5},{5,6},{6,7},{8,9},{9,10},{10,11},{12,13},{... | collective-permute-start | bytes 49160 | tf_op jit(solution)/shard_map/ppermute | solution.py:259
  33.1 5.5 %collective-permute-start.10 = (bf16[64,128]{1,0:T(8,128)(2,1)S(1)}, bf16[64,128]{1,0:T(8,128)(2,1)S(1)}, u32[]{:S(2)}, u32[]{:S(2)}) collective-permute-start(bf16[64,128]{1,0:T(8,128)(2,1)S(1)} %copy-done.10), channel_id=1, source_target_pairs={{1,0},{2,1},{3,2},{5,4},{6,5},{7,6},{9,8},{10,9},{11,10},{13,12},{... | collective-permute-start | bytes 49160 | tf_op jit(solution)/shard_map/ppermute | solution.py:259
  38.6 1.9 collective-permute-start.14
  40.6 2.4 %collective-permute-start.13 = (bf16[48,64,8]{1,2,0:T(8,128)(2,1)S(1)}, bf16[48,64,8]{1,2,0:T(8,128)(2,1)S(1)}, u32[]{:S(2)}, u32[]{:S(2)}) collective-permute-start(bf16[48,64,8]{1,2,0:T(8,128)(2,1)S(1)} %copy.18), channel_id=1, source_target_pairs={{1,0},{2,1},{3,2},{5,4},{6,5},{7,6},{9,8},{10,9},{11,10},{13,12},{... | collective-permute-start | bytes 147464 | tf_op jit(solution)/shard_map/ppermute | solution.py:259
  43.8 0.9 reshape.25.taps
  47.3 31.1 %forward.1 = (bf16[4096,256]{1,0:T(8,128)(2,1)}, bf16[3584,256]{1,0:T(8,128)(2,1)}, f32[2048,128]{1,0:T(8,128)}, f32[3584,256]{1,0:T(8,128)}) custom-call(s32[2]{0:T(128)} %pad_add_fusion.place, s32[2]{0:T(128)} %dil.3, bf16[32,64]{1,0:T(8,128)(2,1)} %copy-done.9, bf16[32,64]{1,0:T(8,128)(2,1)} %own.3, bf16[32,64]{1,0:T(8,128)(2,1)} %copy-done.16, ...), custom_call_target="tpu_custom_call" | custom-call | tf_op jit(solution)/shard_map/forward/pallas_call | solution.py:281
  79.2 1.8 pad_maximum_fusion.cot
  81.0 59.9 %backward.1 = (bf16[32,64,128]{2,1,0:T(8,128)(2,1)}, f32[1024,128]{1,0:T(8,128)}, f32[32,64]{1,0:T(8,128)}, f32[5,32,64]{2,1,0:T(8,128)}) custom-call(s32[2]{0:T(128)} %pad_add_fusion.place, s32[2]{0:T(128)} %dil.3, bf16[4096,256]{1,0:T(8,128)(2,1)} %get-tuple-element.18.s0, bf16[3584,256]{1,0:T(8,128)(2,1)} %get-tuple-element.19.s1, ...), custom_call_target="tpu_custom_call" | custom-call | tf_op jit(solution)/shard_map/backward/pallas_call | solution.py:299
  141.0 54.4 %all_to_all.10 = f32[256,4,128]{2,1,0:T(4,128)S(1)} all-to-all(f32[256,4,128]{2,1,0:T(4,128)} %bitcast.19), channel_id=1, replica_groups=mesh['bins'=64,'band'=4] {'bins','band'}, dimensions={0} | all-to-all | bytes 1048576 | tf_op jit(solution)/shard_map/all_to_all | solution.py:321
  196.5 5.3 %all-to-all-start.1 = ((f32[256,4,128]{2,1,0:T(4,128)}), f32[256,4,128]{2,1,0:T(4,128)S(1)}, u32[]{:S(2)}, u32[]{:S(2)}) async-start(f32[256,4,128]{2,1,0:T(4,128)} %broadcast_in_dim.10), calls=%async_computation.1 | async-start | bytes 1048576 | tf_op jit(solution)/shard_map/all_to_all | solution.py:330
  201.8 8.3 %collective-permute-start.15 = (f32[32,64]{1,0:T(8,128)S(1)}, f32[32,64]{1,0:T(8,128)S(1)}, u32[]{:S(2)}, u32[]{:S(2)}) collective-permute-start(f32[32,64]{1,0:T(8,128)S(1)} %get-tuple-element.34), channel_id=1, source_target_pairs={{0,0},{1,17},{2,34},{3,51},{4,4},{5,21},{6,38},{7,55},{8,8},{9,25}... | collective-permute-start | bytes 24584 | tf_op jit(solution)/shard_map/ppermute | solution.py:263
  210.0 4.6 %collective-permute-start.19 = (f32[32,64]{1,0:T(8,128)S(1)}, f32[32,64]{1,0:T(8,128)S(1)}, u32[]{:S(2)}, u32[]{:S(2)}) collective-permute-start(f32[32,64]{1,0:T(8,128)S(1)} %get-tuple-element.35), channel_id=1, source_target_pairs={{0,16},{1,33},{2,50},{3,67},{4,20},{5,37},{6,54},{7,71},{8,24},{9,... | collective-permute-start | bytes 24584 | tf_op jit(solution)/shard_map/ppermute | solution.py:263
  214.7 2.9 %collective-permute-start.18 = (f32[32,64]{1,0:T(8,128)S(1)}, f32[32,64]{1,0:T(8,128)S(1)}, u32[]{:S(2)}, u32[]{:S(2)}) collective-permute-start(f32[32,64]{1,0:T(8,128)S(1)} %get-tuple-element.36), channel_id=1, source_target_pairs={{0,12},{1,29},{2,46},{3,63},{4,16},{5,33},{6,50},{7,67},{8,20},{9,... | collective-permute-start | bytes 24584 | tf_op jit(solution)/shard_map/ppermute | solution.py:263
  217.5 4.1 %collective-permute-start.17 = (f32[32,64]{1,0:T(8,128)S(1)}, f32[32,64]{1,0:T(8,128)S(1)}, u32[]{:S(2)}, u32[]{:S(2)}) collective-permute-start(f32[32,64]{1,0:T(8,128)S(1)} %get-tuple-element.37), channel_id=1, source_target_pairs={{0,8},{1,25},{2,42},{3,59},{4,12},{5,29},{6,46},{7,63},{8,16},{9,3... | collective-permute-start | bytes 24584 | tf_op jit(solution)/shard_map/ppermute | solution.py:263
  221.6 6.5 %collective-permute-start.16 = (f32[32,64]{1,0:T(8,128)S(1)}, f32[32,64]{1,0:T(8,128)S(1)}, u32[]{:S(2)}, u32[]{:S(2)}) collective-permute-start(f32[32,64]{1,0:T(8,128)S(1)} %get-tuple-element.38), channel_id=1, source_target_pairs={{0,4},{1,21},{2,38},{3,55},{4,8},{5,25},{6,42},{7,59},{8,12},{9,29... | collective-permute-start | bytes 24584 | tf_op jit(solution)/shard_map/ppermute | solution.py:263
  229.2 2.9 %collective-permute-start.21 = (f32[32,64]{1,0:T(8,128)S(1)}, f32[32,64]{1,0:T(8,128)S(1)}, u32[]{:S(2)}, u32[]{:S(2)}) collective-permute-start(f32[32,64]{1,0:T(8,128)S(1)} %add_add_fusion), channel_id=1, source_target_pairs={{0,2},{1,3},{2,0},{3,1},{4,6},{5,7},{6,4},{7,5},{8,10},{9,11},{10,... | collective-permute-start | bytes 24584 | tf_op jit(solution)/shard_map/ppermute | solution.py:328
  232.1 1.2 collective-permute-done.22
  234.7 2.0 unpack.1
  (76 shorter events, 8.6 us)
Async XLA Ops:
  1.6 9.6 %collective-permute-start.11 = (bf16[8,64,128]{2,1,0:T(8,128)(2,1)S(1)}, bf16[8,64,128]{2,1,0:T(8,128)(2,1)S(1)}, u32[]{:S(2)}, u32[]{:S(2)}) collective-permute-start(bf16[8,64,128]{2,1,0:T(8,128)(2,1)S(1)} %get-tuple-element.33), channel_id=1, source_target_pairs={{0,4},{1,5},{2,6},{3,7},{4,8},{5,9},{6,10},{7,11},{8,12},{9,13},{1... | collective-permute-start | bytes 393224 | tf_op jit(solution)/shard_map/ppermute | solution.py:259
  6.0 12.9 %collective-permute-start.8 = (bf16[32,64]{1,0:T(8,128)(2,1)}, bf16[32,64]{1,0:T(8,128)(2,1)S(1)}, u32[]{:S(2)}, u32[]{:S(2)}) collective-permute-start(bf16[32,64]{1,0:T(8,128)(2,1)} %own.3), channel_id=1, source_target_pairs={{20,0},{37,1},{54,2},{71,3},{24,4},{41,5},{58,6},{75,7},{28,8},{45... | collective-permute-start | bytes 12296 | tf_op jit(solution)/shard_map/ppermute | solution.py:259
  7.3 13.0 %collective-permute-start.7 = (bf16[32,64]{1,0:T(8,128)(2,1)}, bf16[32,64]{1,0:T(8,128)(2,1)S(1)}, u32[]{:S(2)}, u32[]{:S(2)}) collective-permute-start(bf16[32,64]{1,0:T(8,128)(2,1)} %own.3), channel_id=1, source_target_pairs={{16,0},{33,1},{50,2},{67,3},{20,4},{37,5},{54,6},{71,7},{24,8},{41... | collective-permute-start | bytes 12296 | tf_op jit(solution)/shard_map/ppermute | solution.py:259
  8.6 13.0 %collective-permute-start.6 = (bf16[32,64]{1,0:T(8,128)(2,1)}, bf16[32,64]{1,0:T(8,128)(2,1)S(1)}, u32[]{:S(2)}, u32[]{:S(2)}) collective-permute-start(bf16[32,64]{1,0:T(8,128)(2,1)} %own.3), channel_id=1, source_target_pairs={{12,0},{29,1},{46,2},{63,3},{16,4},{33,5},{50,6},{67,7},{20,8},{37... | collective-permute-start | bytes 12296 | tf_op jit(solution)/shard_map/ppermute | solution.py:259
  9.9 13.9 %collective-permute-start.5 = (bf16[32,64]{1,0:T(8,128)(2,1)}, bf16[32,64]{1,0:T(8,128)(2,1)S(1)}, u32[]{:S(2)}, u32[]{:S(2)}) collective-permute-start(bf16[32,64]{1,0:T(8,128)(2,1)} %own.3), channel_id=1, source_target_pairs={{8,0},{25,1},{42,2},{59,3},{12,4},{29,5},{46,6},{63,7},{16,8},{33,... | collective-permute-start | bytes 12296 | tf_op jit(solution)/shard_map/ppermute | solution.py:259
  11.2 6.4 %collective-permute-start.12 = (bf16[8,64,128]{2,1,0:T(8,128)(2,1)S(1)}, bf16[8,64,128]{2,1,0:T(8,128)(2,1)S(1)}, u32[]{:S(2)}, u32[]{:S(2)}) collective-permute-start(bf16[8,64,128]{2,1,0:T(8,128)(2,1)S(1)} %get-tuple-element.32), channel_id=1, source_target_pairs={{4,0},{5,1},{6,2},{7,3},{8,4},{9,5},{10,6},{11,7},{12,8},{13,9},{1... | collective-permute-start | bytes 393224 | tf_op jit(solution)/shard_map/ppermute | solution.py:259
  12.6 31.0 %copy-start.1 = (bf16[2,3,3,64,64]{4,3,2,1,0:T(8,128)(2,1)S(1)}, bf16[2,3,3,64,64]{4,3,2,1,0:T(8,128)(2,1)}, u32[]{:S(2)}) copy-start(bf16[2,3,3,64,64]{4,3,2,1,0:T(8,128)(2,1)} %param.11) | copy-start | bytes 442372
  17.6 10.5 %collective-permute-start.4 = (bf16[32,64]{1,0:T(8,128)(2,1)}, bf16[32,64]{1,0:T(8,128)(2,1)S(1)}, u32[]{:S(2)}, u32[]{:S(2)}) collective-permute-start(bf16[32,64]{1,0:T(8,128)(2,1)} %own.3), channel_id=1, source_target_pairs={{4,0},{21,1},{38,2},{55,3},{8,4},{25,5},{42,6},{59,7},{12,8},{29,9... | collective-permute-start | bytes 12296 | tf_op jit(solution)/shard_map/ppermute | solution.py:259
  19.0 26.1 %copy-start.14 = (bf16[32,64]{1,0:T(8,128)(2,1)}, bf16[32,64]{1,0:T(8,128)(2,1)S(1)}, u32[]{:S(2)}) copy-start(bf16[32,64]{1,0:T(8,128)(2,1)S(1)} %collective-permute-done.8.w6) | copy-start | bytes 12292
  19.0 14.1 %collective-permute-start.3 = (bf16[32,64]{1,0:T(8,128)(2,1)}, bf16[32,64]{1,0:T(8,128)(2,1)S(1)}, u32[]{:S(2)}, u32[]{:S(2)}) collective-permute-start(bf16[32,64]{1,0:T(8,128)(2,1)} %own.3), channel_id=1, source_target_pairs={{0,0},{17,1},{34,2},{51,3},{4,4},{21,5},{38,6},{55,7},{8,8},{25,9}... | collective-permute-start | bytes 12296 | tf_op jit(solution)/shard_map/ppermute | solution.py:259
  20.3 24.8 %copy-start.4 = (bf16[32,64]{1,0:T(8,128)(2,1)}, bf16[32,64]{1,0:T(8,128)(2,1)S(1)}, u32[]{:S(2)}) copy-start(bf16[32,64]{1,0:T(8,128)(2,1)S(1)} %collective-permute-done.7.w5) | copy-start | bytes 12292
  20.3 18.3 %collective-permute-start.2 = (bf16[32,64]{1,0:T(8,128)(2,1)}, bf16[32,64]{1,0:T(8,128)(2,1)S(1)}, u32[]{:S(2)}, u32[]{:S(2)}) collective-permute-start(bf16[32,64]{1,0:T(8,128)(2,1)} %own.3), channel_id=1, source_target_pairs={{13,1},{30,2},{47,3},{0,4},{17,5},{34,6},{51,7},{4,8},{21,9},{38,1... | collective-permute-start | bytes 12296 | tf_op jit(solution)/shard_map/ppermute | solution.py:259
  21.6 23.5 %copy-start.5 = (bf16[32,64]{1,0:T(8,128)(2,1)}, bf16[32,64]{1,0:T(8,128)(2,1)S(1)}, u32[]{:S(2)}) copy-start(bf16[32,64]{1,0:T(8,128)(2,1)S(1)} %collective-permute-done.6.w4) | copy-start | bytes 12292
  21.6 18.9 %collective-permute-start.1 = (bf16[32,64]{1,0:T(8,128)(2,1)}, bf16[32,64]{1,0:T(8,128)(2,1)S(1)}, u32[]{:S(2)}, u32[]{:S(2)}) collective-permute-start(bf16[32,64]{1,0:T(8,128)(2,1)} %own.3), channel_id=1, source_target_pairs={{4,0},{5,1},{6,2},{7,3},{8,4},{9,5},{10,6},{11,7},{12,8},{13,9},{1... | collective-permute-start | bytes 12296 | tf_op jit(solution)/shard_map/ppermute | solution.py:259
  23.9 22.3 %copy-start.6 = (bf16[32,64]{1,0:T(8,128)(2,1)}, bf16[32,64]{1,0:T(8,128)(2,1)S(1)}, u32[]{:S(2)}) copy-start(bf16[32,64]{1,0:T(8,128)(2,1)S(1)} %collective-permute-done.5.w3) | copy-start | bytes 12292
  23.9 22.2 %collective-permute-start = (bf16[32,64]{1,0:T(8,128)(2,1)S(1)}, bf16[32,64]{1,0:T(8,128)(2,1)S(1)}, u32[]{:S(2)}, u32[]{:S(2)}) collective-permute-start(bf16[32,64]{1,0:T(8,128)(2,1)S(1)} %copy-done.3), channel_id=1, source_target_pairs={{0,4},{1,5},{2,6},{3,7},{4,8},{5,9},{6,10},{7,11},{8,12},{9,13},{1... | collective-permute-start | bytes 12296 | tf_op jit(solution)/shard_map/ppermute | solution.py:259
  28.1 18.0 %copy-start.7 = (bf16[32,64]{1,0:T(8,128)(2,1)}, bf16[32,64]{1,0:T(8,128)(2,1)S(1)}, u32[]{:S(2)}) copy-start(bf16[32,64]{1,0:T(8,128)(2,1)S(1)} %collective-permute-done.4.w2) | copy-start | bytes 12292
  28.1 18.0 %collective-permute-start.9 = (bf16[64,128]{1,0:T(8,128)(2,1)S(1)}, bf16[64,128]{1,0:T(8,128)(2,1)S(1)}, u32[]{:S(2)}, u32[]{:S(2)}) collective-permute-start(bf16[64,128]{1,0:T(8,128)(2,1)S(1)} %copy-done.10), channel_id=1, source_target_pairs={{0,1},{1,2},{2,3},{4,5},{5,6},{6,7},{8,9},{9,10},{10,11},{12,13},{... | collective-permute-start | bytes 49160 | tf_op jit(solution)/shard_map/ppermute | solution.py:259
  33.1 13.0 %collective-permute-start.10 = (bf16[64,128]{1,0:T(8,128)(2,1)S(1)}, bf16[64,128]{1,0:T(8,128)(2,1)S(1)}, u32[]{:S(2)}, u32[]{:S(2)}) collective-permute-start(bf16[64,128]{1,0:T(8,128)(2,1)S(1)} %copy-done.10), channel_id=1, source_target_pairs={{1,0},{2,1},{3,2},{5,4},{6,5},{7,6},{9,8},{10,9},{11,10},{13,12},{... | collective-permute-start | bytes 49160 | tf_op jit(solution)/shard_map/ppermute | solution.py:259
  38.6 40.2 %collective-permute-start.14 = (bf16[48,64,8]{1,2,0:T(8,128)(2,1)S(1)}, bf16[48,64,8]{1,2,0:T(8,128)(2,1)S(1)}, u32[]{:S(2)}, u32[]{:S(2)}) collective-permute-start(bf16[48,64,8]{1,2,0:T(8,128)(2,1)S(1)} %copy.19), channel_id=1, source_target_pairs={{0,1},{1,2},{2,3},{4,5},{5,6},{6,7},{8,9},{9,10},{10,11},{12,13},{... | collective-permute-start | bytes 147464 | tf_op jit(solution)/shard_map/ppermute | solution.py:259
  40.6 37.9 %collective-permute-start.13 = (bf16[48,64,8]{1,2,0:T(8,128)(2,1)S(1)}, bf16[48,64,8]{1,2,0:T(8,128)(2,1)S(1)}, u32[]{:S(2)}, u32[]{:S(2)}) collective-permute-start(bf16[48,64,8]{1,2,0:T(8,128)(2,1)S(1)} %copy.18), channel_id=1, source_target_pairs={{1,0},{2,1},{3,2},{5,4},{6,5},{7,6},{9,8},{10,9},{11,10},{13,12},{... | collective-permute-start | bytes 147464 | tf_op jit(solution)/shard_map/ppermute | solution.py:259
  140.9 60.8 %copy-start.2 = (f32[5,32,64]{2,1,0:T(8,128)S(1)}, f32[5,32,64]{2,1,0:T(8,128)}, u32[]{:S(2)}) copy-start(f32[5,32,64]{2,1,0:T(8,128)} %get-tuple-element.24) | copy-start | bytes 122884
  140.9 88.1 %copy-start.11 = (f32[32,64]{1,0:T(8,128)S(1)}, f32[32,64]{1,0:T(8,128)}, u32[]{:S(2)}) copy-start(f32[32,64]{1,0:T(8,128)} %get-tuple-element.23) | copy-start | bytes 24580
  196.5 37.4 %all-to-all-start.1 = ((f32[256,4,128]{2,1,0:T(4,128)}), f32[256,4,128]{2,1,0:T(4,128)S(1)}, u32[]{:S(2)}, u32[]{:S(2)}) async-start(f32[256,4,128]{2,1,0:T(4,128)} %broadcast_in_dim.10), calls=%async_computation.1 | async-start | bytes 1048576 | tf_op jit(solution)/shard_map/all_to_all | solution.py:330
  201.8 26.4 %collective-permute-start.15 = (f32[32,64]{1,0:T(8,128)S(1)}, f32[32,64]{1,0:T(8,128)S(1)}, u32[]{:S(2)}, u32[]{:S(2)}) collective-permute-start(f32[32,64]{1,0:T(8,128)S(1)} %get-tuple-element.34), channel_id=1, source_target_pairs={{0,0},{1,17},{2,34},{3,51},{4,4},{5,21},{6,38},{7,55},{8,8},{9,25}... | collective-permute-start | bytes 24584 | tf_op jit(solution)/shard_map/ppermute | solution.py:263
  210.0 18.2 %collective-permute-start.19 = (f32[32,64]{1,0:T(8,128)S(1)}, f32[32,64]{1,0:T(8,128)S(1)}, u32[]{:S(2)}, u32[]{:S(2)}) collective-permute-start(f32[32,64]{1,0:T(8,128)S(1)} %get-tuple-element.35), channel_id=1, source_target_pairs={{0,16},{1,33},{2,50},{3,67},{4,20},{5,37},{6,54},{7,71},{8,24},{9,... | collective-permute-start | bytes 24584 | tf_op jit(solution)/shard_map/ppermute | solution.py:263
  214.7 13.5 %collective-permute-start.18 = (f32[32,64]{1,0:T(8,128)S(1)}, f32[32,64]{1,0:T(8,128)S(1)}, u32[]{:S(2)}, u32[]{:S(2)}) collective-permute-start(f32[32,64]{1,0:T(8,128)S(1)} %get-tuple-element.36), channel_id=1, source_target_pairs={{0,12},{1,29},{2,46},{3,63},{4,16},{5,33},{6,50},{7,67},{8,20},{9,... | collective-permute-start | bytes 24584 | tf_op jit(solution)/shard_map/ppermute | solution.py:263
  217.5 10.7 %collective-permute-start.17 = (f32[32,64]{1,0:T(8,128)S(1)}, f32[32,64]{1,0:T(8,128)S(1)}, u32[]{:S(2)}, u32[]{:S(2)}) collective-permute-start(f32[32,64]{1,0:T(8,128)S(1)} %get-tuple-element.37), channel_id=1, source_target_pairs={{0,8},{1,25},{2,42},{3,59},{4,12},{5,29},{6,46},{7,63},{8,16},{9,3... | collective-permute-start | bytes 24584 | tf_op jit(solution)/shard_map/ppermute | solution.py:263
  221.6 7.4 %collective-permute-start.16 = (f32[32,64]{1,0:T(8,128)S(1)}, f32[32,64]{1,0:T(8,128)S(1)}, u32[]{:S(2)}, u32[]{:S(2)}) collective-permute-start(f32[32,64]{1,0:T(8,128)S(1)} %get-tuple-element.38), channel_id=1, source_target_pairs={{0,4},{1,21},{2,38},{3,55},{4,8},{5,25},{6,42},{7,59},{8,12},{9,29... | collective-permute-start | bytes 24584 | tf_op jit(solution)/shard_map/ppermute | solution.py:263
  229.1 4.2 %collective-permute-start.22 = (f32[32,64]{1,0:T(8,128)S(1)}, f32[32,64]{1,0:T(8,128)S(1)}, u32[]{:S(2)}, u32[]{:S(2)}) collective-permute-start(f32[32,64]{1,0:T(8,128)S(1)} %add_add_fusion), channel_id=1, source_target_pairs={{0,3},{1,0},{2,1},{3,2},{4,7},{5,4},{6,5},{7,6},{8,11},{9,8},{10,9... | collective-permute-start | bytes 24584 | tf_op jit(solution)/shard_map/ppermute | solution.py:328
  229.2 4.2 %collective-permute-start.21 = (f32[32,64]{1,0:T(8,128)S(1)}, f32[32,64]{1,0:T(8,128)S(1)}, u32[]{:S(2)}, u32[]{:S(2)}) collective-permute-start(f32[32,64]{1,0:T(8,128)S(1)} %add_add_fusion), channel_id=1, source_target_pairs={{0,2},{1,3},{2,0},{3,1},{4,6},{5,7},{6,4},{7,5},{8,10},{9,11},{10,... | collective-permute-start | bytes 24584 | tf_op jit(solution)/shard_map/ppermute | solution.py:328
  232.0 1.3 collective-permute-start.20
  (9 other events, 55.7 us)

commit v2 on v0

v2 whole, which is shorter than its diff:
```python
import functools
import math

import jax
import jax.numpy as jnp
from jax import lax
from jax.experimental import pallas as pl
from jax.experimental.pallas import tpu as pltpu
from jax.sharding import PartitionSpec as P

LAYERS = 2
F32 = jnp.float32
BF16 = jnp.bfloat16
HALF = 128
WIDE = 256
RIM0 = 16
RIM1 = 12
RIM2 = 8
RIM3 = 4
CHUNK = 32
LIMIT = 56 * 1024 * 1024
VMEM = pl.BlockSpec(memory_space=pltpu.VMEM)
SMEM = pl.BlockSpec(memory_space=pltpu.SMEM)


def sigmoid(value):
    return 0.5 * jnp.tanh(0.5 * value) + 0.5


def lanes_of(width):
    return lax.broadcasted_iota(jnp.int32, (1, width), 1)


def up(value, amount):
    first = lanes_of(HALF) < amount
    a = pltpu.roll(value[:, :HALF], amount, 1)
    b = pltpu.roll(value[:, HALF:], amount, 1)
    return jnp.concatenate([jnp.where(first, b, a), jnp.where(first, a, b)], 1)


def down(value, amount):
    first = lanes_of(HALF) < HALF - amount
    a = pltpu.roll(value[:, :HALF], HALF - amount, 1)
    b = pltpu.roll(value[:, HALF:], HALF - amount, 1)
    return jnp.concatenate([jnp.where(first, a, b), jnp.where(first, b, a)], 1)


def sweep(count, held, body):
    def step(at, carry):
        for k in range(held):
            body(at * held + k)
        return carry

    lax.fori_loop(0, count // held, step, 0)


def middle_kernel(
    rows, c, total_bins, total_band,
    place, dil, feats, cot_up, cot, cot_down, from_lo, from_hi, emb, lw, rw, taps, back_taps,
    pair_map, payload,
    proj, embed, s0, s1, slope_s, slope0, wide_cot, pairs, g1, g0, sums, edge,
):
    bins = total_bins // rows
    group = emb.shape[1]
    span = group // rows
    first_bin = place[0] * rows
    first_offset = place[1] * group
    rate0, rate1 = dil[0], dil[1]
    edges = from_lo.shape[0] - c

    def rows_at(row, count=1):
        return pl.ds(pl.multiple_of(row * c, c), count * c)

    def mask_of(bin_id):
        lane = lanes_of(WIDE)
        offset = first_offset + jnp.where(lane < 192, lane, lane - WIDE)
        top = jnp.minimum(total_band, total_bins - bin_id)
        top = jnp.where(bin_id >= 0, top, 0)
        return jnp.where((offset >= 0) & (offset < top), 1.0, 0.0).astype(F32)

    def block(index):
        inside = (index >= 0) & (index < bins)
        half = feats[jnp.clip(index, 0, bins - 1)].astype(F32) * jnp.where(inside, 1.0, 0.0)
        return jnp.concatenate([half[:, :c], half[:, c:]], 0)

    base = place[0] + place[1] * span
    near = [block(place[0] + k) for k in (-1, 0, 1)]
    window = [block(base + k) for k in range(-1, span + 2)]
    filler = jnp.zeros((WIDE - (span + 3) * rows, c), F32)
    fw = jnp.concatenate(window + [filler], 0).astype(BF16)
    right = jnp.dot(fw, rw[...], preferred_element_type=F32).astype(BF16).astype(F32)
    filler = jnp.zeros((WIDE - 3 * rows, c), F32)
    fl = jnp.concatenate(near + [filler], 0).astype(BF16)
    left = jnp.dot(fl, lw[...], preferred_element_type=F32).astype(BF16).astype(F32)
    proj[...] = jnp.concatenate([right, left], 1).T
    beside = jnp.where(
        lanes_of(HALF) < HALF // 2, from_hi[edges:, :].astype(F32), from_lo[edges:, :].astype(F32)
    )
    embed[...] = jnp.concatenate([emb[...].astype(F32), beside], 1)
    wide_cot[0:RIM2] = cot_up[...]
    wide_cot[RIM2 : RIM2 + rows] = cot[...]
    wide_cot[RIM2 + rows :] = cot_down[...]

    def state_row(row):
        lag = down(proj[0:c, :], RIM0 + row)
        mine = pltpu.roll(proj[c : 2 * c, 0:HALF], HALF - RIM0 - row, 1)[:, 0:1]
        summed = mine + lag + embed[...]
        sig = sigmoid(summed)
        mask = mask_of(first_bin - RIM0 + row)
        s0[rows_at(row), :] = (summed * sig * mask).astype(BF16)
        slope = sig * (1.0 + summed * (1.0 - sig)) * mask
        slope_s[rows_at(row), :] = slope[:, 0:HALF]

    sweep(rows + 2 * RIM0, 16, state_row)

    def convolved(weights, source, base_row, rate):
        view = jnp.concatenate([source[rows_at(base_row + rate * k), :] for k in (-1, 0, 1)], 0)
        parts = jnp.dot(weights, view, preferred_element_type=F32)
        return parts[0:c], parts[c : 2 * c], parts[2 * c : 3 * c]

    def layer_row0(row):
        a, b, d = convolved(taps[0], s0, row + RIM0 - RIM1, rate0)
        pre = up(a, rate0) + b + down(d, rate0)
        sig = sigmoid(pre)
        mask = mask_of(first_bin - RIM1 + row)
        s1[rows_at(row), :] = (pre * sig * mask).astype(BF16)
        slope0[rows_at(row), :] = sig * (1.0 + pre * (1.0 - sig)) * mask

    sweep(rows + 2 * RIM1, 28, layer_row0)

    def layer_row1(row):
        a, b, d = convolved(taps[1], s1, row + RIM1 - RIM2, rate1)
        pre = up(a, rate1) + b + down(d, rate1)
        sig = sigmoid(pre)
        mask = mask_of(first_bin - RIM2 + row)
        slope = sig * (1.0 + pre * (1.0 - sig)) * mask
        pairs[row] = (pre * sig * mask)[:, 0:HALF].astype(BF16)
        tile = rows_at(row // 16)
        turn = (row % 16) * RIM2
        hi = pltpu.roll(from_hi[tile, :].astype(F32), (HALF - turn) % HALF, 1)
        lo = pltpu.roll(from_lo[tile, :].astype(F32), HALF - RIM2 - turn, 1)
        rim = jnp.where(lanes_of(HALF) < HALF // 2, hi, lo)
        grad = jnp.concatenate([wide_cot[row].astype(F32), rim], 1)
        g1[rows_at(row), :] = (grad * slope).astype(BF16)

    sweep(rows + 2 * RIM2, 16, layer_row1)
    pair_map[...] = pairs[RIM2 : RIM2 + rows]

    def back_row(row):
        a, b, d = convolved(back_taps[1], g1, row + RIM2 - RIM3, -rate1)
        back = down(a, rate1) + b + up(d, rate1)
        slope = slope0[rows_at(row + RIM1 - RIM3), :]
        g0[rows_at(row), :] = (back * slope).astype(BF16)

    sweep(rows + 2 * RIM3, 40, back_row)

    def tap_sums(rate, state, rim_s, grads, rim_g):
        lane = lanes_of(HALF)

        def views(row):
            view = [state[rows_at(row + rim_s + rate * k), :] for k in (-1, 0, 1)]
            grad = grads[rows_at(row + rim_g), 0:HALF].astype(F32)
            low = pltpu.roll(grad, HALF - rate, 1)
            high = pltpu.roll(grad, rate, 1)
            low0 = jnp.where(lane < HALF - rate, low, 0.0)
            high1 = jnp.where(lane < rate, high, 0.0)
            first = jnp.concatenate([low0, grad, high - high1], 0)
            second = jnp.concatenate([low - low0, jnp.zeros_like(grad), high1], 0)
            return jnp.concatenate(view, 0), jnp.concatenate([first, second], 1).astype(BF16)

        def step(at, total):
            both = [views(at * CHUNK + k) for k in range(CHUNK)]
            view = jnp.concatenate([v for v, _ in both], 1)
            grad = jnp.concatenate([g for _, g in both], 1)
            return total + lax.dot_general(
                view, grad, (((1,), (1,)), ((), ())), preferred_element_type=F32
            )

        return lax.fori_loop(0, rows // CHUNK, step, jnp.zeros((3 * c, 3 * c), F32))

    def place_rows(start, value):
        count = value.shape[0] // 4
        payload[start // 4 : start // 4 + count, 4:8, :] = value.reshape(count, 4, HALF).astype(
            BF16
        )

    total1 = tap_sums(rate1, s1, RIM1, g1, RIM2)
    place_rows(3 * c, total1[:, 0:HALF])
    edge[...] = total1[:, HALF : 3 * c]
    total0 = tap_sums(rate0, s0, RIM0, g0, RIM3)
    place_rows(0, total0[:, 0:HALF])
    place_rows(6 * c, jnp.concatenate([total0[:, HALF : 3 * c], edge[...]], 1))

    sums[...] = jnp.zeros_like(sums)
    lane = lanes_of(HALF)

    def last_row(row):
        a, b, d = convolved(back_taps[0], g0, row + RIM3, -rate0)
        back = (down(a, rate0) + b + up(d, rate0))[:, 0:HALF]
        grad = back * slope_s[rows_at(row + RIM0), :]
        total = jnp.sum(grad, axis=1, keepdims=True)
        sums[:, 0:HALF] += jnp.where(lane == row, total, 0.0)
        turned = pltpu.roll(grad, row, 1)
        wrapped = jnp.where(lane < row, turned, 0.0)
        sums[:, HALF : 2 * HALF] += turned - wrapped
        sums[:, 2 * HALF : 3 * HALF] += wrapped
        sums[:, 3 * HALF : 4 * HALF] += grad

    sweep(rows, 16, last_row)

    highest = lax.Precision.HIGHEST
    both = sums[:, 0 : 3 * HALF]
    both = jnp.concatenate([both, jnp.zeros_like(both)], 0).T
    left_grad = both[0:rows, 0:c]
    right_grad = both[HALF : HALF + rows + group, 0:c]
    fwin = jnp.concatenate([near[1]] + window[1 : span + 2], 0)
    fwin = jnp.concatenate([fwin, jnp.zeros((WIDE - fwin.shape[0], c), F32)], 0)
    fwin = jnp.concatenate([fwin, jnp.zeros_like(fwin)], 1).T[0:c]
    grad_left = jnp.dot(fwin[:, 0:rows], left_grad, precision=highest, preferred_element_type=F32)
    grad_right = jnp.dot(
        fwin[:, rows : 2 * rows + group], right_grad, precision=highest, preferred_element_type=F32
    )
    place_rows(9 * c, jnp.concatenate([grad_left, grad_right], 1))
    spare = payload.shape[0] - 10 * c // 4
    payload[10 * c // 4 :, 4:8, :] = jnp.zeros((spare, 4, HALF), BF16)
    at = pl.ds((10 * c + place[1] * c) // 4, c // 4)
    payload[at, 4:8, :] = sums[:, 3 * HALF : 4 * HALF].reshape(c // 4, 4, HALF).astype(BF16)

    transposed = (((1,), (1,)), ((), ()))
    feature_left = lax.dot_general(
        left_grad, lw[...].astype(F32), transposed, precision=highest, preferred_element_type=F32
    )
    feature_right = lax.dot_general(
        right_grad, rw[...].astype(F32), transposed, precision=highest, preferred_element_type=F32
    )
    payload[:, 0:4, :] = jnp.zeros((payload.shape[0], 4, HALF), BF16)

    def packed(value):
        return jnp.concatenate([value[0 : rows // 2], value[rows // 2 :]], 1).reshape(4, 4, HALF)

    mine = pl.ds(place[0] * 4, 4)
    payload[mine, 0:4, :] = packed(feature_left).astype(BF16)
    for k in range(span + 1):
        part = packed(feature_right[k * rows : (k + 1) * rows])

        @pl.when(base + k < bins)
        def _():
            target = pl.ds((base + k) * 4, 4)
            old = payload[target, 0:4, :].astype(F32)
            payload[target, 0:4, :] = (old + part).astype(BF16)


def middle(rows, c, group, total_bins, total_band, devices, args):
    tall = lambda rim: (rows + 2 * rim) * c
    return pl.pallas_call(
        functools.partial(middle_kernel, rows, c, total_bins, total_band),
        out_shape=(
            jax.ShapeDtypeStruct((rows, c, group), BF16),
            jax.ShapeDtypeStruct((devices, 8, HALF), BF16),
        ),
        in_specs=[SMEM] * 2 + [VMEM] * (len(args) - 2),
        out_specs=(VMEM,) * 2,
        scratch_shapes=[
            pltpu.VMEM((2 * c, WIDE), F32),
            pltpu.VMEM((c, WIDE), F32),
            pltpu.VMEM((tall(RIM0), WIDE), BF16),
            pltpu.VMEM((tall(RIM1), WIDE), BF16),
            pltpu.VMEM((tall(RIM0), HALF), F32),
            pltpu.VMEM((tall(RIM1), WIDE), F32),
            pltpu.VMEM((rows + 2 * RIM2, c, HALF), BF16),
            pltpu.VMEM((rows + 2 * RIM2, c, HALF), BF16),
            pltpu.VMEM((tall(RIM2), WIDE), BF16),
            pltpu.VMEM((tall(RIM3), WIDE), BF16),
            pltpu.VMEM((c, 4 * HALF), F32),
            pltpu.VMEM((3 * c, 3 * c - HALF), F32),
        ],
        compiler_params=pltpu.CompilerParams(vmem_limit_bytes=LIMIT),
        name="middle",
    )(*args)


def edge_kernel(rows, c, cot_up, cot, cot_down, emb, to_lo, to_hi):
    lane = lanes_of(HALF)
    count = rows + 2 * RIM2
    for tile in range(count // 16):
        low = jnp.zeros((c, HALF), F32)
        high = jnp.zeros((c, HALF), F32)
        for k in range(16):
            row = tile * 16 + k
            if row < RIM2:
                value = cot_up[row]
            elif row < RIM2 + rows:
                value = cot[row - RIM2]
            else:
                value = cot_down[row - RIM2 - rows]
            value = value.astype(F32)
            here = (lane >= RIM2 * k) & (lane < RIM2 * (k + 1))
            low = jnp.where(here, pltpu.roll(value, RIM2 * k, 1), low)
            high = jnp.where(here, pltpu.roll(value, RIM2 * (k + 1) % HALF, 1), high)
        to_lo[tile * c : (tile + 1) * c, :] = low.astype(BF16)
        to_hi[tile * c : (tile + 1) * c, :] = high.astype(BF16)
    to_lo[count // 16 * c :, :] = emb[...]
    to_hi[count // 16 * c :, :] = emb[...]


def share_kernel(parts, share, features):
    total = jnp.sum(parts[...].astype(F32), axis=0)
    features[...] = total[0:4]
    share[...] = jnp.broadcast_to(total[4:8].astype(BF16)[None], share.shape)


def unpack_kernel(c, whole_scale, offset_scale, place, total, left, right, offset, kernels):
    def piece(start):
        value = total[start // 4 : (start + c) // 4].astype(F32)
        return value.reshape(c, HALF)

    for p in range(3):
        rest = piece((6 + p) * c) * whole_scale
        for layer in range(2):
            main = piece((3 * layer + p) * c) * whole_scale
            kernels[layer, p, 0] = main[:, 0:c]
            kernels[layer, p, 1] = main[:, c : 2 * c]
            kernels[layer, p, 2] = rest[:, layer * c : (layer + 1) * c]
    both = piece(9 * c) * whole_scale
    left[...] = both[:, 0:c]
    right[...] = both[:, c : 2 * c]
    at = pl.ds((10 * c + place[1] * c) // 4, c // 4)
    offset[...] = total[at].astype(F32).reshape(c, HALF) * offset_scale


def per_device(features, left_weight, right_weight, offset_embed, kernels, dilation, cotangent):
    rows, c = features.shape
    group = offset_embed.shape[1]
    bins, band = lax.axis_size("bins"), lax.axis_size("band")
    devices = bins * band
    total_bins, total_band = rows * bins, group * band
    every = ("bins", "band")
    place = jnp.stack([lax.axis_index("bins"), lax.axis_index("band")]).astype(jnp.int32)

    def beside(block, axis, step):
        count = lax.axis_size(axis)
        route = [(i + step, i) for i in range(count) if 0 <= i + step < count]
        return lax.ppermute(block, axis, route)

    packed = jnp.concatenate([features[: rows // 2], features[rows // 2 :]], 1)
    feats = lax.all_to_all(
        jnp.broadcast_to(packed[None], (bins,) + packed.shape), "bins", 0, 0, tiled=True
    )
    cot_up = beside(cotangent[rows - RIM2 :], "bins", -1)
    cot_down = beside(cotangent[:RIM2], "bins", 1)
    edge_shape = jax.ShapeDtypeStruct(((rows + 2 * RIM2) // 16 * c + c, HALF), BF16)
    to_lo, to_hi = pl.pallas_call(
        functools.partial(edge_kernel, rows, c),
        out_shape=(edge_shape, edge_shape),
        in_specs=[VMEM] * 4,
        out_specs=(VMEM,) * 2,
        compiler_params=pltpu.CompilerParams(vmem_limit_bytes=LIMIT),
        name="edges",
    )(cot_up, cotangent, cot_down, offset_embed)
    from_lo = beside(to_hi, "band", -1)
    from_hi = beside(to_lo, "band", 1)

    taps = jnp.transpose(kernels, (0, 2, 4, 1, 3)).reshape(LAYERS, 3 * c, 3 * c)
    back_taps = jnp.transpose(kernels, (0, 2, 3, 1, 4)).reshape(LAYERS, 3 * c, 3 * c)

    pair_map, payload = middle(
        rows, c, group, total_bins, total_band, devices,
        (place, dilation, feats, cot_up, cotangent, cot_down, from_lo, from_hi, offset_embed,
         left_weight, right_weight, taps, back_taps),
    )
    parts = lax.all_to_all(payload, every, 0, 0, tiled=True)
    share, feature_part = pl.pallas_call(
        share_kernel,
        out_shape=(
            jax.ShapeDtypeStruct((devices, 4, HALF), BF16),
            jax.ShapeDtypeStruct((4, HALF), F32),
        ),
        in_specs=[VMEM],
        out_specs=(VMEM,) * 2,
        compiler_params=pltpu.CompilerParams(vmem_limit_bytes=LIMIT),
        name="shares",
    )(parts)
    total = lax.all_to_all(share, every, 0, 0, tiled=True)
    quarters = lax.all_gather(feature_part, "band")
    pairs = quarters.reshape(rows // 2, HALF)
    grad_features = jnp.concatenate([pairs[:, :c], pairs[:, c:]], 0) / math.sqrt(total_band)
    whole_scale = 1.0 / math.sqrt(total_bins * total_band)
    grad_left, grad_right, grad_offset, grad_kernels = pl.pallas_call(
        functools.partial(unpack_kernel, c, whole_scale, 1.0 / math.sqrt(total_bins)),
        out_shape=(
            jax.ShapeDtypeStruct((c, c), F32),
            jax.ShapeDtypeStruct((c, c), F32),
            jax.ShapeDtypeStruct((c, group), F32),
            jax.ShapeDtypeStruct((LAYERS, 3, 3, c, c), F32),
        ),
        in_specs=[SMEM, VMEM],
        out_specs=(VMEM,) * 4,
        compiler_params=pltpu.CompilerParams(vmem_limit_bytes=LIMIT),
        name="unpack",
    )(place, total)
    return pair_map, grad_features, grad_left, grad_right, grad_offset, grad_kernels


def solution(mesh):
    return jax.shard_map(
        per_device,
        mesh=mesh,
        in_specs=(P("bins", None), P(), P(), P(None, "band"), P(), P(), P("bins", None, "band")),
        out_specs=(P("bins", None, "band"), P("bins", None), P(), P(), P(None, "band"), P()),
        check_vma=False,
    )
```

time: 792 us -> 124 us (0.16); the launches traced: 782 us -> 124 us
  blocking collectives: 443 us -> 41.8 us
  starting transfers between devices: 155 us -> 31.3 us
  waiting for transfers between devices: 87.9 us -> 12 us
  Pallas kernels: 0 us -> 28.5 us
  matrix products: 26.4 us -> 0 us
  between operations: 25.1 us -> 0.76 us
  local copies, waits for them, and re-layouts: 32.2 us -> 7.95 us
  other arithmetic: 12.6 us -> 1.3 us
    psum x3 -> x0, blocking collectives: 443 us -> none  [the longest x1 298 us: per_device(): offset_sum = lax.psum(offset_part, 'bins')]
    ppermute x48 -> x4, starting transfers between devices: 155 us -> 11 us  [beside(): return lax.ppermute(block, axis, route)]
    ppermute x48 -> x4, waiting for transfers between devices: 87.9 us -> 4.77 us  [beside(): return lax.ppermute(block, axis, route)]
    all_to_all x0 -> x1, blocking collectives: none -> 34.6 us  [per_device(): parts = lax.all_to_all(payload, every, 0, 0, tiled=True)]
    pallas_call x0 -> x4, Pallas kernels: none -> 28.5 us  [the longest x1 22.3 us: middle(): pl.pallas_call(functools.partial(middle_kernel, rows, c, total_bins, tota...]
    dot_general x60 -> x0, matrix products: 26.4 us -> none  [the longest x18 9.42 us: per_device(): jnp.einsum('icd,ce->ied', view, kernels[layer, row_tap, col_tap], preferr...]
    all_to_all x0 -> x2, starting transfers between devices: none -> 20.4 us  [the longest x1 15.1 us: per_device(): lax.all_to_all(jnp.broadcast_to(packed[None], (bins,) + packed.shape), 'b...]
    slice x19 -> x3, local copies, waits for them, and re-layouts: 9.71 us -> 0.85 us  [the longest x1 0.76 us: per_device(): packed = jnp.concatenate([features[:rows // 2], features[rows // 2:]], 1)]
  transfers between devices with their start and end apart: 49 -> 6, of which waited for: 18 -> 3; matrix products, arithmetic and copies ran while one was open for 4% -> 3% of each run, Pallas kernels for 0% -> 2%
where the time goes in v2:
time: 124 us
  blocking collectives  41.8 us (34%)
  starting transfers between devices  31.3 us (25%)
  Pallas kernels  28.5 us (23%)
  waiting for transfers between devices  12 us (10%)
  local copies, waits for them, and re-layouts  7.95 us (6%)
  other arithmetic  1.3 us (1%)
    all_to_all x1, blocking collectives, per_device(): parts = lax.all_to_all(payload, every, 0, 0, tiled=True)  34.6 us
    pallas_call x1, Pallas kernels, middle(): pl.pallas_call(functools.partial(middle_kernel, rows, c, total_bins, tota...  22.3 us
    all_to_all x1, starting transfers between devices, per_device(): lax.all_to_all(jnp.broadcast_to(packed[None], (bins,) + packed.shape), 'b...  15.1 us
    ppermute x4, starting transfers between devices, beside(): return lax.ppermute(block, axis, route)  11 us
    all_gather x1, blocking collectives, per_device(): quarters = lax.all_gather(feature_part, 'band')  7.23 us
    all_to_all x1, waiting for transfers between devices, per_device(): total = lax.all_to_all(share, every, 0, 0, tiled=True)  7.2 us
    all_to_all x1, starting transfers between devices, per_device(): total = lax.all_to_all(share, every, 0, 0, tiled=True)  5.26 us
    ppermute x4, waiting for transfers between devices, beside(): return lax.ppermute(block, axis, route)  4.77 us
  transfers between devices with their start and end apart: 6, of which 3 were waited for; matrix products, arithmetic and copies ran while one was open for 3% of the time, Pallas kernels for 2%

profile of v2, /device:TPU:1, one launch (start us, length us, event | category | flops | bytes accessed | tf_op | source)
XLA Modules:
  0.0 123.7 jit_solution(16715342326837112776)
XLA Ops:
  0.6 0.8 fusion.2
  1.4 0.1 pad_maximum_fusion
  1.5 0.7 broadcast_in_dim.2
  2.2 15.1 %all-to-all-start = ((bf16[64,16,128]{2,1,0:T(8,128)(2,1)}), bf16[64,16,128]{2,1,0:T(8,128)(2,1)S(1)}, u32[]{:S(2)}, u32[]{:S(2)}) async-start(bf16[64,16,128]{2,1,0:T(8,128)(2,1)} %broadcast_in_dim.2), calls=%async_computation | async-start | bytes 524288 | tf_op jit(solution)/shard_map/all_to_all | solution.py:346
  17.4 1.4 %collective-permute-start.1 = (bf16[8,64,128]{2,1,0:T(8,128)(2,1)S(1)}, bf16[8,64,128]{2,1,0:T(8,128)(2,1)S(1)}, u32[]{:S(2)}, u32[]{:S(2)}) collective-permute-start(bf16[8,64,128]{2,1,0:T(8,128)(2,1)S(1)} %get-tuple-element.26), channel_id=1, source_target_pairs={{4,0},{8,4},{12,8},{16,12},{20,16},{24,20},{28,24},{32,28},{36,32}... | collective-permute-start | bytes 393224 | tf_op jit(solution)/shard_map/ppermute | solution.py:343
  18.8 4.0 %collective-permute-start = (bf16[8,64,128]{2,1,0:T(8,128)(2,1)S(1)}, bf16[8,64,128]{2,1,0:T(8,128)(2,1)S(1)}, u32[]{:S(2)}, u32[]{:S(2)}) collective-permute-start(bf16[8,64,128]{2,1,0:T(8,128)(2,1)S(1)} %get-tuple-element.27), channel_id=1, source_target_pairs={{0,4},{4,8},{8,12},{12,16},{16,20},{20,24},{24,28},{28,32},{32,36}... | collective-permute-start | bytes 393224 | tf_op jit(solution)/shard_map/ppermute | solution.py:343
  22.8 0.2 copy.17
  23.1 0.9 reshape.22.taps
  24.0 0.3 copy.18
  24.3 0.9 reshape.23.back_taps
  25.2 1.5 %collective-permute-done.1.cot_down = bf16[8,64,128]{2,1,0:T(8,128)(2,1)S(1)} collective-permute-done((bf16[8,64,128]{2,1,0:T(8,128)(2,1)S(1)}, bf16[8,64,128]{2,1,0:T(8,128)(2,1)S(1)}, u32[]{:S(2)}, u32[]{:S(2)}) %collective-permute-start.1) | collective-permute-done | bytes 131104 | tf_op jit(solution)/shard_map/ppermute | solution.py:343
  26.7 0.6 copy-done.4
  27.4 0.6 copy-done.5
  28.0 2.2 %edges.1 = (bf16[256,128]{1,0:T(8,128)(2,1)}, bf16[256,128]{1,0:T(8,128)(2,1)}) custom-call(bf16[8,64,128]{2,1,0:T(8,128)(2,1)} %copy-done.5, bf16[32,64,128]{2,1,0:T(8,128)(2,1)} %cot.3, bf16[8,64,128]{2,1,0:T(8,128)(2,1)} %copy-done.4, bf16[64,128]{1,0:T(8,128)(2,1)} %emb.3), custom_call_target="tpu_custom_call" | custom-call | tf_op jit(solution)/shard_map/edges/pallas_call | solution.py:352
  30.2 3.6 %collective-permute-start.2 = (bf16[256,128]{1,0:T(8,128)(2,1)}, bf16[256,128]{1,0:T(8,128)(2,1)S(1)}, u32[]{:S(2)}, u32[]{:S(2)}) collective-permute-start(bf16[256,128]{1,0:T(8,128)(2,1)} %get-tuple-element.16), channel_id=1, source_target_pairs={{0,1},{1,2},{2,3},{4,5},{5,6},{6,7},{8,9},{9,10},{10,11},{12,13},{... | collective-permute-start | bytes 196616 | tf_op jit(solution)/shard_map/ppermute | solution.py:343
  33.9 1.9 %collective-permute-start.3 = (bf16[256,128]{1,0:T(8,128)(2,1)}, bf16[256,128]{1,0:T(8,128)(2,1)S(1)}, u32[]{:S(2)}, u32[]{:S(2)}) collective-permute-start(bf16[256,128]{1,0:T(8,128)(2,1)} %get-tuple-element.17), channel_id=1, source_target_pairs={{1,0},{2,1},{3,2},{5,4},{6,5},{7,6},{9,8},{10,9},{11,10},{13,12},{... | collective-permute-start | bytes 196616 | tf_op jit(solution)/shard_map/ppermute | solution.py:343
  35.8 0.6 pad_add_fusion.place
  36.4 3.3 %collective-permute-done.3.from_hi = bf16[256,128]{1,0:T(8,128)(2,1)S(1)} collective-permute-done((bf16[256,128]{1,0:T(8,128)(2,1)}, bf16[256,128]{1,0:T(8,128)(2,1)S(1)}, u32[]{:S(2)}, u32[]{:S(2)}) %collective-permute-start.3) | collective-permute-done | bytes 65568 | tf_op jit(solution)/shard_map/ppermute | solution.py:343
  39.7 0.6 copy-done.7
  40.3 0.7 copy-done.3
  41.0 22.3 %middle.1 = (bf16[32,64,128]{2,1,0:T(8,128)(2,1)}, bf16[256,8,128]{2,1,0:T(8,128)(2,1)}) custom-call(s32[2]{0:T(128)} %pad_add_fusion.place, s32[2]{0:T(128)} %dil.1, bf16[64,16,128]{2,1,0:T(8,128)(2,1)} %copy-done.3, bf16[8,64,128]{2,1,0:T(8,128)(2,1)} %copy-done.5, bf16[32,64,128]{2,1,0:T(8,128)(2,1)} %cot.3, bf16[8,64,128]{2,1,0:T(8,128)(2,1)} %copy-done.4, ...), custom_call_target="tpu_custom_call" | custom-call | tf_op jit(solution)/shard_map/middle/pallas_call | solution.py:255
  63.3 34.6 %all_to_all.15.parts = bf16[256,8,128]{2,1,0:T(8,128)(2,1)} all-to-all(bf16[256,8,128]{2,1,0:T(8,128)(2,1)} %get-tuple-element.19), channel_id=1, replica_groups=mesh['bins'=64,'band'=4] {'bins','band'}, dimensions={0} | all-to-all | bytes 1048576 | tf_op jit(solution)/shard_map/all_to_all | solution.py:371
  97.9 2.1 %shares.1 = (bf16[256,4,128]{2,1,0:T(4,128)(2,1)}, f32[4,128]{1,0:T(4,128)}) custom-call(bf16[256,8,128]{2,1,0:T(8,128)(2,1)} %all_to_all.15.parts), custom_call_target="tpu_custom_call" | custom-call | tf_op jit(solution)/shard_map/shares/pallas_call | solution.py:372
  100.0 5.3 %all-to-all-start.2 = ((bf16[256,4,128]{2,1,0:T(4,128)(2,1)}), bf16[256,4,128]{2,1,0:T(4,128)(2,1)S(1)}, u32[]{:S(2)}, u32[]{:S(2)}) async-start(bf16[256,4,128]{2,1,0:T(4,128)(2,1)} %get-tuple-element.21), calls=%async_computation.2 | async-start | bytes 524288 | tf_op jit(solution)/shard_map/all_to_all | solution.py:383
  105.2 0.0 copy-start.8
  105.2 0.7 copy-done.8
  105.9 7.2 %all-gather.1 = f32[4,4,128]{2,1,0:T(4,128)S(1)} all-gather(f32[1,4,128]{2,1,0:T(4,128)S(1)} %bitcast.9), channel_id=2, replica_groups=mesh['bins'=64,'band'=4] {'band'}, dimensions={0}, use_global_device_ids=true | all-gather | bytes 10240 | tf_op jit(solution)/shard_map/all_gather | solution.py:384
  113.1 0.1 fusion.1
  113.2 0.6 maximum_multiply_fusion
  113.8 7.2 %all-to-all-done.2.total = bf16[256,4,128]{2,1,0:T(4,128)(2,1)S(1)} async-done(((bf16[256,4,128]{2,1,0:T(4,128)(2,1)}), bf16[256,4,128]{2,1,0:T(4,128)(2,1)S(1)}, u32[]{:S(2)}, u32[]{:S(2)}) %all-to-all-start.2) | async-done | bytes 262176 | tf_op jit(solution)/shard_map/all_to_all | solution.py:383
  121.0 0.7 copy-done.2
  121.7 1.9 %unpack.1 = (f32[64,64]{1,0:T(8,128)}, f32[64,64]{1,0:T(8,128)}, f32[64,128]{1,0:T(8,128)}, f32[2,3,3,64,64]{4,3,2,1,0:T(8,128)}) custom-call(s32[2]{0:T(128)} %pad_add_fusion.place, bf16[256,4,128]{2,1,0:T(4,128)(2,1)} %copy-done.2), custom_call_target="tpu_custom_call" | custom-call | tf_op jit(solution)/shard_map/unpack/pallas_call | solution.py:388
  (15 shorter events, 0.1 us)
Async XLA Ops:
  0.6 16.7 %copy-start = (bf16[32,64,128]{2,1,0:T(8,128)(2,1)S(1)}, bf16[32,64,128]{2,1,0:T(8,128)(2,1)}, u32[]{:S(2)}) copy-start(bf16[32,64,128]{2,1,0:T(8,128)(2,1)} %cot.3) | copy-start | bytes 1572868
  2.2 37.4 %all-to-all-start = ((bf16[64,16,128]{2,1,0:T(8,128)(2,1)}), bf16[64,16,128]{2,1,0:T(8,128)(2,1)S(1)}, u32[]{:S(2)}, u32[]{:S(2)}) async-start(bf16[64,16,128]{2,1,0:T(8,128)(2,1)} %broadcast_in_dim.2), calls=%async_computation | async-start | bytes 524288 | tf_op jit(solution)/shard_map/all_to_all | solution.py:346
  17.4 5.5 %copy-start.1 = (bf16[2,3,3,64,64]{4,3,2,1,0:T(8,128)(2,1)S(1)}, bf16[2,3,3,64,64]{4,3,2,1,0:T(8,128)(2,1)}, u32[]{:S(2)}) copy-start(bf16[2,3,3,64,64]{4,3,2,1,0:T(8,128)(2,1)} %param.11) | copy-start | bytes 442372
  17.4 9.3 %collective-permute-start.1 = (bf16[8,64,128]{2,1,0:T(8,128)(2,1)S(1)}, bf16[8,64,128]{2,1,0:T(8,128)(2,1)S(1)}, u32[]{:S(2)}, u32[]{:S(2)}) collective-permute-start(bf16[8,64,128]{2,1,0:T(8,128)(2,1)S(1)} %get-tuple-element.26), channel_id=1, source_target_pairs={{4,0},{8,4},{12,8},{16,12},{20,16},{24,20},{28,24},{32,28},{36,32}... | collective-permute-start | bytes 393224 | tf_op jit(solution)/shard_map/ppermute | solution.py:343
  18.8 7.9 %collective-permute-start = (bf16[8,64,128]{2,1,0:T(8,128)(2,1)S(1)}, bf16[8,64,128]{2,1,0:T(8,128)(2,1)S(1)}, u32[]{:S(2)}, u32[]{:S(2)}) collective-permute-start(bf16[8,64,128]{2,1,0:T(8,128)(2,1)S(1)} %get-tuple-element.27), channel_id=1, source_target_pairs={{0,4},{4,8},{8,12},{12,16},{16,20},{20,24},{24,28},{28,32},{32,36}... | collective-permute-start | bytes 393224 | tf_op jit(solution)/shard_map/ppermute | solution.py:343
  26.7 0.7 copy-start.4
  27.4 0.6 copy-start.5
  30.2 6.2 %collective-permute-start.2 = (bf16[256,128]{1,0:T(8,128)(2,1)}, bf16[256,128]{1,0:T(8,128)(2,1)S(1)}, u32[]{:S(2)}, u32[]{:S(2)}) collective-permute-start(bf16[256,128]{1,0:T(8,128)(2,1)} %get-tuple-element.16), channel_id=1, source_target_pairs={{0,1},{1,2},{2,3},{4,5},{5,6},{6,7},{8,9},{9,10},{10,11},{12,13},{... | collective-permute-start | bytes 196616 | tf_op jit(solution)/shard_map/ppermute | solution.py:343
  33.9 5.8 %collective-permute-start.3 = (bf16[256,128]{1,0:T(8,128)(2,1)}, bf16[256,128]{1,0:T(8,128)(2,1)S(1)}, u32[]{:S(2)}, u32[]{:S(2)}) collective-permute-start(bf16[256,128]{1,0:T(8,128)(2,1)} %get-tuple-element.17), channel_id=1, source_target_pairs={{1,0},{2,1},{3,2},{5,4},{6,5},{7,6},{9,8},{10,9},{11,10},{13,12},{... | collective-permute-start | bytes 196616 | tf_op jit(solution)/shard_map/ppermute | solution.py:343
  36.4 3.3 %copy-start.6 = (bf16[256,128]{1,0:T(8,128)(2,1)}, bf16[256,128]{1,0:T(8,128)(2,1)S(1)}, u32[]{:S(2)}) copy-start(bf16[256,128]{1,0:T(8,128)(2,1)S(1)} %collective-permute-done.2.from_lo) | copy-start | bytes 196612
  39.7 0.6 copy-start.7
  40.3 0.7 copy-start.3
  100.0 21.1 %all-to-all-start.2 = ((bf16[256,4,128]{2,1,0:T(4,128)(2,1)}), bf16[256,4,128]{2,1,0:T(4,128)(2,1)S(1)}, u32[]{:S(2)}, u32[]{:S(2)}) async-start(bf16[256,4,128]{2,1,0:T(4,128)(2,1)} %get-tuple-element.21), calls=%async_computation.2 | async-start | bytes 524288 | tf_op jit(solution)/shard_map/all_to_all | solution.py:383
  105.2 0.7 copy-start.8
  121.0 0.7 copy-start.2

commit v3 on v2

--- a/solution.py
+++ b/solution.py
@@ -18,7 +18,8 @@
 RIM2 = 8
 RIM3 = 4
 CHUNK = 32
-LIMIT = 56 * 1024 * 1024
+LIMIT = 28 * 1024 * 1024
+SMALL = 8 * 1024 * 1024
 VMEM = pl.BlockSpec(memory_space=pltpu.VMEM)
 SMEM = pl.BlockSpec(memory_space=pltpu.SMEM)
 
@@ -56,8 +57,8 @@
 
 def middle_kernel(
     rows, c, total_bins, total_band,
-    place, dil, feats, cot_up, cot, cot_down, from_lo, from_hi, emb, lw, rw, taps, back_taps,
-    pair_map, payload,
+    place, dil, near4, first4, last4, cot_up, cot, cot_down, from_lo, from_hi, emb, lw, rw,
+    taps, back_taps, pair_map, payload,
     proj, embed, s0, s1, slope_s, slope0, wide_cot, pairs, g1, g0, sums, edge,
 ):
     bins = total_bins // rows
@@ -78,14 +79,13 @@
         top = jnp.where(bin_id >= 0, top, 0)
         return jnp.where((offset >= 0) & (offset < top), 1.0, 0.0).astype(F32)
 
-    def block(index):
-        inside = (index >= 0) & (index < bins)
-        half = feats[jnp.clip(index, 0, bins - 1)].astype(F32) * jnp.where(inside, 1.0, 0.0)
+    def block(blocks, at):
+        half = blocks[at * rows // 2 : (at + 1) * rows // 2, :].astype(F32)
         return jnp.concatenate([half[:, :c], half[:, c:]], 0)
 
     base = place[0] + place[1] * span
-    near = [block(place[0] + k) for k in (-1, 0, 1)]
-    window = [block(base + k) for k in range(-1, span + 2)]
+    near = [block(near4, k) for k in range(3)]
+    window = [block(first4, k) for k in range(4)] + [block(last4, k) for k in range(1, 4)]
     filler = jnp.zeros((WIDE - (span + 3) * rows, c), F32)
     fw = jnp.concatenate(window + [filler], 0).astype(BF16)
     right = jnp.dot(fw, rw[...], preferred_element_type=F32).astype(BF16).astype(F32)
@@ -97,9 +97,9 @@
         lanes_of(HALF) < HALF // 2, from_hi[edges:, :].astype(F32), from_lo[edges:, :].astype(F32)
     )
     embed[...] = jnp.concatenate([emb[...].astype(F32), beside], 1)
-    wide_cot[0:RIM2] = cot_up[...]
+    wide_cot[0:RIM2] = cot_up[0 : RIM2 * c, :].reshape(RIM2, c, group)
     wide_cot[RIM2 : RIM2 + rows] = cot[...]
-    wide_cot[RIM2 + rows :] = cot_down[...]
+    wide_cot[RIM2 + rows :] = cot_down[0 : RIM2 * c, :].reshape(RIM2, c, group)
 
     def state_row(row):
         lag = down(proj[0:c, :], RIM0 + row)
@@ -279,7 +279,7 @@
     )(*args)
 
 
-def edge_kernel(rows, c, cot_up, cot, cot_down, emb, to_lo, to_hi):
+def edge_kernel(rows, c, cot_up, cot, cot_down, own, beyond, emb, to_lo, to_hi, blocks):
     lane = lanes_of(HALF)
     count = rows + 2 * RIM2
     for tile in range(count // 16):
@@ -288,11 +288,11 @@
         for k in range(16):
             row = tile * 16 + k
             if row < RIM2:
-                value = cot_up[row]
+                value = cot_up[row * c : (row + 1) * c, :]
             elif row < RIM2 + rows:
                 value = cot[row - RIM2]
             else:
-                value = cot_down[row - RIM2 - rows]
+                value = cot_down[(row - RIM2 - rows) * c : (row - RIM2 - rows + 1) * c, :]
             value = value.astype(F32)
             here = (lane >= RIM2 * k) & (lane < RIM2 * (k + 1))
             low = jnp.where(here, pltpu.roll(value, RIM2 * k, 1), low)
@@ -301,12 +301,21 @@
         to_hi[tile * c : (tile + 1) * c, :] = high.astype(BF16)
     to_lo[count // 16 * c :, :] = emb[...]
     to_hi[count // 16 * c :, :] = emb[...]
-
-
-def share_kernel(parts, share, features):
-    total = jnp.sum(parts[...].astype(F32), axis=0)
-    features[...] = total[0:4]
-    share[...] = jnp.broadcast_to(total[4:8].astype(BF16)[None], share.shape)
+    half = rows // 2
+    blocks[0:half, :] = cot_up[RIM2 * c :, :]
+    blocks[half : 2 * half, :] = own[...]
+    blocks[2 * half : 3 * half, :] = cot_down[RIM2 * c :, :]
+    blocks[3 * half :, :] = beyond[...]
+
+
+def greet_kernel(rows, c, features, first, last, to_up, to_down, own):
+    half = rows // 2
+    packed = jnp.concatenate([features[0:half, :], features[half:, :]], 1)
+    own[...] = packed
+    to_down[0 : RIM2 * c, :] = first[...].reshape(RIM2 * c, HALF)
+    to_down[RIM2 * c :, :] = packed
+    to_up[0 : RIM2 * c, :] = last[...].reshape(RIM2 * c, HALF)
+    to_up[RIM2 * c :, :] = packed
 
 
 def unpack_kernel(c, whole_scale, offset_scale, place, total, left, right, offset, kernels):
@@ -342,21 +351,50 @@
         route = [(i + step, i) for i in range(count) if 0 <= i + step < count]
         return lax.ppermute(block, axis, route)
 
-    packed = jnp.concatenate([features[: rows // 2], features[rows // 2 :]], 1)
-    feats = lax.all_to_all(
-        jnp.broadcast_to(packed[None], (bins,) + packed.shape), "bins", 0, 0, tiled=True
-    )
-    cot_up = beside(cotangent[rows - RIM2 :], "bins", -1)
-    cot_down = beside(cotangent[:RIM2], "bins", 1)
+    def joint(block, step):
+        route = []
+        for i in range(bins):
+            for b in range(band):
+                source = i + b * (group // rows) + step
+                if source < bins:
+                    route.append((source * band + b, i * band + b))
+        return lax.ppermute(block, every, route)
+
+    half = rows // 2
+    greeting = jax.ShapeDtypeStruct((RIM2 * c + half, HALF), BF16)
+    block_of = jax.ShapeDtypeStruct((half, HALF), BF16)
+    last = rows // RIM2 - 1
+    to_up, to_down, own = pl.pallas_call(
+        functools.partial(greet_kernel, rows, c),
+        grid=(1,),
+        out_shape=(greeting, greeting, block_of),
+        in_specs=[
+            pl.BlockSpec((rows, c), lambda _: (0, 0)),
+            pl.BlockSpec((RIM2, c, group), lambda _: (0, 0, 0)),
+            pl.BlockSpec((RIM2, c, group), lambda _: (last, 0, 0)),
+        ],
+        out_specs=(
+            pl.BlockSpec(greeting.shape, lambda _: (0, 0)),
+            pl.BlockSpec(greeting.shape, lambda _: (0, 0)),
+            pl.BlockSpec(block_of.shape, lambda _: (0, 0)),
+        ),
+        compiler_params=pltpu.CompilerParams(vmem_limit_bytes=SMALL),
+        name="greet",
+    )(features, cotangent, cotangent)
+    cot_up = beside(to_up, "bins", -1)
+    cot_down = beside(to_down, "bins", 1)
+    beyond = beside(own, "bins", 2)
     edge_shape = jax.ShapeDtypeStruct(((rows + 2 * RIM2) // 16 * c + c, HALF), BF16)
-    to_lo, to_hi = pl.pallas_call(
+    to_lo, to_hi, blocks = pl.pallas_call(
         functools.partial(edge_kernel, rows, c),
-        out_shape=(edge_shape, edge_shape),
-        in_specs=[VMEM] * 4,
-        out_specs=(VMEM,) * 2,
-        compiler_params=pltpu.CompilerParams(vmem_limit_bytes=LIMIT),
+        out_shape=(edge_shape, edge_shape, jax.ShapeDtypeStruct((4 * half, HALF), BF16)),
+        in_specs=[VMEM] * 6,
+        out_specs=(VMEM,) * 3,
+        compiler_params=pltpu.CompilerParams(vmem_limit_bytes=SMALL),
         name="edges",
-    )(cot_up, cotangent, cot_down, offset_embed)
+    )(cot_up, cotangent, cot_down, own, beyond, offset_embed)
+    first4 = joint(blocks, 0)
+    last4 = joint(blocks, 3)
     from_lo = beside(to_hi, "band", -1)
     from_hi = beside(to_lo, "band", 1)
 
@@ -365,21 +403,13 @@
 
     pair_map, payload = middle(
         rows, c, group, total_bins, total_band, devices,
-        (place, dilation, feats, cot_up, cotangent, cot_down, from_lo, from_hi, offset_embed,
-         left_weight, right_weight, taps, back_taps),
+        (place, dilation, blocks, first4, last4, cot_up, cotangent, cot_down, from_lo, from_hi,
+         offset_embed, left_weight, right_weight, taps, back_taps),
     )
     parts = lax.all_to_all(payload, every, 0, 0, tiled=True)
-    share, feature_part = pl.pallas_call(
-        share_kernel,
-        out_shape=(
-            jax.ShapeDtypeStruct((devices, 4, HALF), BF16),
-            jax.ShapeDtypeStruct((4, HALF), F32),
-        ),
-        in_specs=[VMEM],
-        out_specs=(VMEM,) * 2,
-        compiler_params=pltpu.CompilerParams(vmem_limit_bytes=LIMIT),
-        name="shares",
-    )(parts)
+    summed = jnp.sum(parts.astype(F32), axis=0)
+    feature_part = summed[:4]
+    share = jnp.broadcast_to(summed[None, 4:].astype(BF16), (devices, 4, HALF))
     total = lax.all_to_all(share, every, 0, 0, tiled=True)
     quarters = lax.all_gather(feature_part, "band")
     pairs = quarters.reshape(rows // 2, HALF)
@@ -395,7 +425,7 @@
         ),
         in_specs=[SMEM, VMEM],
         out_specs=(VMEM,) * 4,
-        compiler_params=pltpu.CompilerParams(vmem_limit_bytes=LIMIT),
+        compiler_params=pltpu.CompilerParams(vmem_limit_bytes=SMALL),
         name="unpack",
     )(place, total)
     return pair_map, grad_features, grad_left, grad_right, grad_offset, grad_kernels

time: 124 us -> 116 us (0.935)
  starting transfers between devices: 31.3 us -> 21.8 us
  blocking collectives: 41.8 us -> 49 us
  Pallas kernels: 28.5 us -> 23.3 us
  local copies, waits for them, and re-layouts: 7.95 us -> 3.63 us
  waiting for transfers between devices: 12 us -> 15.5 us
    all_to_all x1 -> x0, starting transfers between devices: 15.1 us -> none  [per_device(): lax.all_to_all(jnp.broadcast_to(packed[None], (bins,) + packed.shape), 'b...]
    all_to_all x1, blocking collectives: 34.6 us -> 41.8 us  [per_device(): parts = lax.all_to_all(payload, every, 0, 0, tiled=True)]
    ppermute x4 -> x5, starting transfers between devices: 11 us -> 13.9 us  [beside(): return lax.ppermute(block, axis, route)]
    ppermute x0 -> x2, starting transfers between devices: none -> 2.58 us  [joint(): return lax.ppermute(block, every, route)]
    unnamed x18 -> x17, local copies, waits for them, and re-layouts: 3.99 us -> 1.77 us
    pallas_call x1, Pallas kernels: 2.09 us -> 0.07 us  [per_device(): pl.pallas_call(functools.partial(greet_kernel, rows, c), grid=(1,), out_s...]
    ppermute x4 -> x5, waiting for transfers between devices: 4.77 us -> 6.63 us  [beside(): return lax.ppermute(block, axis, route)]
    pallas_call x1, Pallas kernels: 2.2 us -> 0.45 us  [per_device(): pl.pallas_call(functools.partial(edge_kernel, rows, c), out_shape=(edge_s...]
  transfers between devices with their start and end apart: 6 -> 8, of which waited for: 3 -> 4; matrix products, arithmetic and copies ran while one was open for 3% -> 2% of each run, Pallas kernels for 2% -> 0%
where the time goes in v3:
time: 116 us; the launch traced here: 115 us
  blocking collectives  49 us (42%)
  Pallas kernels  23.3 us (20%)
  starting transfers between devices  21.8 us (19%)
  waiting for transfers between devices  15.5 us (13%)
  local copies, waits for them, and re-layouts  3.63 us (3%)
    all_to_all x1, blocking collectives, per_device(): parts = lax.all_to_all(payload, every, 0, 0, tiled=True)  41.8 us
    pallas_call x1, Pallas kernels, middle(): pl.pallas_call(functools.partial(middle_kernel, rows, c, total_bins, tota...  21.3 us
    ppermute x5, starting transfers between devices, beside(): return lax.ppermute(block, axis, route)  13.9 us
    all_to_all x1, waiting for transfers between devices, per_device(): total = lax.all_to_all(share, every, 0, 0, tiled=True)  7.83 us
    all_gather x1, blocking collectives, per_device(): quarters = lax.all_gather(feature_part, 'band')  7.27 us
    ppermute x5, waiting for transfers between devices, beside(): return lax.ppermute(block, axis, route)  6.63 us
    all_to_all x1, starting transfers between devices, per_device(): total = lax.all_to_all(share, every, 0, 0, tiled=True)  5.26 us
    ppermute x2, starting transfers between devices, joint(): return lax.ppermute(block, every, route)  2.58 us
  transfers between devices with their start and end apart: 8, of which 4 were waited for; matrix products, arithmetic and copies ran while one was open for 2% of the time, Pallas kernels for 0%

profile of v3, /device:TPU:1, one launch (start us, length us, event | category | flops | bytes accessed | tf_op | source)
XLA Modules:
  0.0 115.0 jit_solution(14420800707585129118)
XLA Ops:
  0.6 1.0 copy-done
  1.7 0.7 copy-done.5
  2.4 0.1 greet.1
  2.4 4.5 %collective-permute-start = (bf16[528,128]{1,0:T(8,128)(2,1)S(1)}, bf16[528,128]{1,0:T(8,128)(2,1)S(1)}, u32[]{:S(2)}, u32[]{:S(2)}) collective-permute-start(bf16[528,128]{1,0:T(8,128)(2,1)S(1)} %get-tuple-element.18), channel_id=1, source_target_pairs={{0,4},{4,8},{8,12},{12,16},{16,20},{20,24},{24,28},{28,32},{32,36}... | collective-permute-start | bytes 405512 | tf_op jit(solution)/shard_map/ppermute | solution.py:352
  7.0 1.3 %collective-permute-start.1 = (bf16[528,128]{1,0:T(8,128)(2,1)S(1)}, bf16[528,128]{1,0:T(8,128)(2,1)S(1)}, u32[]{:S(2)}, u32[]{:S(2)}) collective-permute-start(bf16[528,128]{1,0:T(8,128)(2,1)S(1)} %get-tuple-element.19), channel_id=1, source_target_pairs={{4,0},{8,4},{12,8},{16,12},{20,16},{24,20},{28,24},{32,28},{36,32}... | collective-permute-start | bytes 405512 | tf_op jit(solution)/shard_map/ppermute | solution.py:352
  8.3 1.3 %collective-permute-start.2 = (bf16[16,128]{1,0:T(8,128)(2,1)S(1)}, bf16[16,128]{1,0:T(8,128)(2,1)S(1)}, u32[]{:S(2)}, u32[]{:S(2)}) collective-permute-start(bf16[16,128]{1,0:T(8,128)(2,1)S(1)} %get-tuple-element.20.own), channel_id=1, source_target_pairs={{8,0},{12,4},{16,8},{20,12},{24,16},{28,20},{32,24},{36,28},{40,32... | collective-permute-start | bytes 12296 | tf_op jit(solution)/shard_map/ppermute | solution.py:352
  9.6 0.0 copy-start.7
  9.6 5.2 %collective-permute-done.2.beyond = bf16[16,128]{1,0:T(8,128)(2,1)S(1)} collective-permute-done((bf16[16,128]{1,0:T(8,128)(2,1)S(1)}, bf16[16,128]{1,0:T(8,128)(2,1)S(1)}, u32[]{:S(2)}, u32[]{:S(2)}) %collective-permute-start.2) | collective-permute-done | bytes 4128 | tf_op jit(solution)/shard_map/ppermute | solution.py:352
  14.8 0.5 edges.1
  15.3 1.3 %collective-permute-start.4 = (bf16[64,128]{1,0:T(8,128)(2,1)S(1)}, bf16[64,128]{1,0:T(8,128)(2,1)S(1)}, u32[]{:S(2)}, u32[]{:S(2)}) collective-permute-start(bf16[64,128]{1,0:T(8,128)(2,1)S(1)} %get-tuple-element.21.near4), channel_id=1, source_target_pairs={{12,0},{29,1},{46,2},{63,3},{16,4},{33,5},{50,6},{67,7},{20,8},{37... | collective-permute-start | bytes 49160 | tf_op jit(solution)/shard_map/ppermute | solution.py:361
  16.6 1.3 %collective-permute-start.3 = (bf16[64,128]{1,0:T(8,128)(2,1)S(1)}, bf16[64,128]{1,0:T(8,128)(2,1)S(1)}, u32[]{:S(2)}, u32[]{:S(2)}) collective-permute-start(bf16[64,128]{1,0:T(8,128)(2,1)S(1)} %get-tuple-element.21.near4), channel_id=1, source_target_pairs={{0,0},{17,1},{34,2},{51,3},{4,4},{21,5},{38,6},{55,7},{8,8},{25,9}... | collective-permute-start | bytes 49160 | tf_op jit(solution)/shard_map/ppermute | solution.py:361
  17.9 4.9 %collective-permute-start.5 = (bf16[256,128]{1,0:T(8,128)(2,1)S(1)}, bf16[256,128]{1,0:T(8,128)(2,1)S(1)}, u32[]{:S(2)}, u32[]{:S(2)}) collective-permute-start(bf16[256,128]{1,0:T(8,128)(2,1)S(1)} %get-tuple-element.22), channel_id=1, source_target_pairs={{0,1},{1,2},{2,3},{4,5},{5,6},{6,7},{8,9},{9,10},{10,11},{12,13},{... | collective-permute-start | bytes 196616 | tf_op jit(solution)/shard_map/ppermute | solution.py:352
  22.8 1.9 %collective-permute-start.6 = (bf16[256,128]{1,0:T(8,128)(2,1)S(1)}, bf16[256,128]{1,0:T(8,128)(2,1)S(1)}, u32[]{:S(2)}, u32[]{:S(2)}) collective-permute-start(bf16[256,128]{1,0:T(8,128)(2,1)S(1)} %get-tuple-element.23), channel_id=1, source_target_pairs={{1,0},{2,1},{3,2},{5,4},{6,5},{7,6},{9,8},{10,9},{11,10},{13,12},{... | collective-permute-start | bytes 196616 | tf_op jit(solution)/shard_map/ppermute | solution.py:352
  24.7 0.1 pad_add_fusion.place
  24.8 0.2 copy.17
  25.1 0.2 reshape.23.taps
  25.3 0.3 copy.18
  25.6 0.0 copy-start.4
  25.6 0.0 copy-start.6
  25.6 0.2 reshape.24.back_taps
  25.9 1.1 collective-permute-done.4.last4
  26.9 1.4 %collective-permute-done.6.from_hi = bf16[256,128]{1,0:T(8,128)(2,1)S(1)} collective-permute-done((bf16[256,128]{1,0:T(8,128)(2,1)S(1)}, bf16[256,128]{1,0:T(8,128)(2,1)S(1)}, u32[]{:S(2)}, u32[]{:S(2)}) %collective-permute-start.6) | collective-permute-done | bytes 65568 | tf_op jit(solution)/shard_map/ppermute | solution.py:352
  28.4 21.3 %middle.1 = (bf16[32,64,128]{2,1,0:T(8,128)(2,1)}, bf16[256,8,128]{2,1,0:T(8,128)(2,1)S(1)}) custom-call(s32[2]{0:T(128)S(1)} %pad_add_fusion.place, s32[2]{0:T(128)S(1)} %copy-done.6, bf16[64,128]{1,0:T(8,128)(2,1)S(1)} %get-tuple-element.21.near4, bf16[64,128]{1,0:T(8,128)(2,1)S(1)} %collective-permute-done.3.first4, ...), custom_call_target="tpu_custom_call" | custom-call | tf_op jit(solution)/shard_map/middle/pallas_call | solution.py:255
  49.6 41.8 %all_to_all.10 = bf16[256,8,128]{2,1,0:T(8,128)(2,1)S(1)} all-to-all(bf16[256,8,128]{2,1,0:T(8,128)(2,1)S(1)} %get-tuple-element.25), channel_id=1, replica_groups=mesh['bins'=64,'band'=4] {'bins','band'}, dimensions={0} | all-to-all | bytes 1048576 | tf_op jit(solution)/shard_map/all_to_all | solution.py:409
  91.4 0.3 convert_reduce_fusion
  91.7 0.8 broadcast_in_dim.2
  92.5 5.3 %all-to-all-start.1 = ((bf16[256,4,128]{2,1,0:T(4,128)(2,1)}), bf16[256,4,128]{2,1,0:T(4,128)(2,1)S(1)}, u32[]{:S(2)}, u32[]{:S(2)}) async-start(bf16[256,4,128]{2,1,0:T(4,128)(2,1)} %broadcast_in_dim.2), calls=%async_computation.1 | async-start | bytes 524288 | tf_op jit(solution)/shard_map/all_to_all | solution.py:413
  97.7 7.3 %all-gather.1 = f32[4,4,128]{2,1,0:T(4,128)S(1)} all-gather(f32[1,4,128]{2,1,0:T(4,128)S(1)} %slice_bitcast_fusion), channel_id=2, replica_groups=mesh['bins'=64,'band'=4] {'band'}, dimensions={0}, use_global_device_ids=true | all-gather | bytes 10240 | tf_op jit(solution)/shard_map/all_gather | solution.py:414
  105.0 0.1 fusion
  105.1 0.6 maximum_multiply_fusion
  105.7 7.8 %all-to-all-done.1.total = bf16[256,4,128]{2,1,0:T(4,128)(2,1)S(1)} async-done(((bf16[256,4,128]{2,1,0:T(4,128)(2,1)}), bf16[256,4,128]{2,1,0:T(4,128)(2,1)S(1)}, u32[]{:S(2)}, u32[]{:S(2)}) %all-to-all-start.1) | async-done | bytes 262176 | tf_op jit(solution)/shard_map/all_to_all | solution.py:413
  113.5 1.5 %unpack.1 = (f32[64,64]{1,0:T(8,128)}, f32[64,64]{1,0:T(8,128)}, f32[64,128]{1,0:T(8,128)}, f32[2,3,3,64,64]{4,3,2,1,0:T(8,128)}) custom-call(s32[2]{0:T(128)S(1)} %pad_add_fusion.place, bf16[256,4,128]{2,1,0:T(4,128)(2,1)S(1)} %all-to-all-done.1.total), custom_call_target="tpu_custom_call" | custom-call | tf_op jit(solution)/shard_map/unpack/pallas_call | solution.py:418
  (18 shorter events, 0.1 us)
Async XLA Ops:
  0.6 1.0 copy-start
  1.7 0.7 copy-start.5
  2.4 12.4 %copy-start.1 = (bf16[32,64,128]{2,1,0:T(8,128)(2,1)S(1)}, bf16[32,64,128]{2,1,0:T(8,128)(2,1)}, u32[]{:S(2)}) copy-start(bf16[32,64,128]{2,1,0:T(8,128)(2,1)} %cot.3) | copy-start | bytes 1572868
  2.4 12.3 %copy-start.2 = (bf16[64,128]{1,0:T(8,128)(2,1)S(1)}, bf16[64,128]{1,0:T(8,128)(2,1)}, u32[]{:S(2)}) copy-start(bf16[64,128]{1,0:T(8,128)(2,1)} %emb.3) | copy-start | bytes 49156
  2.4 12.3 %collective-permute-start = (bf16[528,128]{1,0:T(8,128)(2,1)S(1)}, bf16[528,128]{1,0:T(8,128)(2,1)S(1)}, u32[]{:S(2)}, u32[]{:S(2)}) collective-permute-start(bf16[528,128]{1,0:T(8,128)(2,1)S(1)} %get-tuple-element.18), channel_id=1, source_target_pairs={{0,4},{4,8},{8,12},{12,16},{16,20},{20,24},{24,28},{28,32},{32,36}... | collective-permute-start | bytes 405512 | tf_op jit(solution)/shard_map/ppermute | solution.py:352
  7.0 7.8 %collective-permute-start.1 = (bf16[528,128]{1,0:T(8,128)(2,1)S(1)}, bf16[528,128]{1,0:T(8,128)(2,1)S(1)}, u32[]{:S(2)}, u32[]{:S(2)}) collective-permute-start(bf16[528,128]{1,0:T(8,128)(2,1)S(1)} %get-tuple-element.19), channel_id=1, source_target_pairs={{4,0},{8,4},{12,8},{16,12},{20,16},{24,20},{28,24},{32,28},{36,32}... | collective-permute-start | bytes 405512 | tf_op jit(solution)/shard_map/ppermute | solution.py:352
  8.3 6.5 %collective-permute-start.2 = (bf16[16,128]{1,0:T(8,128)(2,1)S(1)}, bf16[16,128]{1,0:T(8,128)(2,1)S(1)}, u32[]{:S(2)}, u32[]{:S(2)}) collective-permute-start(bf16[16,128]{1,0:T(8,128)(2,1)S(1)} %get-tuple-element.20.own), channel_id=1, source_target_pairs={{8,0},{12,4},{16,8},{20,12},{24,16},{28,20},{32,24},{36,28},{40,32... | collective-permute-start | bytes 12296 | tf_op jit(solution)/shard_map/ppermute | solution.py:352
  9.6 15.2 %copy-start.7 = (bf16[2,3,3,64,64]{4,3,2,1,0:T(8,128)(2,1)S(1)}, bf16[2,3,3,64,64]{4,3,2,1,0:T(8,128)(2,1)}, u32[]{:S(2)}) copy-start(bf16[2,3,3,64,64]{4,3,2,1,0:T(8,128)(2,1)} %param.11) | copy-start | bytes 442372
  15.3 11.7 %collective-permute-start.4 = (bf16[64,128]{1,0:T(8,128)(2,1)S(1)}, bf16[64,128]{1,0:T(8,128)(2,1)S(1)}, u32[]{:S(2)}, u32[]{:S(2)}) collective-permute-start(bf16[64,128]{1,0:T(8,128)(2,1)S(1)} %get-tuple-element.21.near4), channel_id=1, source_target_pairs={{12,0},{29,1},{46,2},{63,3},{16,4},{33,5},{50,6},{67,7},{20,8},{37... | collective-permute-start | bytes 49160 | tf_op jit(solution)/shard_map/ppermute | solution.py:361
  16.6 10.4 %collective-permute-start.3 = (bf16[64,128]{1,0:T(8,128)(2,1)S(1)}, bf16[64,128]{1,0:T(8,128)(2,1)S(1)}, u32[]{:S(2)}, u32[]{:S(2)}) collective-permute-start(bf16[64,128]{1,0:T(8,128)(2,1)S(1)} %get-tuple-element.21.near4), channel_id=1, source_target_pairs={{0,0},{17,1},{34,2},{51,3},{4,4},{21,5},{38,6},{55,7},{8,8},{25,9}... | collective-permute-start | bytes 49160 | tf_op jit(solution)/shard_map/ppermute | solution.py:361
  17.9 9.1 %collective-permute-start.5 = (bf16[256,128]{1,0:T(8,128)(2,1)S(1)}, bf16[256,128]{1,0:T(8,128)(2,1)S(1)}, u32[]{:S(2)}, u32[]{:S(2)}) collective-permute-start(bf16[256,128]{1,0:T(8,128)(2,1)S(1)} %get-tuple-element.22), channel_id=1, source_target_pairs={{0,1},{1,2},{2,3},{4,5},{5,6},{6,7},{8,9},{9,10},{10,11},{12,13},{... | collective-permute-start | bytes 196616 | tf_op jit(solution)/shard_map/ppermute | solution.py:352
  22.8 5.6 %collective-permute-start.6 = (bf16[256,128]{1,0:T(8,128)(2,1)S(1)}, bf16[256,128]{1,0:T(8,128)(2,1)S(1)}, u32[]{:S(2)}, u32[]{:S(2)}) collective-permute-start(bf16[256,128]{1,0:T(8,128)(2,1)S(1)} %get-tuple-element.23), channel_id=1, source_target_pairs={{1,0},{2,1},{3,2},{5,4},{6,5},{7,6},{9,8},{10,9},{11,10},{13,12},{... | collective-permute-start | bytes 196616 | tf_op jit(solution)/shard_map/ppermute | solution.py:352
  25.6 2.8 %copy-start.3 = (bf16[64,64]{1,0:T(8,128)(2,1)S(1)}, bf16[64,64]{1,0:T(8,128)(2,1)}, u32[]{:S(2)}) copy-start(bf16[64,64]{1,0:T(8,128)(2,1)} %lw.1) | copy-start | bytes 24580
  25.6 2.8 %copy-start.4 = (bf16[64,64]{1,0:T(8,128)(2,1)S(1)}, bf16[64,64]{1,0:T(8,128)(2,1)}, u32[]{:S(2)}) copy-start(bf16[64,64]{1,0:T(8,128)(2,1)} %rw.1) | copy-start | bytes 24580
  25.6 2.8 %copy-start.6 = (s32[2]{0:T(128)S(1)}, s32[2]{0:T(128)}, u32[]{:S(2)}) copy-start(s32[2]{0:T(128)} %dil.1) | copy-start | bytes 28
  92.5 21.1 %all-to-all-start.1 = ((bf16[256,4,128]{2,1,0:T(4,128)(2,1)}), bf16[256,4,128]{2,1,0:T(4,128)(2,1)S(1)}, u32[]{:S(2)}, u32[]{:S(2)}) async-start(bf16[256,4,128]{2,1,0:T(4,128)(2,1)} %broadcast_in_dim.2), calls=%async_computation.1 | async-start | bytes 524288 | tf_op jit(solution)/shard_map/all_to_all | solution.py:413

commit v4 on v2

--- a/solution.py
+++ b/solution.py
@@ -18,7 +18,9 @@
 RIM2 = 8
 RIM3 = 4
 CHUNK = 32
-LIMIT = 56 * 1024 * 1024
+HELD = 32
+LIMIT = 28 * 1024 * 1024
+SMALL = 8 * 1024 * 1024
 VMEM = pl.BlockSpec(memory_space=pltpu.VMEM)
 SMEM = pl.BlockSpec(memory_space=pltpu.SMEM)
 
@@ -45,20 +47,38 @@
     return jnp.concatenate([jnp.where(first, a, b), jnp.where(first, b, a)], 1)
 
 
-def sweep(count, held, body):
+def sweep(count, held, body, before=None):
     def step(at, carry):
+        given = () if before is None else before(at)
         for k in range(held):
-            body(at * held + k)
+            body(at * held + k, k, *given)
         return carry
 
     lax.fori_loop(0, count // held, step, 0)
+
+
+def lane_sums(values):
+    lane = lanes_of(HALF)
+    span = 1
+    while len(values) > 1:
+        even = (lane // span) % 2 == 0
+        values = [
+            jnp.where(even, a, b) + pltpu.roll(jnp.where(even, b, a), HALF - span, 1)
+            for a, b in zip(values[0::2], values[1::2])
+        ]
+        span *= 2
+    (total,) = values
+    while span < HALF:
+        total = total + pltpu.roll(total, span, 1)
+        span *= 2
+    return total
 
 
 def middle_kernel(
     rows, c, total_bins, total_band,
     place, dil, feats, cot_up, cot, cot_down, from_lo, from_hi, emb, lw, rw, taps, back_taps,
     pair_map, payload,
-    proj, embed, s0, s1, slope_s, slope0, wide_cot, pairs, g1, g0, sums, edge,
+    proj, lefts, pick, embed, s0, s1, slope_s, slope0, wide_cot, pairs, g1, g0, sums, edge,
 ):
     bins = total_bins // rows
     group = emb.shape[1]
@@ -79,8 +99,7 @@
         return jnp.where((offset >= 0) & (offset < top), 1.0, 0.0).astype(F32)
 
     def block(index):
-        inside = (index >= 0) & (index < bins)
-        half = feats[jnp.clip(index, 0, bins - 1)].astype(F32) * jnp.where(inside, 1.0, 0.0)
+        half = feats[jnp.clip(index, 0, bins - 1)].astype(F32)
         return jnp.concatenate([half[:, :c], half[:, c:]], 0)
 
     base = place[0] + place[1] * span
@@ -89,10 +108,12 @@
     filler = jnp.zeros((WIDE - (span + 3) * rows, c), F32)
     fw = jnp.concatenate(window + [filler], 0).astype(BF16)
     right = jnp.dot(fw, rw[...], preferred_element_type=F32).astype(BF16).astype(F32)
-    filler = jnp.zeros((WIDE - 3 * rows, c), F32)
-    fl = jnp.concatenate(near + [filler], 0).astype(BF16)
-    left = jnp.dot(fl, lw[...], preferred_element_type=F32).astype(BF16).astype(F32)
-    proj[...] = jnp.concatenate([right, left], 1).T
+    proj[...] = jnp.concatenate([right, jnp.zeros_like(right)], 1).T[0:c]
+    fl = jnp.concatenate(near, 0).astype(BF16)
+    lefts[...] = jnp.dot(fl, lw[...], preferred_element_type=F32).astype(BF16)
+    lane = lax.broadcasted_iota(jnp.int32, (16, 16 * HALF), 1)
+    which = lax.broadcasted_iota(jnp.int32, (16, 16 * HALF), 0)
+    pick[...] = jnp.where(lane // HALF == which, 1.0, 0.0).astype(BF16)
     beside = jnp.where(
         lanes_of(HALF) < HALF // 2, from_hi[edges:, :].astype(F32), from_lo[edges:, :].astype(F32)
     )
@@ -101,24 +122,31 @@
     wide_cot[RIM2 : RIM2 + rows] = cot[...]
     wide_cot[RIM2 + rows :] = cot_down[...]
 
-    def state_row(row):
-        lag = down(proj[0:c, :], RIM0 + row)
-        mine = pltpu.roll(proj[c : 2 * c, 0:HALF], HALF - RIM0 - row, 1)[:, 0:1]
-        summed = mine + lag + embed[...]
+    def state_step(at):
+        mine = lax.dot_general(
+            lefts[pl.ds(pl.multiple_of(at * 16 + RIM0, 16), 16), :], pick[...],
+            (((0,), (0,)), ((), ())), preferred_element_type=F32,
+        )
+        return (mine,)
+
+    def state_row(row, k, mine):
+        lag = down(proj[...], RIM0 + row)
+        mine = mine[:, k * HALF : (k + 1) * HALF]
+        summed = jnp.concatenate([mine, mine], 1) + lag + embed[...]
         sig = sigmoid(summed)
         mask = mask_of(first_bin - RIM0 + row)
         s0[rows_at(row), :] = (summed * sig * mask).astype(BF16)
         slope = sig * (1.0 + summed * (1.0 - sig)) * mask
         slope_s[rows_at(row), :] = slope[:, 0:HALF]
 
-    sweep(rows + 2 * RIM0, 16, state_row)
+    sweep(rows + 2 * RIM0, 16, state_row, state_step)
 
     def convolved(weights, source, base_row, rate):
         view = jnp.concatenate([source[rows_at(base_row + rate * k), :] for k in (-1, 0, 1)], 0)
         parts = jnp.dot(weights, view, preferred_element_type=F32)
         return parts[0:c], parts[c : 2 * c], parts[2 * c : 3 * c]
 
-    def layer_row0(row):
+    def layer_row0(row, k):
         a, b, d = convolved(taps[0], s0, row + RIM0 - RIM1, rate0)
         pre = up(a, rate0) + b + down(d, rate0)
         sig = sigmoid(pre)
@@ -126,27 +154,28 @@
         s1[rows_at(row), :] = (pre * sig * mask).astype(BF16)
         slope0[rows_at(row), :] = sig * (1.0 + pre * (1.0 - sig)) * mask
 
-    sweep(rows + 2 * RIM1, 28, layer_row0)
-
-    def layer_row1(row):
+    sweep(rows + 2 * RIM1, 56, layer_row0)
+
+    def layer_step1(at):
+        return from_lo[rows_at(at), :].astype(F32), from_hi[rows_at(at), :].astype(F32)
+
+    def layer_row1(row, k, lo, hi):
         a, b, d = convolved(taps[1], s1, row + RIM1 - RIM2, rate1)
         pre = up(a, rate1) + b + down(d, rate1)
         sig = sigmoid(pre)
         mask = mask_of(first_bin - RIM2 + row)
         slope = sig * (1.0 + pre * (1.0 - sig)) * mask
         pairs[row] = (pre * sig * mask)[:, 0:HALF].astype(BF16)
-        tile = rows_at(row // 16)
-        turn = (row % 16) * RIM2
-        hi = pltpu.roll(from_hi[tile, :].astype(F32), (HALF - turn) % HALF, 1)
-        lo = pltpu.roll(from_lo[tile, :].astype(F32), HALF - RIM2 - turn, 1)
+        lo = pltpu.roll(lo, (HALF - RIM2 * (k + 1)) % HALF, 1)
+        hi = pltpu.roll(hi, (HALF - RIM2 * k) % HALF, 1)
         rim = jnp.where(lanes_of(HALF) < HALF // 2, hi, lo)
         grad = jnp.concatenate([wide_cot[row].astype(F32), rim], 1)
         g1[rows_at(row), :] = (grad * slope).astype(BF16)
 
-    sweep(rows + 2 * RIM2, 16, layer_row1)
+    sweep(rows + 2 * RIM2, 16, layer_row1, layer_step1)
     pair_map[...] = pairs[RIM2 : RIM2 + rows]
 
-    def back_row(row):
+    def back_row(row, k):
         a, b, d = convolved(back_taps[1], g1, row + RIM2 - RIM3, -rate1)
         back = down(a, rate1) + b + up(d, rate1)
         slope = slope0[rows_at(row + RIM1 - RIM3), :]
@@ -194,19 +223,33 @@
     sums[...] = jnp.zeros_like(sums)
     lane = lanes_of(HALF)
 
-    def last_row(row):
-        a, b, d = convolved(back_taps[0], g0, row + RIM3, -rate0)
-        back = (down(a, rate0) + b + up(d, rate0))[:, 0:HALF]
-        grad = back * slope_s[rows_at(row + RIM0), :]
-        total = jnp.sum(grad, axis=1, keepdims=True)
-        sums[:, 0:HALF] += jnp.where(lane == row, total, 0.0)
-        turned = pltpu.roll(grad, row, 1)
-        wrapped = jnp.where(lane < row, turned, 0.0)
-        sums[:, HALF : 2 * HALF] += turned - wrapped
-        sums[:, 2 * HALF : 3 * HALF] += wrapped
-        sums[:, 3 * HALF : 4 * HALF] += grad
-
-    sweep(rows, 16, last_row)
+    def last_step(at, carry):
+        grads = []
+        offset_sum = jnp.zeros((c, HALF), F32)
+        window = jnp.zeros((c, HALF), F32)
+        wrap = jnp.zeros((c, HALF), F32)
+        for k in range(HELD):
+            row = at * HELD + k
+            a, b, d = convolved(back_taps[0], g0, row + RIM3, -rate0)
+            back = (down(a, rate0) + b + up(d, rate0))[:, 0:HALF]
+            grad = back * slope_s[rows_at(row + RIM0), :]
+            grads.append(grad)
+            offset_sum = offset_sum + grad
+            turned = pltpu.roll(grad, k, 1) if k else grad
+            wrapped = jnp.where(lane < k, turned, 0.0)
+            window = window + (turned - wrapped)
+            wrap = wrap + wrapped
+        here = (lane >= at * HELD) & (lane < (at + 1) * HELD)
+        sums[:, 0:HALF] += jnp.where(here, lane_sums(grads), 0.0)
+        first = lane < at * HELD
+        window = pltpu.roll(window, at * HELD, 1)
+        wrap = pltpu.roll(wrap, at * HELD, 1)
+        sums[:, HALF : 2 * HALF] += jnp.where(first, 0.0, window)
+        sums[:, 2 * HALF : 3 * HALF] += jnp.where(first, window, 0.0) + wrap
+        sums[:, 3 * HALF : 4 * HALF] += offset_sum
+        return carry
+
+    lax.fori_loop(0, rows // HELD, last_step, 0)
 
     highest = lax.Precision.HIGHEST
     both = sums[:, 0 : 3 * HALF]
@@ -261,7 +304,9 @@
         in_specs=[SMEM] * 2 + [VMEM] * (len(args) - 2),
         out_specs=(VMEM,) * 2,
         scratch_shapes=[
-            pltpu.VMEM((2 * c, WIDE), F32),
+            pltpu.VMEM((c, WIDE), F32),
+            pltpu.VMEM((3 * rows, c), BF16),
+            pltpu.VMEM((16, 16 * HALF), BF16),
             pltpu.VMEM((c, WIDE), F32),
             pltpu.VMEM((tall(RIM0), WIDE), BF16),
             pltpu.VMEM((tall(RIM1), WIDE), BF16),
@@ -303,10 +348,9 @@
     to_hi[count // 16 * c :, :] = emb[...]
 
 
-def share_kernel(parts, share, features):
-    total = jnp.sum(parts[...].astype(F32), axis=0)
-    features[...] = total[0:4]
-    share[...] = jnp.broadcast_to(total[4:8].astype(BF16)[None], share.shape)
+def greet_kernel(rows, c, features, everywhere):
+    packed = jnp.concatenate([features[0 : rows // 2, :], features[rows // 2 :, :]], 1)
+    everywhere[...] = jnp.broadcast_to(packed[None], everywhere.shape)
 
 
 def unpack_kernel(c, whole_scale, offset_scale, place, total, left, right, offset, kernels):
@@ -339,13 +383,17 @@
 
     def beside(block, axis, step):
         count = lax.axis_size(axis)
-        route = [(i + step, i) for i in range(count) if 0 <= i + step < count]
-        return lax.ppermute(block, axis, route)
-
-    packed = jnp.concatenate([features[: rows // 2], features[rows // 2 :]], 1)
-    feats = lax.all_to_all(
-        jnp.broadcast_to(packed[None], (bins,) + packed.shape), "bins", 0, 0, tiled=True
-    )
+        return lax.ppermute(block, axis, [((i + step) % count, i) for i in range(count)])
+
+    everywhere = pl.pallas_call(
+        functools.partial(greet_kernel, rows, c),
+        out_shape=jax.ShapeDtypeStruct((bins, rows // 2, HALF), BF16),
+        in_specs=[VMEM],
+        out_specs=VMEM,
+        compiler_params=pltpu.CompilerParams(vmem_limit_bytes=SMALL),
+        name="greet",
+    )(features)
+    feats = lax.all_to_all(everywhere, "bins", 0, 0, tiled=True)
     cot_up = beside(cotangent[rows - RIM2 :], "bins", -1)
     cot_down = beside(cotangent[:RIM2], "bins", 1)
     edge_shape = jax.ShapeDtypeStruct(((rows + 2 * RIM2) // 16 * c + c, HALF), BF16)
@@ -354,7 +402,7 @@
         out_shape=(edge_shape, edge_shape),
         in_specs=[VMEM] * 4,
         out_specs=(VMEM,) * 2,
-        compiler_params=pltpu.CompilerParams(vmem_limit_bytes=LIMIT),
+        compiler_params=pltpu.CompilerParams(vmem_limit_bytes=SMALL),
         name="edges",
     )(cot_up, cotangent, cot_down, offset_embed)
     from_lo = beside(to_hi, "band", -1)
@@ -369,17 +417,9 @@
          left_weight, right_weight, taps, back_taps),
     )
     parts = lax.all_to_all(payload, every, 0, 0, tiled=True)
-    share, feature_part = pl.pallas_call(
-        share_kernel,
-        out_shape=(
-            jax.ShapeDtypeStruct((devices, 4, HALF), BF16),
-            jax.ShapeDtypeStruct((4, HALF), F32),
-        ),
-        in_specs=[VMEM],
-        out_specs=(VMEM,) * 2,
-        compiler_params=pltpu.CompilerParams(vmem_limit_bytes=LIMIT),
-        name="shares",
-    )(parts)
+    summed = jnp.sum(parts.astype(F32), axis=0)
+    feature_part = summed[:4]
+    share = jnp.broadcast_to(summed[None, 4:].astype(BF16), (devices, 4, HALF))
     total = lax.all_to_all(share, every, 0, 0, tiled=True)
     quarters = lax.all_gather(feature_part, "band")
     pairs = quarters.reshape(rows // 2, HALF)
@@ -395,7 +435,7 @@
         ),
         in_specs=[SMEM, VMEM],
         out_specs=(VMEM,) * 4,
-        compiler_params=pltpu.CompilerParams(vmem_limit_bytes=LIMIT),
+        compiler_params=pltpu.CompilerParams(vmem_limit_bytes=SMALL),
         name="unpack",
     )(place, total)
     return pair_map, grad_features, grad_left, grad_right, grad_offset, grad_kernels

time: 124 us -> 107 us (0.86)
  Pallas kernels: 28.5 us -> 18.8 us
  blocking collectives: 41.8 us -> 33 us
  waiting for transfers between devices: 12 us -> 20.1 us
  local copies, waits for them, and re-layouts: 7.95 us -> 2.66 us
    all_to_all x1, blocking collectives: 34.6 us -> 25.7 us  [per_device(): parts = lax.all_to_all(payload, every, 0, 0, tiled=True)]
    ppermute x4, waiting for transfers between devices: 4.77 us -> 12.2 us  [beside(): lax.ppermute(block, axis, [((i + step) % count, i) for i in range(count)])]
    pallas_call x1, Pallas kernels: 22.3 us -> 16 us  [middle(): pl.pallas_call(functools.partial(middle_kernel, rows, c, total_bins, tota...]
    unnamed x18 -> x15, local copies, waits for them, and re-layouts: 3.99 us -> 0.78 us
    pallas_call x1, Pallas kernels: 2.2 us -> 0.45 us  [per_device(): pl.pallas_call(functools.partial(edge_kernel, rows, c), out_shape=(edge_s...]
    pallas_call x1, Pallas kernels: 2.09 us -> 0.8 us  [per_device(): pl.pallas_call(functools.partial(greet_kernel, rows, c), out_shape=jax.Sh...]
  transfers between devices with their start and end apart: 6 -> 6, of which waited for: 3 -> 5; matrix products, arithmetic and copies ran while one was open for 3% -> 2% of each run, Pallas kernels for 2% -> 0%
where the time goes in v4:
time: 107 us
  blocking collectives  33 us (31%)
  starting transfers between devices  30.3 us (28%)
  waiting for transfers between devices  20.1 us (19%)
  Pallas kernels  18.8 us (18%)
  local copies, waits for them, and re-layouts  2.66 us (2%)
    all_to_all x1, blocking collectives, per_device(): parts = lax.all_to_all(payload, every, 0, 0, tiled=True)  25.7 us
    pallas_call x1, Pallas kernels, middle(): pl.pallas_call(functools.partial(middle_kernel, rows, c, total_bins, tota...  16 us
    all_to_all x1, starting transfers between devices, per_device(): feats = lax.all_to_all(everywhere, 'bins', 0, 0, tiled=True)  15.1 us
    ppermute x4, waiting for transfers between devices, beside(): lax.ppermute(block, axis, [((i + step) % count, i) for i in range(count)])  12.2 us
    ppermute x4, starting transfers between devices, beside(): lax.ppermute(block, axis, [((i + step) % count, i) for i in range(count)])  9.94 us
    all_to_all x1, waiting for transfers between devices, per_device(): total = lax.all_to_all(share, every, 0, 0, tiled=True)  7.83 us
    all_gather x1, blocking collectives, per_device(): quarters = lax.all_gather(feature_part, 'band')  7.27 us
    all_to_all x1, starting transfers between devices, per_device(): total = lax.all_to_all(share, every, 0, 0, tiled=True)  5.26 us
  transfers between devices with their start and end apart: 6, of which 5 were waited for; matrix products, arithmetic and copies ran while one was open for 2% of the time, Pallas kernels for 0%

profile of v4, /device:TPU:1, one launch (start us, length us, event | category | flops | bytes accessed | tf_op | source)
XLA Modules:
  0.0 106.5 jit_solution(5051257764698985968)
XLA Ops:
  0.6 0.0 copy-start
  0.6 0.0 copy-start.4
  0.7 0.7 copy-done.4
  1.4 0.8 greet.1
  2.2 15.1 %all-to-all-start = ((bf16[64,16,128]{2,1,0:T(8,128)(2,1)}), bf16[64,16,128]{2,1,0:T(8,128)(2,1)S(1)}, u32[]{:S(2)}, u32[]{:S(2)}) async-start(bf16[64,16,128]{2,1,0:T(8,128)(2,1)} %greet.1), calls=%async_computation | async-start | bytes 524288 | tf_op jit(solution)/shard_map/all_to_all | solution.py:396
  17.3 0.0 copy-start.6
  17.4 7.1 %collective-permute-start.1 = (bf16[8,64,128]{2,1,0:T(8,128)(2,1)S(1)}, bf16[8,64,128]{2,1,0:T(8,128)(2,1)S(1)}, u32[]{:S(2)}, u32[]{:S(2)}) collective-permute-start(bf16[8,64,128]{2,1,0:T(8,128)(2,1)S(1)} %get-tuple-element.22), channel_id=1, source_target_pairs={{4,0},{8,4},{12,8},{16,12},{20,16},{24,20},{28,24},{32,28},{36,32}... | collective-permute-start | bytes 393224 | tf_op jit(solution)/shard_map/ppermute | solution.py:386
  24.5 0.0 collective-permute-start
  24.5 0.2 copy.17
  24.8 0.2 reshape.23.taps
  25.0 0.3 copy.18
  25.3 0.0 copy-start.1
  25.3 0.2 reshape.24.back_taps
  25.5 1.1 %collective-permute-done.1.cot_down = bf16[8,64,128]{2,1,0:T(8,128)(2,1)S(1)} collective-permute-done((bf16[8,64,128]{2,1,0:T(8,128)(2,1)S(1)}, bf16[8,64,128]{2,1,0:T(8,128)(2,1)S(1)}, u32[]{:S(2)}, u32[]{:S(2)}) %collective-permute-start.1) | collective-permute-done | bytes 131104 | tf_op jit(solution)/shard_map/ppermute | solution.py:386
  26.6 7.6 %collective-permute-done.cot_up = bf16[8,64,128]{2,1,0:T(8,128)(2,1)S(1)} collective-permute-done((bf16[8,64,128]{2,1,0:T(8,128)(2,1)S(1)}, bf16[8,64,128]{2,1,0:T(8,128)(2,1)S(1)}, u32[]{:S(2)}, u32[]{:S(2)}) %collective-permute-start) | collective-permute-done | bytes 131104 | tf_op jit(solution)/shard_map/ppermute | solution.py:386
  34.2 0.4 edges.1
  34.7 2.7 %collective-permute-start.2 = (bf16[256,128]{1,0:T(8,128)(2,1)S(1)}, bf16[256,128]{1,0:T(8,128)(2,1)S(1)}, u32[]{:S(2)}, u32[]{:S(2)}) collective-permute-start(bf16[256,128]{1,0:T(8,128)(2,1)S(1)} %get-tuple-element.14), channel_id=1, source_target_pairs={{3,0},{0,1},{1,2},{2,3},{7,4},{4,5},{5,6},{6,7},{11,8},{8,9},{9,10... | collective-permute-start | bytes 196616 | tf_op jit(solution)/shard_map/ppermute | solution.py:386
  37.4 0.1 collective-permute-start.3
  37.5 0.1 pad_add_fusion.place
  37.6 1.2 %collective-permute-done.2.from_lo = bf16[256,128]{1,0:T(8,128)(2,1)S(1)} collective-permute-done((bf16[256,128]{1,0:T(8,128)(2,1)S(1)}, bf16[256,128]{1,0:T(8,128)(2,1)S(1)}, u32[]{:S(2)}, u32[]{:S(2)}) %collective-permute-start.2) | collective-permute-done | bytes 65568 | tf_op jit(solution)/shard_map/ppermute | solution.py:386
  38.8 2.4 %collective-permute-done.3.from_hi = bf16[256,128]{1,0:T(8,128)(2,1)S(1)} collective-permute-done((bf16[256,128]{1,0:T(8,128)(2,1)S(1)}, bf16[256,128]{1,0:T(8,128)(2,1)S(1)}, u32[]{:S(2)}, u32[]{:S(2)}) %collective-permute-start.3) | collective-permute-done | bytes 65568 | tf_op jit(solution)/shard_map/ppermute | solution.py:386
  41.1 0.0 all-to-all-done.feats
  41.2 16.0 %middle.1 = (bf16[32,64,128]{2,1,0:T(8,128)(2,1)}, bf16[256,8,128]{2,1,0:T(8,128)(2,1)S(1)}) custom-call(s32[2]{0:T(128)S(1)} %pad_add_fusion.place, s32[2]{0:T(128)S(1)} %copy-done.5, bf16[64,16,128]{2,1,0:T(8,128)(2,1)S(1)} %all-to-all-done.feats, bf16[8,64,128]{2,1,0:T(8,128)(2,1)S(1)} %collective-permute-done.cot_up, bf16[32,64,128]{2,1,0:T(8,128)(2,1)S(1)} %copy-done, ...), custom_call_target="tpu_custom_call" | custom-call | tf_op jit(solution)/shard_map/middle/pallas_call | solution.py:298
  57.1 25.7 %all_to_all.15 = bf16[256,8,128]{2,1,0:T(8,128)(2,1)S(1)} all-to-all(bf16[256,8,128]{2,1,0:T(8,128)(2,1)S(1)} %get-tuple-element.17), channel_id=1, replica_groups=mesh['bins'=64,'band'=4] {'bins','band'}, dimensions={0} | all-to-all | bytes 1048576 | tf_op jit(solution)/shard_map/all_to_all | solution.py:419
  82.9 0.3 convert_reduce_fusion
  83.2 0.8 broadcast_in_dim.2
  83.9 5.3 %all-to-all-start.2 = ((bf16[256,4,128]{2,1,0:T(4,128)(2,1)}), bf16[256,4,128]{2,1,0:T(4,128)(2,1)S(1)}, u32[]{:S(2)}, u32[]{:S(2)}) async-start(bf16[256,4,128]{2,1,0:T(4,128)(2,1)} %broadcast_in_dim.2), calls=%async_computation.2 | async-start | bytes 524288 | tf_op jit(solution)/shard_map/all_to_all | solution.py:423
  89.2 7.3 %all-gather.1 = f32[4,4,128]{2,1,0:T(4,128)S(1)} all-gather(f32[1,4,128]{2,1,0:T(4,128)S(1)} %slice_bitcast_fusion), channel_id=2, replica_groups=mesh['bins'=64,'band'=4] {'band'}, dimensions={0}, use_global_device_ids=true | all-gather | bytes 10240 | tf_op jit(solution)/shard_map/all_gather | solution.py:424
  96.5 0.1 fusion.1
  96.6 0.6 maximum_multiply_fusion
  97.2 7.8 %all-to-all-done.2.total = bf16[256,4,128]{2,1,0:T(4,128)(2,1)S(1)} async-done(((bf16[256,4,128]{2,1,0:T(4,128)(2,1)}), bf16[256,4,128]{2,1,0:T(4,128)(2,1)S(1)}, u32[]{:S(2)}, u32[]{:S(2)}) %all-to-all-start.2) | async-done | bytes 262176 | tf_op jit(solution)/shard_map/all_to_all | solution.py:423
  105.0 1.5 %unpack.1 = (f32[64,64]{1,0:T(8,128)}, f32[64,64]{1,0:T(8,128)}, f32[64,128]{1,0:T(8,128)}, f32[2,3,3,64,64]{4,3,2,1,0:T(8,128)}) custom-call(s32[2]{0:T(128)S(1)} %pad_add_fusion.place, bf16[256,4,128]{2,1,0:T(4,128)(2,1)S(1)} %all-to-all-done.2.total), custom_call_target="tpu_custom_call" | custom-call | tf_op jit(solution)/shard_map/unpack/pallas_call | solution.py:428
  (13 shorter events, 0.1 us)
Async XLA Ops:
  0.6 16.7 %copy-start = (bf16[32,64,128]{2,1,0:T(8,128)(2,1)S(1)}, bf16[32,64,128]{2,1,0:T(8,128)(2,1)}, u32[]{:S(2)}) copy-start(bf16[32,64,128]{2,1,0:T(8,128)(2,1)} %cot.3) | copy-start | bytes 1572868
  0.6 0.8 copy-start.4
  2.2 38.9 %all-to-all-start = ((bf16[64,16,128]{2,1,0:T(8,128)(2,1)}), bf16[64,16,128]{2,1,0:T(8,128)(2,1)S(1)}, u32[]{:S(2)}, u32[]{:S(2)}) async-start(bf16[64,16,128]{2,1,0:T(8,128)(2,1)} %greet.1), calls=%async_computation | async-start | bytes 524288 | tf_op jit(solution)/shard_map/all_to_all | solution.py:396
  17.3 7.2 %copy-start.6 = (bf16[2,3,3,64,64]{4,3,2,1,0:T(8,128)(2,1)S(1)}, bf16[2,3,3,64,64]{4,3,2,1,0:T(8,128)(2,1)}, u32[]{:S(2)}) copy-start(bf16[2,3,3,64,64]{4,3,2,1,0:T(8,128)(2,1)} %param.11) | copy-start | bytes 442372
  17.4 9.3 %collective-permute-start.1 = (bf16[8,64,128]{2,1,0:T(8,128)(2,1)S(1)}, bf16[8,64,128]{2,1,0:T(8,128)(2,1)S(1)}, u32[]{:S(2)}, u32[]{:S(2)}) collective-permute-start(bf16[8,64,128]{2,1,0:T(8,128)(2,1)S(1)} %get-tuple-element.22), channel_id=1, source_target_pairs={{4,0},{8,4},{12,8},{16,12},{20,16},{24,20},{28,24},{32,28},{36,32}... | collective-permute-start | bytes 393224 | tf_op jit(solution)/shard_map/ppermute | solution.py:386
  24.5 9.7 %collective-permute-start = (bf16[8,64,128]{2,1,0:T(8,128)(2,1)S(1)}, bf16[8,64,128]{2,1,0:T(8,128)(2,1)S(1)}, u32[]{:S(2)}, u32[]{:S(2)}) collective-permute-start(bf16[8,64,128]{2,1,0:T(8,128)(2,1)S(1)} %get-tuple-element.23), channel_id=1, source_target_pairs={{252,0},{0,4},{4,8},{8,12},{12,16},{16,20},{20,24},{24,28},{28,32}... | collective-permute-start | bytes 393224 | tf_op jit(solution)/shard_map/ppermute | solution.py:386
  25.3 9.0 %copy-start.1 = (bf16[64,128]{1,0:T(8,128)(2,1)S(1)}, bf16[64,128]{1,0:T(8,128)(2,1)}, u32[]{:S(2)}) copy-start(bf16[64,128]{1,0:T(8,128)(2,1)} %emb.3) | copy-start | bytes 49156
  34.2 6.9 %copy-start.2 = (bf16[64,64]{1,0:T(8,128)(2,1)S(1)}, bf16[64,64]{1,0:T(8,128)(2,1)}, u32[]{:S(2)}) copy-start(bf16[64,64]{1,0:T(8,128)(2,1)} %lw.1) | copy-start | bytes 24580
  34.2 6.9 %copy-start.3 = (bf16[64,64]{1,0:T(8,128)(2,1)S(1)}, bf16[64,64]{1,0:T(8,128)(2,1)}, u32[]{:S(2)}) copy-start(bf16[64,64]{1,0:T(8,128)(2,1)} %rw.1) | copy-start | bytes 24580
  34.7 4.1 %collective-permute-start.2 = (bf16[256,128]{1,0:T(8,128)(2,1)S(1)}, bf16[256,128]{1,0:T(8,128)(2,1)S(1)}, u32[]{:S(2)}, u32[]{:S(2)}) collective-permute-start(bf16[256,128]{1,0:T(8,128)(2,1)S(1)} %get-tuple-element.14), channel_id=1, source_target_pairs={{3,0},{0,1},{1,2},{2,3},{7,4},{4,5},{5,6},{6,7},{11,8},{8,9},{9,10... | collective-permute-start | bytes 196616 | tf_op jit(solution)/shard_map/ppermute | solution.py:386
  37.4 3.7 %collective-permute-start.3 = (bf16[256,128]{1,0:T(8,128)(2,1)S(1)}, bf16[256,128]{1,0:T(8,128)(2,1)S(1)}, u32[]{:S(2)}, u32[]{:S(2)}) collective-permute-start(bf16[256,128]{1,0:T(8,128)(2,1)S(1)} %get-tuple-element.15), channel_id=1, source_target_pairs={{1,0},{2,1},{3,2},{0,3},{5,4},{6,5},{7,6},{4,7},{9,8},{10,9},{11,1... | collective-permute-start | bytes 196616 | tf_op jit(solution)/shard_map/ppermute | solution.py:386
  37.5 3.6 %copy-start.5 = (s32[2]{0:T(128)S(1)}, s32[2]{0:T(128)}, u32[]{:S(2)}) copy-start(s32[2]{0:T(128)} %dil.1) | copy-start | bytes 28
  83.9 21.1 %all-to-all-start.2 = ((bf16[256,4,128]{2,1,0:T(4,128)(2,1)}), bf16[256,4,128]{2,1,0:T(4,128)(2,1)S(1)}, u32[]{:S(2)}, u32[]{:S(2)}) async-start(bf16[256,4,128]{2,1,0:T(4,128)(2,1)} %broadcast_in_dim.2), calls=%async_computation.2 | async-start | bytes 524288 | tf_op jit(solution)/shard_map/all_to_all | solution.py:423

commit v5 on v4

--- a/solution.py
+++ b/solution.py
@@ -18,9 +18,11 @@
 RIM2 = 8
 RIM3 = 4
 CHUNK = 32
+HELD0 = 64
 HELD = 32
 LIMIT = 28 * 1024 * 1024
 SMALL = 8 * 1024 * 1024
+WHOLE = 56 * 1024 * 1024
 VMEM = pl.BlockSpec(memory_space=pltpu.VMEM)
 SMEM = pl.BlockSpec(memory_space=pltpu.SMEM)
 
@@ -54,7 +56,10 @@
             body(at * held + k, k, *given)
         return carry
 
-    lax.fori_loop(0, count // held, step, 0)
+    if held == count:
+        step(0, 0)
+    else:
+        lax.fori_loop(0, count // held, step, 0)
 
 
 def lane_sums(values):
@@ -89,7 +94,11 @@
     edges = from_lo.shape[0] - c
 
     def rows_at(row, count=1):
-        return pl.ds(pl.multiple_of(row * c, c), count * c)
+        start = row * c
+        return pl.ds(start if isinstance(row, int) else pl.multiple_of(start, c), count * c)
+
+    def rows_of(start, count):
+        return pl.ds(start if isinstance(start, int) else pl.multiple_of(start, 16), count)
 
     def mask_of(bin_id):
         lane = lanes_of(WIDE)
@@ -111,8 +120,8 @@
     proj[...] = jnp.concatenate([right, jnp.zeros_like(right)], 1).T[0:c]
     fl = jnp.concatenate(near, 0).astype(BF16)
     lefts[...] = jnp.dot(fl, lw[...], preferred_element_type=F32).astype(BF16)
-    lane = lax.broadcasted_iota(jnp.int32, (16, 16 * HALF), 1)
-    which = lax.broadcasted_iota(jnp.int32, (16, 16 * HALF), 0)
+    lane = lax.broadcasted_iota(jnp.int32, (HELD0, HELD0 * HALF), 1)
+    which = lax.broadcasted_iota(jnp.int32, (HELD0, HELD0 * HALF), 0)
     pick[...] = jnp.where(lane // HALF == which, 1.0, 0.0).astype(BF16)
     beside = jnp.where(
         lanes_of(HALF) < HALF // 2, from_hi[edges:, :].astype(F32), from_lo[edges:, :].astype(F32)
@@ -124,7 +133,7 @@
 
     def state_step(at):
         mine = lax.dot_general(
-            lefts[pl.ds(pl.multiple_of(at * 16 + RIM0, 16), 16), :], pick[...],
+            lefts[rows_of(at * HELD0 + RIM0, HELD0), :], pick[...],
             (((0,), (0,)), ((), ())), preferred_element_type=F32,
         )
         return (mine,)
@@ -139,7 +148,7 @@
         slope = sig * (1.0 + summed * (1.0 - sig)) * mask
         slope_s[rows_at(row), :] = slope[:, 0:HALF]
 
-    sweep(rows + 2 * RIM0, 16, state_row, state_step)
+    sweep(rows + 2 * RIM0, HELD0, state_row, state_step)
 
     def convolved(weights, source, base_row, rate):
         view = jnp.concatenate([source[rows_at(base_row + rate * k), :] for k in (-1, 0, 1)], 0)
@@ -157,22 +166,23 @@
     sweep(rows + 2 * RIM1, 56, layer_row0)
 
     def layer_step1(at):
-        return from_lo[rows_at(at), :].astype(F32), from_hi[rows_at(at), :].astype(F32)
-
-    def layer_row1(row, k, lo, hi):
+        tiles = [rows_at(tile) for tile in range((rows + 2 * RIM2) // 16)]
+        return [(from_lo[t, :].astype(F32), from_hi[t, :].astype(F32)) for t in tiles]
+
+    def layer_row1(row, k, *tiles):
         a, b, d = convolved(taps[1], s1, row + RIM1 - RIM2, rate1)
         pre = up(a, rate1) + b + down(d, rate1)
         sig = sigmoid(pre)
         mask = mask_of(first_bin - RIM2 + row)
         slope = sig * (1.0 + pre * (1.0 - sig)) * mask
         pairs[row] = (pre * sig * mask)[:, 0:HALF].astype(BF16)
-        lo = pltpu.roll(lo, (HALF - RIM2 * (k + 1)) % HALF, 1)
-        hi = pltpu.roll(hi, (HALF - RIM2 * k) % HALF, 1)
-        rim = jnp.where(lanes_of(HALF) < HALF // 2, hi, lo)
+        lo, hi = tiles[k // 16]
+        here = lanes_of(HALF) // RIM2 == k % 16
+        rim = pltpu.roll(jnp.where(here, hi, lo), (HALF - RIM2 * (k % 16)) % HALF, 1)
         grad = jnp.concatenate([wide_cot[row].astype(F32), rim], 1)
         g1[rows_at(row), :] = (grad * slope).astype(BF16)
 
-    sweep(rows + 2 * RIM2, 16, layer_row1, layer_step1)
+    sweep(rows + 2 * RIM2, rows + 2 * RIM2, layer_row1, layer_step1)
     pair_map[...] = pairs[RIM2 : RIM2 + rows]
 
     def back_row(row, k):
@@ -249,7 +259,10 @@
         sums[:, 3 * HALF : 4 * HALF] += offset_sum
         return carry
 
-    lax.fori_loop(0, rows // HELD, last_step, 0)
+    if rows == HELD:
+        last_step(0, 0)
+    else:
+        lax.fori_loop(0, rows // HELD, last_step, 0)
 
     highest = lax.Precision.HIGHEST
     both = sums[:, 0 : 3 * HALF]
@@ -306,7 +319,7 @@
         scratch_shapes=[
             pltpu.VMEM((c, WIDE), F32),
             pltpu.VMEM((3 * rows, c), BF16),
-            pltpu.VMEM((16, 16 * HALF), BF16),
+            pltpu.VMEM((HELD0, HELD0 * HALF), BF16),
             pltpu.VMEM((c, WIDE), F32),
             pltpu.VMEM((tall(RIM0), WIDE), BF16),
             pltpu.VMEM((tall(RIM1), WIDE), BF16),
@@ -339,16 +352,18 @@
             else:
                 value = cot_down[row - RIM2 - rows]
             value = value.astype(F32)
-            here = (lane >= RIM2 * k) & (lane < RIM2 * (k + 1))
-            low = jnp.where(here, pltpu.roll(value, RIM2 * k, 1), low)
-            high = jnp.where(here, pltpu.roll(value, RIM2 * (k + 1) % HALF, 1), high)
+            value = pltpu.roll(value, RIM2 * k, 1)
+            low = jnp.where(lane // RIM2 == k, value, low)
+            high = jnp.where(lane // RIM2 == (k + 15) % 16, value, high)
         to_lo[tile * c : (tile + 1) * c, :] = low.astype(BF16)
         to_hi[tile * c : (tile + 1) * c, :] = high.astype(BF16)
     to_lo[count // 16 * c :, :] = emb[...]
     to_hi[count // 16 * c :, :] = emb[...]
 
 
-def greet_kernel(rows, c, features, everywhere):
+def greet_kernel(rows, features, first, last, everywhere, low, high):
+    low[...] = first[...]
+    high[...] = last[...]
     packed = jnp.concatenate([features[0 : rows // 2, :], features[rows // 2 :, :]], 1)
     everywhere[...] = jnp.broadcast_to(packed[None], everywhere.shape)
 
@@ -385,17 +400,31 @@
         count = lax.axis_size(axis)
         return lax.ppermute(block, axis, [((i + step) % count, i) for i in range(count)])
 
-    everywhere = pl.pallas_call(
-        functools.partial(greet_kernel, rows, c),
-        out_shape=jax.ShapeDtypeStruct((bins, rows // 2, HALF), BF16),
-        in_specs=[VMEM],
-        out_specs=VMEM,
-        compiler_params=pltpu.CompilerParams(vmem_limit_bytes=SMALL),
+    end = rows // RIM2 - 1
+    row_block = (RIM2, c, group)
+    everywhere, low, high = pl.pallas_call(
+        functools.partial(greet_kernel, rows),
+        grid=(1,),
+        out_shape=(
+            jax.ShapeDtypeStruct((bins, rows // 2, HALF), BF16),
+            jax.ShapeDtypeStruct(row_block, BF16),
+            jax.ShapeDtypeStruct(row_block, BF16),
+        ),
+        in_specs=[
+            pl.BlockSpec((rows, c), lambda _: (0, 0)),
+            pl.BlockSpec(row_block, lambda _: (0, 0, 0)),
+            pl.BlockSpec(row_block, lambda _: (end, 0, 0)),
+        ],
+        out_specs=(
+            pl.BlockSpec((bins, rows // 2, HALF), lambda _: (0, 0, 0)),
+            pl.BlockSpec(row_block, lambda _: (0, 0, 0)),
+            pl.BlockSpec(row_block, lambda _: (0, 0, 0)),
+        ),
+        compiler_params=pltpu.CompilerParams(vmem_limit_bytes=WHOLE),
         name="greet",
-    )(features)
+    )(features, cotangent, cotangent)
     feats = lax.all_to_all(everywhere, "bins", 0, 0, tiled=True)
-    cot_up = beside(cotangent[rows - RIM2 :], "bins", -1)
-    cot_down = beside(cotangent[:RIM2], "bins", 1)
+    cot_up, cot_down = beside(high, "bins", -1), beside(low, "bins", 1)
     edge_shape = jax.ShapeDtypeStruct(((rows + 2 * RIM2) // 16 * c + c, HALF), BF16)
     to_lo, to_hi = pl.pallas_call(
         functools.partial(edge_kernel, rows, c),

time: 107 us -> 105 us (0.981)
  waiting for transfers between devices: 20.1 us -> 18.3 us
  blocking collectives: 33 us -> 34.2 us
    ppermute x4, waiting for transfers between devices: 12.2 us -> 10.4 us  [beside(): lax.ppermute(block, axis, [((i + step) % count, i) for i in range(count)])]
    all_to_all x1, blocking collectives: 25.7 us -> 26.9 us  [per_device(): parts = lax.all_to_all(payload, every, 0, 0, tiled=True)]
  transfers between devices with their start and end apart: 6 -> 6, of which waited for: 5 -> 4; matrix products, arithmetic and copies ran while one was open for 2% -> 2% of each run, Pallas kernels for 0% -> 0%
where the time goes in v5:
time: 105 us
  blocking collectives  34.2 us (33%)
  starting transfers between devices  29.8 us (28%)
  Pallas kernels  18.7 us (18%)
  waiting for transfers between devices  18.3 us (17%)
  local copies, waits for them, and re-layouts  1.9 us (2%)
    all_to_all x1, blocking collectives, per_device(): parts = lax.all_to_all(payload, every, 0, 0, tiled=True)  26.9 us
    all_to_all x1, starting transfers between devices, per_device(): feats = lax.all_to_all(everywhere, 'bins', 0, 0, tiled=True)  15.2 us
    pallas_call x1, Pallas kernels, middle(): pl.pallas_call(functools.partial(middle_kernel, rows, c, total_bins, tota...  15.1 us
    ppermute x4, waiting for transfers between devices, beside(): lax.ppermute(block, axis, [((i + step) % count, i) for i in range(count)])  10.4 us
    ppermute x4, starting transfers between devices, beside(): lax.ppermute(block, axis, [((i + step) % count, i) for i in range(count)])  9.34 us
    all_to_all x1, waiting for transfers between devices, per_device(): total = lax.all_to_all(share, every, 0, 0, tiled=True)  7.83 us
    all_gather x1, blocking collectives, per_device(): quarters = lax.all_gather(feature_part, 'band')  7.27 us
    all_to_all x1, starting transfers between devices, per_device(): total = lax.all_to_all(share, every, 0, 0, tiled=True)  5.26 us
  transfers between devices with their start and end apart: 6, of which 4 were waited for; matrix products, arithmetic and copies ran while one was open for 2% of the time, Pallas kernels for 0%

profile of v5, /device:TPU:1, one launch (start us, length us, event | category | flops | bytes accessed | tf_op | source)
XLA Modules:
  0.0 104.6 jit_solution(13307429358863651046)
XLA Ops:
  0.6 1.8 %greet.1 = (bf16[64,16,128]{2,1,0:T(8,128)(2,1)}, bf16[8,64,128]{2,1,0:T(8,128)(2,1)}, bf16[8,64,128]{2,1,0:T(8,128)(2,1)}) custom-call(bf16[32,64]{1,0:T(8,128)(2,1)} %features.1, bf16[32,64,128]{2,1,0:T(8,128)(2,1)} %cot.3, bf16[32,64,128]{2,1,0:T(8,128)(2,1)} %cot.3), custom_call_target="tpu_custom_call" | custom-call | tf_op jit(solution)/shard_map/greet/pallas_call | solution.py:405
  2.4 15.2 %all-to-all-start = ((bf16[64,16,128]{2,1,0:T(8,128)(2,1)}), bf16[64,16,128]{2,1,0:T(8,128)(2,1)S(1)}, u32[]{:S(2)}, u32[]{:S(2)}) async-start(bf16[64,16,128]{2,1,0:T(8,128)(2,1)} %get-tuple-element.17), calls=%async_computation | async-start | bytes 524288 | tf_op jit(solution)/shard_map/all_to_all | solution.py:426
  17.7 1.1 %collective-permute-start = (bf16[8,64,128]{2,1,0:T(8,128)(2,1)}, bf16[8,64,128]{2,1,0:T(8,128)(2,1)S(1)}, u32[]{:S(2)}, u32[]{:S(2)}) collective-permute-start(bf16[8,64,128]{2,1,0:T(8,128)(2,1)} %get-tuple-element.18), channel_id=1, source_target_pairs={{252,0},{0,4},{4,8},{8,12},{12,16},{16,20},{20,24},{24,28},{28,32}... | collective-permute-start | bytes 393224 | tf_op jit(solution)/shard_map/ppermute | solution.py:401
  18.8 6.2 %collective-permute-start.1 = (bf16[8,64,128]{2,1,0:T(8,128)(2,1)S(1)}, bf16[8,64,128]{2,1,0:T(8,128)(2,1)S(1)}, u32[]{:S(2)}, u32[]{:S(2)}) collective-permute-start(bf16[8,64,128]{2,1,0:T(8,128)(2,1)S(1)} %copy-done.6), channel_id=1, source_target_pairs={{4,0},{8,4},{12,8},{16,12},{20,16},{24,20},{28,24},{32,28},{36,32}... | collective-permute-start | bytes 393224 | tf_op jit(solution)/shard_map/ppermute | solution.py:401
  25.0 0.2 copy.17
  25.2 0.3 reshape.23.taps
  25.5 0.0 copy-start
  25.5 0.3 copy.18
  25.8 0.0 copy-start.1
  25.8 0.2 reshape.24.back_taps
  26.0 6.9 %collective-permute-done.cot_up = bf16[8,64,128]{2,1,0:T(8,128)(2,1)S(1)} collective-permute-done((bf16[8,64,128]{2,1,0:T(8,128)(2,1)}, bf16[8,64,128]{2,1,0:T(8,128)(2,1)S(1)}, u32[]{:S(2)}, u32[]{:S(2)}) %collective-permute-start) | collective-permute-done | bytes 131104 | tf_op jit(solution)/shard_map/ppermute | solution.py:401
  32.9 0.0 collective-permute-done.1.cot_down
  32.9 0.0 copy-start.2
  32.9 0.0 copy-start.3
  33.0 0.3 edges.1
  33.2 2.0 %collective-permute-start.2 = (bf16[256,128]{1,0:T(8,128)(2,1)S(1)}, bf16[256,128]{1,0:T(8,128)(2,1)S(1)}, u32[]{:S(2)}, u32[]{:S(2)}) collective-permute-start(bf16[256,128]{1,0:T(8,128)(2,1)S(1)} %get-tuple-element.20), channel_id=1, source_target_pairs={{3,0},{0,1},{1,2},{2,3},{7,4},{4,5},{5,6},{6,7},{11,8},{8,9},{9,10... | collective-permute-start | bytes 196616 | tf_op jit(solution)/shard_map/ppermute | solution.py:401
  35.2 0.1 collective-permute-start.3
  35.3 0.1 pad_add_fusion.place
  35.4 1.2 %collective-permute-done.2.from_lo = bf16[256,128]{1,0:T(8,128)(2,1)S(1)} collective-permute-done((bf16[256,128]{1,0:T(8,128)(2,1)S(1)}, bf16[256,128]{1,0:T(8,128)(2,1)S(1)}, u32[]{:S(2)}, u32[]{:S(2)}) %collective-permute-start.2) | collective-permute-done | bytes 65568 | tf_op jit(solution)/shard_map/ppermute | solution.py:401
  36.6 2.4 %collective-permute-done.3.from_hi = bf16[256,128]{1,0:T(8,128)(2,1)S(1)} collective-permute-done((bf16[256,128]{1,0:T(8,128)(2,1)S(1)}, bf16[256,128]{1,0:T(8,128)(2,1)S(1)}, u32[]{:S(2)}, u32[]{:S(2)}) %collective-permute-start.3) | collective-permute-done | bytes 65568 | tf_op jit(solution)/shard_map/ppermute | solution.py:401
  38.9 0.0 all-to-all-done.feats
  38.9 0.0 copy-done.2
  38.9 15.1 %middle.1 = (bf16[32,64,128]{2,1,0:T(8,128)(2,1)}, bf16[256,8,128]{2,1,0:T(8,128)(2,1)S(1)}) custom-call(s32[2]{0:T(128)S(1)} %pad_add_fusion.place, s32[2]{0:T(128)S(1)} %copy-done.4, bf16[64,16,128]{2,1,0:T(8,128)(2,1)S(1)} %all-to-all-done.feats, bf16[8,64,128]{2,1,0:T(8,128)(2,1)S(1)} %collective-permute-done.cot_up, bf16[32,64,128]{2,1,0:T(8,128)(2,1)S(1)} %copy-done, ...), custom_call_target="tpu_custom_call" | custom-call | tf_op jit(solution)/shard_map/middle/pallas_call | solution.py:311
  54.1 26.9 %all_to_all.15 = bf16[256,8,128]{2,1,0:T(8,128)(2,1)S(1)} all-to-all(bf16[256,8,128]{2,1,0:T(8,128)(2,1)S(1)} %get-tuple-element.23), channel_id=1, replica_groups=mesh['bins'=64,'band'=4] {'bins','band'}, dimensions={0} | all-to-all | bytes 1048576 | tf_op jit(solution)/shard_map/all_to_all | solution.py:448
  81.0 0.3 convert_reduce_fusion
  81.2 0.8 broadcast_in_dim.2
  82.0 5.3 %all-to-all-start.2 = ((bf16[256,4,128]{2,1,0:T(4,128)(2,1)}), bf16[256,4,128]{2,1,0:T(4,128)(2,1)S(1)}, u32[]{:S(2)}, u32[]{:S(2)}) async-start(bf16[256,4,128]{2,1,0:T(4,128)(2,1)} %broadcast_in_dim.2), calls=%async_computation.2 | async-start | bytes 524288 | tf_op jit(solution)/shard_map/all_to_all | solution.py:452
  87.3 7.3 %all-gather.1 = f32[4,4,128]{2,1,0:T(4,128)S(1)} all-gather(f32[1,4,128]{2,1,0:T(4,128)S(1)} %slice_bitcast_fusion), channel_id=2, replica_groups=mesh['bins'=64,'band'=4] {'band'}, dimensions={0}, use_global_device_ids=true | all-gather | bytes 10240 | tf_op jit(solution)/shard_map/all_gather | solution.py:453
  94.6 0.1 fusion
  94.6 0.6 maximum_multiply_fusion
  95.3 7.8 %all-to-all-done.2.total = bf16[256,4,128]{2,1,0:T(4,128)(2,1)S(1)} async-done(((bf16[256,4,128]{2,1,0:T(4,128)(2,1)}), bf16[256,4,128]{2,1,0:T(4,128)(2,1)S(1)}, u32[]{:S(2)}, u32[]{:S(2)}) %all-to-all-start.2) | async-done | bytes 262176 | tf_op jit(solution)/shard_map/all_to_all | solution.py:452
  103.1 1.5 %unpack.1 = (f32[64,64]{1,0:T(8,128)}, f32[64,64]{1,0:T(8,128)}, f32[64,128]{1,0:T(8,128)}, f32[2,3,3,64,64]{4,3,2,1,0:T(8,128)}) custom-call(s32[2]{0:T(128)S(1)} %pad_add_fusion.place, bf16[256,4,128]{2,1,0:T(4,128)(2,1)S(1)} %all-to-all-done.2.total), custom_call_target="tpu_custom_call" | custom-call | tf_op jit(solution)/shard_map/unpack/pallas_call | solution.py:457
  (12 shorter events, 0.0 us)
Async XLA Ops:
  2.4 22.5 %copy-start.5 = (bf16[2,3,3,64,64]{4,3,2,1,0:T(8,128)(2,1)S(1)}, bf16[2,3,3,64,64]{4,3,2,1,0:T(8,128)(2,1)}, u32[]{:S(2)}) copy-start(bf16[2,3,3,64,64]{4,3,2,1,0:T(8,128)(2,1)} %param.11) | copy-start | bytes 442372
  2.4 16.3 %copy-start.6 = (bf16[8,64,128]{2,1,0:T(8,128)(2,1)S(1)}, bf16[8,64,128]{2,1,0:T(8,128)(2,1)}, u32[]{:S(2)}) copy-start(bf16[8,64,128]{2,1,0:T(8,128)(2,1)} %get-tuple-element.19) | copy-start | bytes 393220
  2.4 36.5 %all-to-all-start = ((bf16[64,16,128]{2,1,0:T(8,128)(2,1)}), bf16[64,16,128]{2,1,0:T(8,128)(2,1)S(1)}, u32[]{:S(2)}, u32[]{:S(2)}) async-start(bf16[64,16,128]{2,1,0:T(8,128)(2,1)} %get-tuple-element.17), calls=%async_computation | async-start | bytes 524288 | tf_op jit(solution)/shard_map/all_to_all | solution.py:426
  17.7 15.2 %collective-permute-start = (bf16[8,64,128]{2,1,0:T(8,128)(2,1)}, bf16[8,64,128]{2,1,0:T(8,128)(2,1)S(1)}, u32[]{:S(2)}, u32[]{:S(2)}) collective-permute-start(bf16[8,64,128]{2,1,0:T(8,128)(2,1)} %get-tuple-element.18), channel_id=1, source_target_pairs={{252,0},{0,4},{4,8},{8,12},{12,16},{16,20},{20,24},{24,28},{28,32}... | collective-permute-start | bytes 393224 | tf_op jit(solution)/shard_map/ppermute | solution.py:401
  18.8 14.1 %collective-permute-start.1 = (bf16[8,64,128]{2,1,0:T(8,128)(2,1)S(1)}, bf16[8,64,128]{2,1,0:T(8,128)(2,1)S(1)}, u32[]{:S(2)}, u32[]{:S(2)}) collective-permute-start(bf16[8,64,128]{2,1,0:T(8,128)(2,1)S(1)} %copy-done.6), channel_id=1, source_target_pairs={{4,0},{8,4},{12,8},{16,12},{20,16},{24,20},{28,24},{32,28},{36,32}... | collective-permute-start | bytes 393224 | tf_op jit(solution)/shard_map/ppermute | solution.py:401
  25.5 7.4 %copy-start = (bf16[32,64,128]{2,1,0:T(8,128)(2,1)S(1)}, bf16[32,64,128]{2,1,0:T(8,128)(2,1)}, u32[]{:S(2)}) copy-start(bf16[32,64,128]{2,1,0:T(8,128)(2,1)} %cot.3) | copy-start | bytes 1572868
  25.8 7.2 %copy-start.1 = (bf16[64,128]{1,0:T(8,128)(2,1)S(1)}, bf16[64,128]{1,0:T(8,128)(2,1)}, u32[]{:S(2)}) copy-start(bf16[64,128]{1,0:T(8,128)(2,1)} %emb.3) | copy-start | bytes 49156
  32.9 6.0 %copy-start.2 = (bf16[64,64]{1,0:T(8,128)(2,1)S(1)}, bf16[64,64]{1,0:T(8,128)(2,1)}, u32[]{:S(2)}) copy-start(bf16[64,64]{1,0:T(8,128)(2,1)} %lw.1) | copy-start | bytes 24580
  32.9 6.0 %copy-start.3 = (bf16[64,64]{1,0:T(8,128)(2,1)S(1)}, bf16[64,64]{1,0:T(8,128)(2,1)}, u32[]{:S(2)}) copy-start(bf16[64,64]{1,0:T(8,128)(2,1)} %rw.1) | copy-start | bytes 24580
  33.2 3.3 %collective-permute-start.2 = (bf16[256,128]{1,0:T(8,128)(2,1)S(1)}, bf16[256,128]{1,0:T(8,128)(2,1)S(1)}, u32[]{:S(2)}, u32[]{:S(2)}) collective-permute-start(bf16[256,128]{1,0:T(8,128)(2,1)S(1)} %get-tuple-element.20), channel_id=1, source_target_pairs={{3,0},{0,1},{1,2},{2,3},{7,4},{4,5},{5,6},{6,7},{11,8},{8,9},{9,10... | collective-permute-start | bytes 196616 | tf_op jit(solution)/shard_map/ppermute | solution.py:401
  35.2 3.7 %collective-permute-start.3 = (bf16[256,128]{1,0:T(8,128)(2,1)S(1)}, bf16[256,128]{1,0:T(8,128)(2,1)S(1)}, u32[]{:S(2)}, u32[]{:S(2)}) collective-permute-start(bf16[256,128]{1,0:T(8,128)(2,1)S(1)} %get-tuple-element.21), channel_id=1, source_target_pairs={{1,0},{2,1},{3,2},{0,3},{5,4},{6,5},{7,6},{4,7},{9,8},{10,9},{11,1... | collective-permute-start | bytes 196616 | tf_op jit(solution)/shard_map/ppermute | solution.py:401
  35.3 3.6 %copy-start.4 = (s32[2]{0:T(128)S(1)}, s32[2]{0:T(128)}, u32[]{:S(2)}) copy-start(s32[2]{0:T(128)} %dil.1) | copy-start | bytes 28
  82.0 21.1 %all-to-all-start.2 = ((bf16[256,4,128]{2,1,0:T(4,128)(2,1)}), bf16[256,4,128]{2,1,0:T(4,128)(2,1)S(1)}, u32[]{:S(2)}, u32[]{:S(2)}) async-start(bf16[256,4,128]{2,1,0:T(4,128)(2,1)} %broadcast_in_dim.2), calls=%async_computation.2 | async-start | bytes 524288 | tf_op jit(solution)/shard_map/all_to_all | solution.py:452

commit v6 on v5

--- a/solution.py
+++ b/solution.py
@@ -247,8 +247,9 @@
             offset_sum = offset_sum + grad
             turned = pltpu.roll(grad, k, 1) if k else grad
             wrapped = jnp.where(lane < k, turned, 0.0)
-            window = window + (turned - wrapped)
+            window = window + turned
             wrap = wrap + wrapped
+        window = window - wrap
         here = (lane >= at * HELD) & (lane < (at + 1) * HELD)
         sums[:, 0:HALF] += jnp.where(here, lane_sums(grads), 0.0)
         first = lane < at * HELD
@@ -370,8 +371,7 @@
 
 def unpack_kernel(c, whole_scale, offset_scale, place, total, left, right, offset, kernels):
     def piece(start):
-        value = total[start // 4 : (start + c) // 4].astype(F32)
-        return value.reshape(c, HALF)
+        return total[start : start + c, :].astype(F32)
 
     for p in range(3):
         rest = piece((6 + p) * c) * whole_scale
@@ -383,8 +383,8 @@
     both = piece(9 * c) * whole_scale
     left[...] = both[:, 0:c]
     right[...] = both[:, c : 2 * c]
-    at = pl.ds((10 * c + place[1] * c) // 4, c // 4)
-    offset[...] = total[at].astype(F32).reshape(c, HALF) * offset_scale
+    at = pl.ds(pl.multiple_of((10 + place[1]) * c, c), c)
+    offset[...] = total[at, :].astype(F32) * offset_scale
 
 
 def per_device(features, left_weight, right_weight, offset_embed, kernels, dilation, cotangent):
@@ -449,7 +449,7 @@
     summed = jnp.sum(parts.astype(F32), axis=0)
     feature_part = summed[:4]
     share = jnp.broadcast_to(summed[None, 4:].astype(BF16), (devices, 4, HALF))
-    total = lax.all_to_all(share, every, 0, 0, tiled=True)
+    total = lax.all_to_all(share, every, 0, 0, tiled=True).reshape(4 * devices, HALF)
     quarters = lax.all_gather(feature_part, "band")
     pairs = quarters.reshape(rows // 2, HALF)
     grad_features = jnp.concatenate([pairs[:, :c], pairs[:, c:]], 0) / math.sqrt(total_band)

time: 105 us -> 105 us (level)
  no operation moved by 1% of the time
where the time goes in v6:
time: 105 us
  blocking collectives  34.2 us (33%)
  starting transfers between devices  29.8 us (28%)
  Pallas kernels  18.7 us (18%)
  waiting for transfers between devices  18.3 us (17%)
  local copies, waits for them, and re-layouts  1.89 us (2%)
    all_to_all x1, blocking collectives, per_device(): parts = lax.all_to_all(payload, every, 0, 0, tiled=True)  26.9 us
    all_to_all x1, starting transfers between devices, per_device(): feats = lax.all_to_all(everywhere, 'bins', 0, 0, tiled=True)  15.2 us
    pallas_call x1, Pallas kernels, middle(): pl.pallas_call(functools.partial(middle_kernel, rows, c, total_bins, tota...  15.1 us
    ppermute x4, waiting for transfers between devices, beside(): lax.ppermute(block, axis, [((i + step) % count, i) for i in range(count)])  10.5 us
    ppermute x4, starting transfers between devices, beside(): lax.ppermute(block, axis, [((i + step) % count, i) for i in range(count)])  9.34 us
    all_to_all x1, waiting for transfers between devices, per_device(): lax.all_to_all(share, every, 0, 0, tiled=True).reshape(4 * devices, HALF)  7.83 us
    all_gather x1, blocking collectives, per_device(): quarters = lax.all_gather(feature_part, 'band')  7.27 us
    all_to_all x1, starting transfers between devices, per_device(): lax.all_to_all(share, every, 0, 0, tiled=True).reshape(4 * devices, HALF)  5.26 us
  transfers between devices with their start and end apart: 6, of which 4 were waited for; matrix products, arithmetic and copies ran while one was open for 2% of the time, Pallas kernels for 0%

profile of v6, /device:TPU:1, one launch (start us, length us, event | category | flops | bytes accessed | tf_op | source)
XLA Modules:
  0.0 104.6 jit_solution(8371019509266808192)
XLA Ops:
  0.6 1.8 %greet.1 = (bf16[64,16,128]{2,1,0:T(8,128)(2,1)}, bf16[8,64,128]{2,1,0:T(8,128)(2,1)}, bf16[8,64,128]{2,1,0:T(8,128)(2,1)}) custom-call(bf16[32,64]{1,0:T(8,128)(2,1)} %features.1, bf16[32,64,128]{2,1,0:T(8,128)(2,1)} %cot.3, bf16[32,64,128]{2,1,0:T(8,128)(2,1)} %cot.3), custom_call_target="tpu_custom_call" | custom-call | tf_op jit(solution)/shard_map/greet/pallas_call | solution.py:405
  2.4 15.2 %all-to-all-start = ((bf16[64,16,128]{2,1,0:T(8,128)(2,1)}), bf16[64,16,128]{2,1,0:T(8,128)(2,1)S(1)}, u32[]{:S(2)}, u32[]{:S(2)}) async-start(bf16[64,16,128]{2,1,0:T(8,128)(2,1)} %get-tuple-element.17), calls=%async_computation | async-start | bytes 524288 | tf_op jit(solution)/shard_map/all_to_all | solution.py:426
  17.7 1.1 %collective-permute-start = (bf16[8,64,128]{2,1,0:T(8,128)(2,1)}, bf16[8,64,128]{2,1,0:T(8,128)(2,1)S(1)}, u32[]{:S(2)}, u32[]{:S(2)}) collective-permute-start(bf16[8,64,128]{2,1,0:T(8,128)(2,1)} %get-tuple-element.18), channel_id=1, source_target_pairs={{252,0},{0,4},{4,8},{8,12},{12,16},{16,20},{20,24},{24,28},{28,32}... | collective-permute-start | bytes 393224 | tf_op jit(solution)/shard_map/ppermute | solution.py:401
  18.8 6.2 %collective-permute-start.1 = (bf16[8,64,128]{2,1,0:T(8,128)(2,1)S(1)}, bf16[8,64,128]{2,1,0:T(8,128)(2,1)S(1)}, u32[]{:S(2)}, u32[]{:S(2)}) collective-permute-start(bf16[8,64,128]{2,1,0:T(8,128)(2,1)S(1)} %copy-done.6), channel_id=1, source_target_pairs={{4,0},{8,4},{12,8},{16,12},{20,16},{24,20},{28,24},{32,28},{36,32}... | collective-permute-start | bytes 393224 | tf_op jit(solution)/shard_map/ppermute | solution.py:401
  25.0 0.2 copy.17
  25.2 0.2 reshape.26.taps
  25.5 0.0 copy-start
  25.5 0.3 copy.18
  25.8 0.0 copy-start.1
  25.8 0.2 reshape.27.back_taps
  26.0 6.9 %collective-permute-done.cot_up = bf16[8,64,128]{2,1,0:T(8,128)(2,1)S(1)} collective-permute-done((bf16[8,64,128]{2,1,0:T(8,128)(2,1)}, bf16[8,64,128]{2,1,0:T(8,128)(2,1)S(1)}, u32[]{:S(2)}, u32[]{:S(2)}) %collective-permute-start) | collective-permute-done | bytes 131104 | tf_op jit(solution)/shard_map/ppermute | solution.py:401
  32.9 0.0 collective-permute-done.1.cot_down
  32.9 0.0 copy-start.2
  32.9 0.0 copy-start.3
  33.0 0.3 edges.1
  33.2 2.0 %collective-permute-start.2 = (bf16[256,128]{1,0:T(8,128)(2,1)S(1)}, bf16[256,128]{1,0:T(8,128)(2,1)S(1)}, u32[]{:S(2)}, u32[]{:S(2)}) collective-permute-start(bf16[256,128]{1,0:T(8,128)(2,1)S(1)} %get-tuple-element.20), channel_id=1, source_target_pairs={{3,0},{0,1},{1,2},{2,3},{7,4},{4,5},{5,6},{6,7},{11,8},{8,9},{9,10... | collective-permute-start | bytes 196616 | tf_op jit(solution)/shard_map/ppermute | solution.py:401
  35.2 0.1 collective-permute-start.3
  35.3 0.1 pad_add_fusion.place
  35.4 1.2 %collective-permute-done.2.from_lo = bf16[256,128]{1,0:T(8,128)(2,1)S(1)} collective-permute-done((bf16[256,128]{1,0:T(8,128)(2,1)S(1)}, bf16[256,128]{1,0:T(8,128)(2,1)S(1)}, u32[]{:S(2)}, u32[]{:S(2)}) %collective-permute-start.2) | collective-permute-done | bytes 65568 | tf_op jit(solution)/shard_map/ppermute | solution.py:401
  36.6 2.4 %collective-permute-done.3.from_hi = bf16[256,128]{1,0:T(8,128)(2,1)S(1)} collective-permute-done((bf16[256,128]{1,0:T(8,128)(2,1)S(1)}, bf16[256,128]{1,0:T(8,128)(2,1)S(1)}, u32[]{:S(2)}, u32[]{:S(2)}) %collective-permute-start.3) | collective-permute-done | bytes 65568 | tf_op jit(solution)/shard_map/ppermute | solution.py:401
  38.9 0.0 all-to-all-done.feats
  38.9 0.0 copy-done.2
  38.9 15.1 %middle.1 = (bf16[32,64,128]{2,1,0:T(8,128)(2,1)}, bf16[256,8,128]{2,1,0:T(8,128)(2,1)S(1)}) custom-call(s32[2]{0:T(128)S(1)} %pad_add_fusion.place, s32[2]{0:T(128)S(1)} %copy-done.4, bf16[64,16,128]{2,1,0:T(8,128)(2,1)S(1)} %all-to-all-done.feats, bf16[8,64,128]{2,1,0:T(8,128)(2,1)S(1)} %collective-permute-done.cot_up, bf16[32,64,128]{2,1,0:T(8,128)(2,1)S(1)} %copy-done, ...), custom_call_target="tpu_custom_call" | custom-call | tf_op jit(solution)/shard_map/middle/pallas_call | solution.py:312
  54.0 26.9 %all_to_all.15 = bf16[256,8,128]{2,1,0:T(8,128)(2,1)S(1)} all-to-all(bf16[256,8,128]{2,1,0:T(8,128)(2,1)S(1)} %get-tuple-element.23), channel_id=1, replica_groups=mesh['bins'=64,'band'=4] {'bins','band'}, dimensions={0} | all-to-all | bytes 1048576 | tf_op jit(solution)/shard_map/all_to_all | solution.py:448
  80.9 0.3 convert_reduce_fusion
  81.2 0.8 broadcast_in_dim.2
  82.0 5.3 %all-to-all-start.2 = ((bf16[256,4,128]{2,1,0:T(4,128)(2,1)}), bf16[256,4,128]{2,1,0:T(4,128)(2,1)S(1)}, u32[]{:S(2)}, u32[]{:S(2)}) async-start(bf16[256,4,128]{2,1,0:T(4,128)(2,1)} %broadcast_in_dim.2), calls=%async_computation.2 | async-start | bytes 524288 | tf_op jit(solution)/shard_map/all_to_all | solution.py:452
  87.3 7.3 %all-gather.1 = f32[4,4,128]{2,1,0:T(4,128)S(1)} all-gather(f32[1,4,128]{2,1,0:T(4,128)S(1)} %slice_bitcast_fusion), channel_id=2, replica_groups=mesh['bins'=64,'band'=4] {'band'}, dimensions={0}, use_global_device_ids=true | all-gather | bytes 10240 | tf_op jit(solution)/shard_map/all_gather | solution.py:453
  94.5 0.1 fusion
  94.6 0.6 maximum_multiply_fusion
  95.2 7.8 %all-to-all-done.2 = bf16[256,4,128]{2,1,0:T(4,128)(2,1)S(1)} async-done(((bf16[256,4,128]{2,1,0:T(4,128)(2,1)}), bf16[256,4,128]{2,1,0:T(4,128)(2,1)S(1)}, u32[]{:S(2)}, u32[]{:S(2)}) %all-to-all-start.2) | async-done | bytes 262176 | tf_op jit(solution)/shard_map/all_to_all | solution.py:452
  103.1 1.5 %unpack.1 = (f32[64,64]{1,0:T(8,128)}, f32[64,64]{1,0:T(8,128)}, f32[64,128]{1,0:T(8,128)}, f32[2,3,3,64,64]{4,3,2,1,0:T(8,128)}) custom-call(s32[2]{0:T(128)S(1)} %pad_add_fusion.place, bf16[1024,128]{1,0:T(8,128)(2,1)S(1)} %bitcast.8), custom_call_target="tpu_custom_call" | custom-call | tf_op jit(solution)/shard_map/unpack/pallas_call | solution.py:457
  (12 shorter events, 0.0 us)
Async XLA Ops:
  2.4 22.5 %copy-start.5 = (bf16[2,3,3,64,64]{4,3,2,1,0:T(8,128)(2,1)S(1)}, bf16[2,3,3,64,64]{4,3,2,1,0:T(8,128)(2,1)}, u32[]{:S(2)}) copy-start(bf16[2,3,3,64,64]{4,3,2,1,0:T(8,128)(2,1)} %param.11) | copy-start | bytes 442372
  2.4 16.3 %copy-start.6 = (bf16[8,64,128]{2,1,0:T(8,128)(2,1)S(1)}, bf16[8,64,128]{2,1,0:T(8,128)(2,1)}, u32[]{:S(2)}) copy-start(bf16[8,64,128]{2,1,0:T(8,128)(2,1)} %get-tuple-element.19) | copy-start | bytes 393220
  2.4 36.5 %all-to-all-start = ((bf16[64,16,128]{2,1,0:T(8,128)(2,1)}), bf16[64,16,128]{2,1,0:T(8,128)(2,1)S(1)}, u32[]{:S(2)}, u32[]{:S(2)}) async-start(bf16[64,16,128]{2,1,0:T(8,128)(2,1)} %get-tuple-element.17), calls=%async_computation | async-start | bytes 524288 | tf_op jit(solution)/shard_map/all_to_all | solution.py:426
  17.7 15.2 %collective-permute-start = (bf16[8,64,128]{2,1,0:T(8,128)(2,1)}, bf16[8,64,128]{2,1,0:T(8,128)(2,1)S(1)}, u32[]{:S(2)}, u32[]{:S(2)}) collective-permute-start(bf16[8,64,128]{2,1,0:T(8,128)(2,1)} %get-tuple-element.18), channel_id=1, source_target_pairs={{252,0},{0,4},{4,8},{8,12},{12,16},{16,20},{20,24},{24,28},{28,32}... | collective-permute-start | bytes 393224 | tf_op jit(solution)/shard_map/ppermute | solution.py:401
  18.8 14.1 %collective-permute-start.1 = (bf16[8,64,128]{2,1,0:T(8,128)(2,1)S(1)}, bf16[8,64,128]{2,1,0:T(8,128)(2,1)S(1)}, u32[]{:S(2)}, u32[]{:S(2)}) collective-permute-start(bf16[8,64,128]{2,1,0:T(8,128)(2,1)S(1)} %copy-done.6), channel_id=1, source_target_pairs={{4,0},{8,4},{12,8},{16,12},{20,16},{24,20},{28,24},{32,28},{36,32}... | collective-permute-start | bytes 393224 | tf_op jit(solution)/shard_map/ppermute | solution.py:401
  25.5 7.4 %copy-start = (bf16[32,64,128]{2,1,0:T(8,128)(2,1)S(1)}, bf16[32,64,128]{2,1,0:T(8,128)(2,1)}, u32[]{:S(2)}) copy-start(bf16[32,64,128]{2,1,0:T(8,128)(2,1)} %cot.3) | copy-start | bytes 1572868
  25.8 7.2 %copy-start.1 = (bf16[64,128]{1,0:T(8,128)(2,1)S(1)}, bf16[64,128]{1,0:T(8,128)(2,1)}, u32[]{:S(2)}) copy-start(bf16[64,128]{1,0:T(8,128)(2,1)} %emb.3) | copy-start | bytes 49156
  32.9 6.0 %copy-start.2 = (bf16[64,64]{1,0:T(8,128)(2,1)S(1)}, bf16[64,64]{1,0:T(8,128)(2,1)}, u32[]{:S(2)}) copy-start(bf16[64,64]{1,0:T(8,128)(2,1)} %lw.1) | copy-start | bytes 24580
  32.9 6.0 %copy-start.3 = (bf16[64,64]{1,0:T(8,128)(2,1)S(1)}, bf16[64,64]{1,0:T(8,128)(2,1)}, u32[]{:S(2)}) copy-start(bf16[64,64]{1,0:T(8,128)(2,1)} %rw.1) | copy-start | bytes 24580
  33.2 3.3 %collective-permute-start.2 = (bf16[256,128]{1,0:T(8,128)(2,1)S(1)}, bf16[256,128]{1,0:T(8,128)(2,1)S(1)}, u32[]{:S(2)}, u32[]{:S(2)}) collective-permute-start(bf16[256,128]{1,0:T(8,128)(2,1)S(1)} %get-tuple-element.20), channel_id=1, source_target_pairs={{3,0},{0,1},{1,2},{2,3},{7,4},{4,5},{5,6},{6,7},{11,8},{8,9},{9,10... | collective-permute-start | bytes 196616 | tf_op jit(solution)/shard_map/ppermute | solution.py:401
  35.2 3.7 %collective-permute-start.3 = (bf16[256,128]{1,0:T(8,128)(2,1)S(1)}, bf16[256,128]{1,0:T(8,128)(2,1)S(1)}, u32[]{:S(2)}, u32[]{:S(2)}) collective-permute-start(bf16[256,128]{1,0:T(8,128)(2,1)S(1)} %get-tuple-element.21), channel_id=1, source_target_pairs={{1,0},{2,1},{3,2},{0,3},{5,4},{6,5},{7,6},{4,7},{9,8},{10,9},{11,1... | collective-permute-start | bytes 196616 | tf_op jit(solution)/shard_map/ppermute | solution.py:401
  35.3 3.6 %copy-start.4 = (s32[2]{0:T(128)S(1)}, s32[2]{0:T(128)}, u32[]{:S(2)}) copy-start(s32[2]{0:T(128)} %dil.1) | copy-start | bytes 28
  82.0 21.1 %all-to-all-start.2 = ((bf16[256,4,128]{2,1,0:T(4,128)(2,1)}), bf16[256,4,128]{2,1,0:T(4,128)(2,1)S(1)}, u32[]{:S(2)}, u32[]{:S(2)}) async-start(bf16[256,4,128]{2,1,0:T(4,128)(2,1)} %broadcast_in_dim.2), calls=%async_computation.2 | async-start | bytes 524288 | tf_op jit(solution)/shard_map/all_to_all | solution.py:452
